TPU v7x, 128 devices: a whole 4x4x4 slice. The times are simulated.
128 devices in a mesh: tm: 16 (over z, x), dish: 8 (over y, core).
Axes of the slice: x: 4, y: 4, z: 4, core: 2. Of those that a mesh axis runs over, the one named last changes fastest.
Arguments:
- tod: float32 [64, 1024, 4096], P('dish', None, 'tm'), may hold values from -8 to 8
- taps: float32 [65], replicated, may hold values from 0.005 to 0.025
- modes_init: float32 [6, 1024], replicated, may hold values from -6 to 6
- weights: float32 [64, 4096], P('dish', 'tm'), may hold values from 0.25 to 4
- block_tile: int32 [64, 32], P('dish', 'tm'), may hold values from 0 to 15, as said below
- block_offset: int32 [64, 32], P('dish', 'tm'), may hold values from 0 to 255
Outputs:
- sky: float32 [16, 1024, 256], P('tm', 'dish')
Inputs may be any that keep to these rules, and one draw needn't show every extreme that they name: `block_tile`: among the blocks of one device (its 8 dishes and its 2 blocks of time), no tile is named more than 2 times, and one tile is named exactly 2 times by the blocks of every device.
All inputs are finite; a program needn't handle non-finite values.
Results may differ from a plain program's by a relative error of at most 0.002.
The roundings to bfloat16 on the way count: a program that leaves them out, or rounds other values in their place, can miss the bound.
Values may be sent and summed in bfloat16 or wider, within the bound.
No kernel may reach another device: no remote copies, remote signals or barrier semaphores. Data moves between devices by JAX's collectives and lax.ppermute only.
A program may use at most 128 MiB of HBM per device.

v0:
```python
import jax
import jax.numpy as jnp
from jax import lax
from jax.sharding import PartitionSpec as P

ITERS = 3
BLOCK = 128
PIX = 256


def with_halo(cells, sides, width):
    for axis, dim in sides:
        count = lax.axis_size(axis)
        ends = count - 1
        head = lax.slice_in_dim(cells, 0, width, axis=dim)
        tail = lax.slice_in_dim(cells, cells.shape[dim] - width, cells.shape[dim], axis=dim)
        cells = jnp.concatenate(
            [
                lax.ppermute(tail, axis, [(i, (i + 1) % count) for i in range(ends)]),
                cells,
                lax.ppermute(head, axis, [((i + 1) % count, i) for i in range(ends)]),
            ],
            axis=dim,
        )
    return cells


def orth(rows):
    result = []
    for index in range(rows.shape[0]):
        vector = rows[index]
        for done in result:
            vector = vector - jnp.sum(vector * done) * done
        result.append(vector / jnp.sqrt(jnp.sum(vector * vector)))
    return jnp.stack(result)


def shards(tod, taps, modes_init, weights, block_tile, block_offset):
    dish_dev, chans, tdev = tod.shape
    width = taps.shape[0]
    reach = (width - 1) // 2
    extended = with_halo(tod, (("tm", 2),), reach)
    source = jnp.arange(tdev + 2 * reach, dtype=jnp.int32)[:, None]
    target = jnp.arange(tdev, dtype=jnp.int32)[None, :]
    lag = source - target
    band = jnp.zeros((tdev + 2 * reach, tdev), jnp.float32)
    for index in range(width):
        band = jnp.where(lag == index, taps[index], band)
    lowpass = jnp.dot(extended.reshape(-1, tdev + 2 * reach), band, precision=lax.Precision.HIGHEST)
    filtered = tod - lowpass.reshape(tod.shape)
    contract = (((0, 2), (0, 2)), ((), ()))
    local_cov = lax.dot_general(filtered, filtered, contract, precision=lax.Precision.HIGHEST)
    cov = lax.psum(local_cov, ("tm", "dish"))
    basis = orth(modes_init)
    for step in range(ITERS):
        basis = orth(jnp.dot(basis, cov, precision=lax.Precision.HIGHEST))
    amounts = jnp.einsum("mc,dct->dmt", basis, filtered, precision=lax.Precision.HIGHEST)
    cleaned = filtered - jnp.einsum("mc,dmt->dct", basis, amounts, precision=lax.Precision.HIGHEST)
    weighted = (weights[:, None, :] * cleaned).astype(jnp.bfloat16)
    per_dish = tdev // BLOCK
    count_blocks = dish_dev * per_dish
    blocks = (
        weighted.reshape(dish_dev, chans, per_dish, BLOCK)
        .transpose(0, 2, 1, 3)
        .reshape(count_blocks, chans, BLOCK)
    )
    owners_of = block_tile.reshape(count_blocks)
    offsets = block_offset.reshape(count_blocks)
    owners = lax.axis_size("tm")
    within = jnp.arange(BLOCK, dtype=jnp.int32)
    most = max(2, (2 * count_blocks + owners - 1) // owners)
    order = jnp.arange(count_blocks, dtype=jnp.int32)
    alike = (owners_of[:, None] == owners_of[None, :]) & (order[None, :] < order[:, None])
    slot = owners_of * most + jnp.sum(alike.astype(jnp.int32), axis=1)
    slots_all = jnp.arange(owners * most, dtype=jnp.int32)
    placing = slots_all[:, None] == slot[None, :]
    outgoing = jnp.einsum(
        "sn,nck->sck", placing.astype(jnp.bfloat16), blocks, preferred_element_type=jnp.float32
    ).astype(jnp.bfloat16)
    places = jnp.sum(jnp.where(placing, offsets[None, :] + 1, 0), axis=1) - 1
    arrived = lax.all_to_all(
        outgoing.reshape(owners, most, chans, BLOCK), "tm", split_axis=0, concat_axis=0, tiled=True
    )
    arrived_places = lax.all_to_all(
        places.reshape(owners, most), "tm", split_axis=0, concat_axis=0, tiled=True
    ).reshape(-1)
    pixel = (arrived_places[:, None] + within[None, :]) % PIX
    onto = (pixel[:, :, None] == jnp.arange(PIX, dtype=jnp.int32)[None, None, :]) & (
        arrived_places >= 0
    )[:, None, None]
    partial_value = jnp.einsum(
        "sck,skp->cp",
        arrived.reshape(owners * most, chans, BLOCK),
        onto.astype(jnp.bfloat16),
        preferred_element_type=jnp.float32,
    )[None]
    return lax.psum_scatter(partial_value, "dish", scatter_dimension=1, tiled=True)


def solution(mesh):
    placed = (P("dish", None, "tm"), P(), P(), P("dish", "tm"), P("dish", "tm"), P("dish", "tm"))
    return jax.shard_map(
        shards, mesh=mesh, in_specs=placed, out_specs=P("tm", "dish", None), check_vma=False
    )
```

profile of v0, /device:TPU:0, one launch (start us, length us, event | category | flops | bytes accessed | tf_op | source)
XLA Modules:
  0.0 641.2 jit_solution(10626276267643632908)
XLA Ops:
  6.5 9.2 %copy.34 = f32[8,1024,256]{1,2,0:T(8,128)} copy(f32[8,1024,256]{2,1,0:T(8,128)} %param.6) | data formatting | bytes 16777216 | tf_op args[0]
  15.7 1.7 fusion.424
  17.4 3.5 collective-permute-start
  21.0 1.3 collective-permute-start.1
  23.6 9.8 %all-to-all-start.1 = ((s32[16,1,2]{2,1,0:T(1,128)}), s32[16,1,2]{2,1,0:T(1,128)S(1)}, u32[]{:S(2)}, u32[]{:S(2)}) async-start(s32[16,1,2]{2,1,0:T(1,128)} %bitcast.98), calls=%async_computation.1 | async-start | bytes 16384 | tf_op jit(solution)/shard_map/all_to_all | solution.py:84
  37.6 5.7 collective-permute-done
  43.3 4.3 collective-permute-done.1
  47.6 65.4 %fusion.12 = f32[8,1024,256]{2,1,0:T(8,128)S(1)} fusion(f32[8,1024,256]{2,1,0:T(8,128)} %param.6, f32[8,1024,32]{1,2,0:T(8,128)} %collective-permute-done.1, f32[8,1024,256]{1,2,0:T(8,128)} %copy.34, f32[8,1024,32]{1,2,0:T(8,128)S(1)} %collective-permute-done, f32[]{:T(128)} %bitcast.65, f32[]{:T(128)} %bitcast.64, f32[]{:T(128)} %bitcast.63, f32[]{:T(128)} %bitcast.62, ...), kind=kOutput, calls=%fused_computation.15 | convolution fusion | flops 8071135232 | bytes 27263236 | tf_op jit(solution)/shard_map/dot_general | solution.py:49
  113.0 3.2 copy-done
  116.2 28.2 %convolution_bitcast_fusion = f32[1024,1024]{1,0:T(8,128)} fusion(f32[8,1024,256]{2,1,0:T(8,128)S(1)} %fusion.12), kind=kOutput, calls=%fused_computation.16 | convolution fusion | flops 25769803776 | bytes 12582912 | tf_op jit(solution)/shard_map/dot_general | solution.py:52
  145.1 1.2 multiply_reduce_fusion.68
  147.0 3.8 multiply_reduce_fusion.67
  150.8 1.9 multiply_reduce_fusion.78
  153.3 1.8 multiply_reduce_fusion.75
  155.0 3.8 multiply_reduce_fusion.66
  159.5 2.5 multiply_reduce_fusion.65
  162.0 2.5 multiply_reduce_fusion.69
  165.1 2.5 multiply_reduce_fusion.64
  167.6 1.2 multiply_reduce_fusion.63
  169.4 9.4 %subtract_divide_fusion.15 = (f32[1,1024]{1,0:T(1,128)S(1)}, f32[1,1024]{1,0:T(1,128)S(1)}, f32[1,1024]{1,0:T(1,128)S(1)}, f32[1,1024]{1,0:T(1,128)S(1)}, f32[1,1024]{1,0:T(1,128)S(1)}) fusion(f32[1,1024]{1,0:T(1,128)S(1)} %get-tuple-element.148, f32[]{:T(128)S(6)} %sqrt.77, f32[]{:T(128)} %get-tuple-element.114, f32[]{:T(128)} %get-tuple-element.23, ...), kind=kLoop, calls=%fused_computation.420 | loop fusion | flops 35840 | bytes 45136 | tf_op jit(solution)/shard_map/div | solution.py:34
  178.8 124.2 %all-reduce.2.cloned.1.call-done = f32[1024,1024]{1,0:T(8,128)} async-done(((f32[1024,1024]{1,0:T(8,128)}), f32[1024,1024]{1,0:T(8,128)}) %all-reduce.2.cloned.1.call-update) | async-done | bytes 4194320 | tf_op jit(solution)/shard_map/psum | solution.py:53
  303.0 4.3 fusion.434
  309.2 1.3 multiply_reduce_fusion.47
  311.2 3.9 multiply_reduce_fusion.46
  315.0 1.8 multiply_reduce_fusion.57
  317.5 1.9 multiply_reduce_fusion.54
  319.4 3.6 multiply_reduce_fusion.45
  323.7 2.4 multiply_reduce_fusion.44
  326.1 2.3 multiply_reduce_fusion.48
  329.1 2.4 multiply_reduce_fusion.43
  331.5 1.2 multiply_reduce_fusion.42
  333.4 9.3 %subtract_divide_fusion.10 = (f32[1,1024]{1,0:T(1,128)S(1)}, f32[1,1024]{1,0:T(1,128)S(1)}, f32[1,1024]{1,0:T(1,128)S(1)}, f32[1,1024]{1,0:T(1,128)S(1)}, f32[1,1024]{1,0:T(1,128)S(1)}) fusion(f32[1,1024]{1,0:T(1,128)S(1)} %get-tuple-element.142, f32[]{:T(128)S(6)} %sqrt.83, f32[]{:T(128)} %get-tuple-element.98, f32[]{:T(128)} %get-tuple-element.17, ...), kind=kLoop, calls=%fused_computation.380 | loop fusion | flops 35840 | bytes 45136 | tf_op jit(solution)/shard_map/div | solution.py:34
  342.8 4.3 fusion.435
  349.0 1.3 multiply_reduce_fusion.26
  351.0 3.9 multiply_reduce_fusion.25
  354.8 1.8 multiply_reduce_fusion.36
  357.3 1.9 multiply_reduce_fusion.33
  359.2 3.6 multiply_reduce_fusion.24
  363.5 2.4 multiply_reduce_fusion.23
  365.9 2.3 multiply_reduce_fusion.27
  368.9 2.4 multiply_reduce_fusion.22
  371.3 1.2 multiply_reduce_fusion.21
  373.2 9.3 %subtract_divide_fusion.5 = (f32[1,1024]{1,0:T(1,128)S(1)}, f32[1,1024]{1,0:T(1,128)S(1)}, f32[1,1024]{1,0:T(1,128)S(1)}, f32[1,1024]{1,0:T(1,128)S(1)}, f32[1,1024]{1,0:T(1,128)S(1)}) fusion(f32[1,1024]{1,0:T(1,128)S(1)} %get-tuple-element.136, f32[]{:T(128)S(6)} %sqrt.89, f32[]{:T(128)} %get-tuple-element.82, f32[]{:T(128)} %get-tuple-element.11, ...), kind=kLoop, calls=%fused_computation.340 | loop fusion | flops 35840 | bytes 45136 | tf_op jit(solution)/shard_map/div | solution.py:34
  382.6 4.3 fusion.436
  388.6 1.2 multiply_reduce_fusion.5
  390.6 3.6 multiply_reduce_fusion.4
  394.2 1.8 multiply_reduce_fusion.15
  396.7 1.9 multiply_reduce_fusion.12
  398.6 3.8 multiply_reduce_fusion.3
  403.0 2.6 multiply_reduce_fusion.2
  405.7 2.6 multiply_reduce_fusion.6
  408.9 2.5 multiply_reduce_fusion.1
  411.5 1.2 multiply_reduce_fusion
  413.3 9.4 %subtract_divide_fusion = (f32[1,1024]{1,0:T(1,128)S(1)}, f32[1,1024]{1,0:T(1,128)S(1)}, f32[1,1024]{1,0:T(1,128)S(1)}, f32[1,1024]{1,0:T(1,128)S(1)}, f32[1,1024]{1,0:T(1,128)S(1)}) fusion(f32[1,1024]{1,0:T(1,128)S(1)} %get-tuple-element.130, f32[]{:T(128)S(6)} %sqrt.95, f32[]{:T(128)} %get-tuple-element.66, f32[]{:T(128)} %get-tuple-element.5, ...), kind=kLoop, calls=%fused_computation.300 | loop fusion | flops 35840 | bytes 45136 | tf_op jit(solution)/shard_map/div | solution.py:34
  422.7 6.7 %convolution_bitcast_fusion.1 = f32[8,6,256]{2,1,0:T(8,128)S(1)} fusion(f32[8,1024,256]{2,1,0:T(8,128)} %copy-done, f32[6,1024]{1,0:T(8,128)S(1)} %stack.11), kind=kOutput, calls=%fused_computation.20 | convolution fusion | flops 150994944 | bytes 8462336 | tf_op jit(solution)/shard_map/mc,dct->dmt/dot_general | solution.py:57
  429.5 9.7 %fusion.7 = bf16[8,1024,256]{2,1,0:T(8,128)(2,1)S(1)} fusion(f32[8,1024,256]{2,1,0:T(8,128)} %copy-done, f32[8,256]{1,0:T(8,128)S(1)} %copy-done.3, f32[8,6,256]{2,1,0:T(8,128)S(1)} %convolution_bitcast_fusion.1, f32[6,1024]{1,0:T(8,128)S(1)} %stack.11), kind=kOutput, calls=%fused_computation.8 | convolution fusion | flops 157286400 | bytes 12664832 | tf_op jit(solution)/shard_map/mc,dmt->dct/dot_general | solution.py:58
  439.2 1.1 fusion.425
  440.5 9.5 %convolution_convert_fusion = bf16[32,1024,128]{2,0,1:T(8,128)(2,1)S(1)} fusion(bf16[16,1024,128]{2,1,0:T(8,128)(2,1)S(1)} %bitcast.129, s32[16]{0:T(128)S(1)} %multiply_add_fusion), kind=kOutput, calls=%fused_computation.9 | convolution fusion | flops 138412544 | bytes 12582976 | tf_op jit(solution)/shard_map/sn,nck->sck/dot_general | solution.py:77
  450.1 7.0 %copy.39 = bf16[16,2,1024,128]{3,1,2,0:T(2,128)(2,1)} copy(bf16[16,2,1024,128]{3,1,0,2:T(2,128)(2,1)S(1)} %bitcast.128) | data formatting | bytes 16777216 | tf_op jit(solution)/shard_map/reshape | solution.py:82
  457.1 5.6 all-to-all-start
  464.3 123.2 %all-to-all-done = bf16[16,2,1024,128]{3,1,2,0:T(2,128)(2,1)} async-done(((bf16[16,2,1024,128]{3,1,2,0:T(2,128)(2,1)}), bf16[16,2,1024,128]{3,1,2,0:T(2,128)(2,1)}, u32[]{:S(2)}, u32[]{:S(2)}) %all-to-all-start) | async-done | bytes 8388640 | tf_op jit(solution)/shard_map/all_to_all | solution.py:81
  587.5 8.6 %copy.40 = bf16[16,2,1024,128]{3,2,1,0:T(8,128)(2,1)} copy(bf16[16,2,1024,128]{3,1,2,0:T(2,128)(2,1)} %all-to-all-done) | data formatting | bytes 16777216 | tf_op jit(solution)/shard_map/all_to_all | solution.py:81
  596.1 6.8 %fusion.17 = f32[1,1024,256]{2,1,0:T(8,128)} fusion(bf16[32,1024,128]{2,1,0:T(8,128)(2,1)} %bitcast.130, s32[32,128]{1,0:T(8,128)S(1)} %add_select_fusion, pred[32]{0:T(512)(128)(4,1)S(1)} %broadcast_compare_fusion), kind=kOutput, calls=%fused_computation.19 | convolution fusion | flops 2149580800 | bytes 9453600 | tf_op jit(solution)/shard_map/sck,skp->cp/dot_general | solution.py:91
  603.0 30.9 %reduce-scatter.2.cloned.1.call-done = f32[1,128,256]{2,1,0:T(8,128)} async-done(((f32[1,1024,256]{2,1,0:T(8,128)}), f32[1,128,256]{2,1,0:T(8,128)}) %reduce-scatter.2.cloned.1.call-update) | async-done | bytes 131088 | tf_op jit(solution)/shard_map/reduce_scatter | solution.py:97
  (52 shorter events, 11.4 us)
Async XLA Ops:
  6.5 15.7 %copy-start.4 = (s32[8,2]{0,1:T(2,128)S(1)}, s32[8,2]{0,1:T(2,128)}, u32[]{:S(2)}) copy-start(s32[8,2]{0,1:T(2,128)} %param.10) | copy-start | bytes 196
  6.5 16.1 %copy-start.5 = (s32[8,2]{0,1:T(2,128)S(1)}, s32[8,2]{0,1:T(2,128)}, u32[]{:S(2)}) copy-start(s32[8,2]{0,1:T(2,128)} %param.11) | copy-start | bytes 196
  6.5 26.9 %copy-start.2 = (f32[6,1024]{1,0:T(8,128)S(1)}, f32[6,1024]{1,0:T(8,128)}, u32[]{:S(2)}) copy-start(f32[6,1024]{1,0:T(8,128)} %param.8) | copy-start | bytes 73732
  6.5 28.2 %copy-start.1 = (f32[65]{0:T(128)S(1)}, f32[65]{0:T(128)}, u32[]{:S(2)}) copy-start(f32[65]{0:T(128)} %param.7) | copy-start | bytes 784
  17.4 25.9 %collective-permute-start = (f32[8,1024,32]{1,2,0:T(8,128)S(1)}, f32[8,1024,32]{1,2,0:T(8,128)S(1)}, u32[]{:S(2)}, u32[]{:S(2)}) collective-permute-start(f32[8,1024,32]{1,2,0:T(8,128)S(1)} %get-tuple-element.125), channel_id=1, source_target_pairs={{0,8},{8,16},{16,24},{24,32},{32,40},{40,48},{48,56},{56,64},{64,7... | collective-permute-start | bytes 3145736 | tf_op jit(solution)/shard_map/ppermute | solution.py:19
  21.0 26.7 %collective-permute-start.1 = (f32[8,1024,32]{1,2,0:T(8,128)S(1)}, f32[8,1024,32]{1,2,0:T(8,128)}, u32[]{:S(2)}, u32[]{:S(2)}) collective-permute-start(f32[8,1024,32]{1,2,0:T(8,128)S(1)} %get-tuple-element.126), channel_id=1, source_target_pairs={{8,0},{16,8},{24,16},{32,24},{40,32},{48,40},{56,48},{64,56},{72,6... | collective-permute-start | bytes 3145736 | tf_op jit(solution)/shard_map/ppermute | solution.py:21
  23.6 433.5 %all-to-all-start.1 = ((s32[16,1,2]{2,1,0:T(1,128)}), s32[16,1,2]{2,1,0:T(1,128)S(1)}, u32[]{:S(2)}, u32[]{:S(2)}) async-start(s32[16,1,2]{2,1,0:T(1,128)} %bitcast.98), calls=%async_computation.1 | async-start | bytes 16384 | tf_op jit(solution)/shard_map/all_to_all | solution.py:84
  33.4 269.6 %all-reduce.2.cloned.1.call-start = ((), (), s32[]{:S(2)}) async-start(), calls=%async_computation.3 | async-start | bytes 8388608 | tf_op jit(solution)/shard_map/psum | solution.py:53
  113.0 3.2 copy-start
  342.8 86.7 %copy-start.3 = (f32[8,256]{1,0:T(8,128)S(1)}, f32[8,256]{1,0:T(8,128)}, u32[]{:S(2)}) copy-start(f32[8,256]{1,0:T(8,128)} %param.9) | copy-start | bytes 24580
  457.1 130.5 %all-to-all-start = ((bf16[16,2,1024,128]{3,1,2,0:T(2,128)(2,1)}), bf16[16,2,1024,128]{3,1,2,0:T(2,128)(2,1)}, u32[]{:S(2)}, u32[]{:S(2)}) async-start(bf16[16,2,1024,128]{3,1,2,0:T(2,128)(2,1)} %copy.39), calls=%async_computation | async-start | bytes 16777216 | tf_op jit(solution)/shard_map/all_to_all | solution.py:81
  462.6 171.3 %reduce-scatter.2.cloned.1.call-start = ((), (), s32[]{:S(2)}) async-start(), calls=%async_computation.4 | async-start | bytes 1179648 | tf_op jit(solution)/shard_map/reduce_scatter | solution.py:97
Sparse Core Ops, SparseCore 0:
  144.6 158.3 all-reduce.1
  603.1 30.7 reduce-scatter.1
where the time goes:
time: 653 us; the launch traced here: 641 us
  waiting for transfers between devices  288 us (44%)
  matrix products  139 us (21%)
  other arithmetic  128 us (20%)
  local copies, waits for them, and re-layouts  35.5 us (5%)
  between operations  29.7 us (5%)
  starting transfers between devices  20.5 us (3%)
    psum x1, waiting for transfers between devices, shards(): cov = lax.psum(local_cov, ('tm', 'dish'))  124 us
    all_to_all x1, waiting for transfers between devices, shards(): lax.all_to_all(outgoing.reshape(owners, most, chans, BLOCK), 'tm', split_...  123 us
    dot_general x1, matrix products, shards(): jnp.dot(extended.reshape(-1, tdev + 2 * reach), band, precision=lax.Preci...  65.4 us
    reduce_sum x28, other arithmetic, orth(): vector = vector - jnp.sum(vector * done) * done  64.7 us
    div x4, other arithmetic, orth(): result.append(vector / jnp.sqrt(jnp.sum(vector * vector)))  37.4 us
    reduce_scatter x1, waiting for transfers between devices, shards(): lax.psum_scatter(partial_value, 'dish', scatter_dimension=1, tiled=True)  30.9 us
    dot_general x1, matrix products, shards(): lax.dot_general(filtered, filtered, contract, precision=lax.Precision.HIG...  28.2 us
    reduce_sum x16, other arithmetic, orth(): result.append(vector / jnp.sqrt(jnp.sum(vector * vector)))  24.6 us
  transfers between devices with their start and end apart: 6, of which 5 were waited for; matrix products, arithmetic and copies ran while one was open for 43% of the time, Pallas kernels for 0%

commit v1 on v0

v1 whole, which is shorter than its diff:
```python
import jax
import jax.numpy as jnp
from jax import lax
from jax.experimental import pallas as pl
from jax.experimental.pallas import tpu as pltpu
from jax.sharding import Mesh
from jax.sharding import PartitionSpec as P

ITERS = 3
BLOCK = 128
PIX = 256
MODES = 6
ROWS = 8
CHIPS = 4
CORES = 2
F32 = jnp.float32
BF16 = jnp.bfloat16
PARAMS = pltpu.CompilerParams(vmem_limit_bytes=24 * 1024 * 1024)
VMEM = pl.BlockSpec(memory_space=pltpu.VMEM)
SMEM = pl.BlockSpec(memory_space=pltpu.SMEM)
LAST = (((1,), (1,)), ((), ()))


def split(value, pieces):
    result = []
    for _ in range(pieces):
        piece = value.astype(BF16)
        result.append(piece)
        value = value - piece.astype(F32)
    return result


def rows_of(pieces):
    return jnp.concatenate([piece.astype(F32) for piece in pieces], axis=0).astype(BF16)


def folded(product, pieces):
    total = product[0:ROWS]
    for index in range(1, pieces):
        total = total + product[index * ROWS:(index + 1) * ROWS]
    return total


def mxu(left, right):
    return jnp.dot(left, right, preferred_element_type=F32)


def mxu_last(left, right):
    return lax.dot_general(left, right, LAST, preferred_element_type=F32)


def orth(rows):
    row = lax.broadcasted_iota(jnp.int32, rows.shape, 0)
    for index in range(MODES):
        vector = rows[index:index + 1]
        inner = jnp.sum(rows * vector, axis=1, keepdims=True)
        square = inner[index:index + 1]
        later = rows - (inner / square) * vector
        unit = vector / jnp.sqrt(square)
        rows = jnp.where(row == index, unit, jnp.where(row > index, later, rows))
    return jnp.where(row < MODES, rows, 0.0)


def pack_kernel(reach, tod_ref, head_ref, tail_ref):
    groups = BLOCK // reach
    dishes, chans, tdev = tod_ref.shape
    size = chans // groups
    lane = lax.broadcasted_iota(jnp.int32, (size, BLOCK), 1) // reach

    def body(dish, carry):
        head = jnp.zeros((size, BLOCK), F32)
        tail = jnp.zeros((size, BLOCK), F32)
        for group in range(groups):
            rows = pl.ds(group * size, size)
            first = tod_ref[dish, rows, 0:BLOCK]
            last = tod_ref[dish, rows, tdev - BLOCK:tdev]
            if group:
                first = pltpu.roll(first, group * reach, 1)
            move = (group * reach + reach) % BLOCK
            if move:
                last = pltpu.roll(last, move, 1)
            head = jnp.where(lane == group, first, head)
            tail = jnp.where(lane == group, last, tail)
        head_ref[dish] = head
        tail_ref[dish] = tail
        return carry

    lax.fori_loop(0, dishes, body, 0)


def taps_at(taps_ref, lag):
    def body(index, band):
        return jnp.where(lag == index, taps_ref[index], band)

    return lax.fori_loop(0, taps_ref.shape[0], body, jnp.zeros(lag.shape, F32), unroll=5)


def own_kernel(reach, taps_ref, modes_ref, tod_ref, basis_ref, fix_ref, own_ref, band):
    dishes, chans, tdev = tod_ref.shape
    groups = BLOCK // reach
    part = 64
    source = lax.broadcasted_iota(jnp.int32, (part, tdev), 0)
    target = lax.broadcasted_iota(jnp.int32, (part, tdev), 1)
    for start in range(0, tdev, part):
        pieces = split(taps_at(taps_ref, source + (start + reach) - target), 2)
        band[0, start:start + part] = pieces[0]
        band[1, start:start + part] = pieces[1]
    source = lax.broadcasted_iota(jnp.int32, (reach, tdev), 0)
    target = lax.broadcasted_iota(jnp.int32, (reach, tdev), 1)
    fix_ref[...] = jnp.zeros_like(fix_ref)
    for side, shift in ((0, 0), (1, tdev + reach)):
        pieces = split(taps_at(taps_ref, source + shift - target), 2)
        for group in range(groups):
            rows = pl.ds(side * BLOCK + group * reach, reach)
            fix_ref[0, group, rows, :] = pieces[0]
            fix_ref[1, group, rows, :] = pieces[1]
    basis_ref[...] = orth(modes_ref[...])
    size = 256

    def body(dish, carry):
        for start in range(0, chans, size):
            rows = pl.ds(start, size)
            series = tod_ref[dish, rows, :]
            high, low = split(series, 2)
            lowpass = mxu(high, band[0]) + (mxu(high, band[1]) + mxu(low, band[0]))
            own_ref[dish, rows, :] = series - lowpass
        return carry

    lax.fori_loop(0, dishes, body, 0)


def step(basis, high_ref, mid_ref):
    dishes, chans = high_ref.shape[0], high_ref.shape[1]
    left = rows_of(split(basis, 2))
    amounts = []
    for dish in range(dishes):
        product = folded(mxu(left, high_ref[dish]) + mxu(left, mid_ref[dish]), 2)
        amounts.append(rows_of(split(product, 2)))
    total = jnp.zeros((2 * ROWS, chans), F32)
    for dish in range(dishes):
        total = total + (
            mxu_last(amounts[dish], high_ref[dish]) + mxu_last(amounts[dish], mid_ref[dish])
        )
    return folded(total, 2)


def edge_kernel(basis_ref, fix_ref, own_ref, left_ref, right_ref, pointing_ref,
                high_ref, mid_ref, low_ref, total_ref):
    dishes, chans = own_ref.shape[0], own_ref.shape[1]
    groups = fix_ref.shape[1]
    size = chans // groups

    def body(dish, carry):
        edges = jnp.concatenate([left_ref[dish], right_ref[dish]], axis=1)
        high, low = split(edges, 2)
        for group in range(groups):
            rows = pl.ds(group * size, size)
            lowpass = mxu(high, fix_ref[0, group]) + (
                mxu(high, fix_ref[1, group]) + mxu(low, fix_ref[0, group])
            )
            pieces = split(own_ref[dish, rows, :] - lowpass, 3)
            high_ref[dish, rows, :] = pieces[0]
            mid_ref[dish, rows, :] = pieces[1]
            low_ref[dish, rows, :] = pieces[2]
        return carry

    lax.fori_loop(0, dishes, body, 0)
    total_ref[...] = step(basis_ref[...], high_ref, mid_ref)
    total_ref[MODES:MODES + 1] = pointing_ref[...]


def step_kernel(sums_ref, high_ref, mid_ref, total_ref):
    total_ref[...] = step(orth(sums_ref[...]), high_ref, mid_ref)


def clean_kernel(sums_ref, weight_ref, high_ref, mid_ref, low_ref, out_ref):
    dishes, chans, tdev = high_ref.shape
    basis = split(orth(sums_ref[...]), 3)
    left = rows_of(basis)
    spread = rows_of([basis[i] for i in (0, 0, 0, 1, 1, 2)])
    per_dish = tdev // BLOCK
    owned = chans // (CHIPS * CORES)
    part = owned // CHIPS

    def body(dish, carry):
        product = mxu(left, low_ref[dish]) + mxu(left, mid_ref[dish]) + mxu(left, high_ref[dish])
        amounts = split(folded(product, 3), 3)
        right = rows_of([amounts[i] for i in (0, 1, 2, 0, 1, 0)])
        weight = weight_ref[dish]
        for group in range(CHIPS * CORES):
            rows = pl.ds(group * owned, owned)
            filtered = (low_ref[dish, rows, :].astype(F32) + mid_ref[dish, rows, :].astype(F32)
                        ) + high_ref[dish, rows, :].astype(F32)
            removed = lax.dot_general(
                spread[:, group * owned:(group + 1) * owned], right,
                (((0,), (0,)), ((), ())), preferred_element_type=F32,
            )
            weighted = (weight * (filtered - removed)).astype(BF16)
            for chip in range(CHIPS):
                for block in range(per_dish):
                    out_ref[chip * CHIPS * CORES + group, dish * per_dish + block] = weighted[
                        chip * part:(chip + 1) * part, block * BLOCK:(block + 1) * BLOCK
                    ]
        return carry

    lax.fori_loop(0, dishes, body, 0)


def bin_kernel(pointing_ref, blocks_ref, sky_ref):
    sky_ref[...] = jnp.zeros_like(sky_ref)
    sources, count, chans, width = blocks_ref.shape
    lane = lax.broadcasted_iota(jnp.int32, (chans, width), 1)

    def body(source, carry):
        for block in range(count):
            where = source * 2 * count + block
            tile = pointing_ref[where]
            offset = pointing_ref[where + count]
            half = offset // width
            shift = offset - half * width
            moved = pltpu.roll(blocks_ref[source, block].astype(F32), shift, 1)
            first = jnp.where((lane >= shift) == (half == 0), moved, 0.0)
            sky_ref[tile, :, 0:width] += first
            sky_ref[tile, :, width:2 * width] += moved - first
        return carry

    lax.fori_loop(0, sources, body, 0)


def call(kernel, name, out_shape, in_specs, scratch=()):
    several = isinstance(out_shape, (list, tuple))
    return pl.pallas_call(
        kernel,
        out_shape=out_shape,
        in_specs=in_specs,
        out_specs=[VMEM] * len(out_shape) if several else VMEM,
        scratch_shapes=scratch,
        compiler_params=PARAMS,
        name=name,
    )


def total_over(value, axes):
    for axis in axes:
        count = lax.axis_size(axis)
        parts = [value] + [
            lax.ppermute(value, axis, [(i, (i + s) % count) for i in range(count)])
            for s in range(1, count)
        ]
        while len(parts) > 1:
            parts = [a + b for a, b in zip(parts[::2], parts[1::2])]
        value = parts[0]
    return value


def shards(tod, taps, modes_init, weights, block_tile, block_offset):
    dishes, chans, tdev = tod.shape
    reach = (taps.shape[0] - 1) // 2
    groups = BLOCK // reach
    size = chans // groups
    per_dish = tdev // BLOCK
    times = CHIPS * CHIPS
    sharers = CHIPS * CHIPS * CORES
    part = chans // sharers
    rows_f32 = jax.ShapeDtypeStruct((ROWS, chans), F32)
    edge_f32 = jax.ShapeDtypeStruct((dishes, size, BLOCK), F32)
    piece = pltpu.VMEM((dishes, chans, tdev), BF16)

    with jax.named_scope("edges"):
        head, tail = call(
            lambda *refs: pack_kernel(reach, *refs), "pack", [edge_f32] * 2, [VMEM]
        )(tod)
        ends = times - 1
        from_left = lax.ppermute(tail, ("z", "x"), [(i, i + 1) for i in range(ends)])
        from_right = lax.ppermute(head, ("z", "x"), [(i + 1, i) for i in range(ends)])

    with jax.named_scope("own"):
        modes = jnp.pad(modes_init, ((0, ROWS - MODES), (0, 0)))
        basis, fix, own = call(
            lambda *refs: own_kernel(reach, *refs), "own",
            [rows_f32, jax.ShapeDtypeStruct((2, groups, tdev, tdev), BF16),
             pltpu.VMEM((dishes, chans, tdev), F32)],
            [SMEM, VMEM, VMEM],
            [pltpu.VMEM((2, tdev, tdev), BF16)],
        )(taps, modes, tod)

    with jax.named_scope("pointing"):
        mine = jnp.concatenate([block_tile.reshape(-1), block_offset.reshape(-1)]).astype(F32)
        slot = jnp.arange(sharers, dtype=jnp.int32)[:, None] == lax.axis_index(("x", "y", "c"))
        pointing = jnp.where(slot, mine[None, :], 0.0).reshape(1, sharers * mine.shape[0])

    with jax.named_scope("filtered"):
        high, mid, low, sums = call(
            edge_kernel, "edge", [piece, piece, piece, rows_f32], [VMEM] * 6
        )(basis, fix, own, from_left, from_right, pointing)

    with jax.named_scope("iterations"):
        sums = total_over(sums, ("c", "y", "x"))
        pointing = sums[MODES].astype(jnp.int32)
        sums = total_over(sums, ("z",))
        for _ in range(ITERS - 1):
            sums = call(step_kernel, "step", rows_f32, [VMEM] * 3)(sums, high, mid)
            sums = total_over(sums, ("c", "y", "x", "z"))

    with jax.named_scope("cleaned"):
        blocks = call(
            clean_kernel, "clean",
            jax.ShapeDtypeStruct((sharers, dishes * per_dish, part, BLOCK), BF16), [VMEM] * 5,
        )(sums, weights.reshape(dishes, 1, tdev), high, mid, low)

    with jax.named_scope("channels"):
        arrived = lax.all_to_all(blocks, ("x", "y", "c"), 0, 0, tiled=True)

    with jax.named_scope("binning"):
        sky = call(
            bin_kernel, "bin", jax.ShapeDtypeStruct((times, part, PIX), F32), [SMEM, VMEM]
        )(pointing, arrived)

    with jax.named_scope("tiles"):
        parts = lax.all_to_all(sky, ("z", "x"), 0, 0, tiled=True)
        parts = parts.reshape(CHIPS, CHIPS * part, PIX)
        return jnp.sum(parts, axis=0, keepdims=True)


def solution(mesh):
    chips = Mesh(mesh.devices.reshape(CHIPS, CHIPS, CHIPS, CORES), ("z", "x", "y", "c"))
    dish, time = ("y", "c"), ("z", "x")
    placed = (P(dish, None, time), P(), P(), P(dish, time), P(dish, time), P(dish, time))
    return jax.shard_map(
        shards, mesh=chips, in_specs=placed, out_specs=P(time, dish, None), check_vma=False
    )
```

time: 653 us -> 223 us (0.34); the launches traced: 641 us -> 222 us
  waiting for transfers between devices: 288 us -> 99.5 us
  matrix products: 139 us -> 0 us
  other arithmetic: 128 us -> 0.95 us
  Pallas kernels: 0 us -> 43.1 us
  starting transfers between devices: 20.5 us -> 53.1 us
  between operations: 29.7 us -> 0.23 us
  local copies, waits for them, and re-layouts: 35.5 us -> 9.23 us
  blocking collectives: 0 us -> 15.7 us
    dot_general x9 -> x0, matrix products: 139 us -> none  [the longest x1 65.4 us: shards(): jnp.dot(extended.reshape(-1, tdev + 2 * reach), band, precision=lax.Preci...]
    psum x1 -> x0, waiting for transfers between devices: 124 us -> none  [shards(): cov = lax.psum(local_cov, ('tm', 'dish'))]
    reduce_sum x46 -> x1, other arithmetic: 89.6 us -> 0.69 us  [shards(): return jnp.sum(parts, axis=0, keepdims=True)]
    all_to_all x2 -> x1, waiting for transfers between devices: 123 us -> 52.8 us  [shards(): arrived = lax.all_to_all(blocks, ('x', 'y', 'c'), 0, 0, tiled=True)]
    pallas_call x0 -> x7, Pallas kernels: none -> 43.1 us  [the longest x1 8.62 us: shards(): call(edge_kernel, 'edge', [piece, piece, piece, rows_f32], [VMEM] * 6)]
    ppermute x2 -> x32, starting transfers between devices: 4.84 us -> 47.8 us  [the longest x30 43 us: total_over(): lax.ppermute(value, axis, [(i, (i + s) % count) for i in range(count)])]
    div x4 -> x0, other arithmetic: 37.4 us -> none  [orth(): result.append(vector / jnp.sqrt(jnp.sum(vector * vector)))]
    ppermute x2 -> x32, waiting for transfers between devices: 9.98 us -> 46.7 us  [the longest x30 33.3 us: total_over(): lax.ppermute(value, axis, [(i, (i + s) % count) for i in range(count)])]
  transfers between devices with their start and end apart: 6 -> 33, of which waited for: 5 -> 30; matrix products, arithmetic and copies ran while one was open for 43% -> 0% of each run, Pallas kernels for 0% -> 3%
where the time goes in v1:
time: 223 us; the launch traced here: 222 us
  waiting for transfers between devices  99.5 us (45%)
  starting transfers between devices  53.1 us (24%)
  Pallas kernels  43.1 us (19%)
  blocking collectives  15.7 us (7%)
  local copies, waits for them, and re-layouts  9.23 us (4%)
    all_to_all x1, waiting for transfers between devices, shards(): arrived = lax.all_to_all(blocks, ('x', 'y', 'c'), 0, 0, tiled=True)  52.8 us
    ppermute x30, starting transfers between devices, total_over(): lax.ppermute(value, axis, [(i, (i + s) % count) for i in range(count)])  43 us
    ppermute x30, waiting for transfers between devices, total_over(): lax.ppermute(value, axis, [(i, (i + s) % count) for i in range(count)])  33.3 us
    all_to_all x1, blocking collectives, shards(): parts = lax.all_to_all(sky, ('z', 'x'), 0, 0, tiled=True)  15.7 us
    ppermute x1, waiting for transfers between devices, shards(): lax.ppermute(tail, ('z', 'x'), [(i, i + 1) for i in range(ends)])  9.58 us
    unnamed x18, local copies, waits for them, and re-layouts  8.97 us
    pallas_call x1, Pallas kernels, shards(): call(edge_kernel, 'edge', [piece, piece, piece, rows_f32], [VMEM] * 6)  8.62 us
    pallas_call x1, Pallas kernels, shards(): call(bin_kernel, 'bin', jax.ShapeDtypeStruct((times, part, PIX), F32), [S...  8.02 us
  transfers between devices with their start and end apart: 33, of which 30 were waited for; matrix products, arithmetic and copies ran while one was open for 0% of the time, Pallas kernels for 3%

profile of v1, /device:TPU:0, one launch (start us, length us, event | category | flops | bytes accessed | tf_op | source)
XLA Modules:
  0.0 221.8 jit_solution(10514689777756196017)
XLA Ops:
  0.0 3.4 %copy-done = f32[8,1024,256]{2,1,0:T(8,128)S(1)} copy-done((f32[8,1024,256]{2,1,0:T(8,128)S(1)}, f32[8,1024,256]{2,1,0:T(8,128)}, u32[]{:S(2)}) %copy-start) | copy-done | bytes 8388632
  3.4 3.1 %pack.1 = (f32[8,256,128]{2,1,0:T(8,128)S(1)}, f32[8,256,128]{2,1,0:T(8,128)}) custom-call(f32[8,1024,256]{2,1,0:T(8,128)S(1)} %copy-done), custom_call_target="tpu_custom_call" | custom-call | tf_op jit(solution)/shard_map/edges/pack/pallas_call | solution.py:270
  6.5 3.5 %collective-permute-start = (f32[8,256,128]{2,1,0:T(8,128)}, f32[8,256,128]{2,1,0:T(8,128)S(1)}, u32[]{:S(2)}, u32[]{:S(2)}) collective-permute-start(f32[8,256,128]{2,1,0:T(8,128)} %get-tuple-element.17), channel_id=1, source_target_pairs={{0,8},{8,16},{16,24},{24,32},{32,40},{40,48},{48,56},{56,64},{64,7... | collective-permute-start | bytes 3145736 | tf_op jit(solution)/shard_map/edges/ppermute | solution.py:274
  10.1 1.3 collective-permute-start.1
  12.0 3.4 %copy-done.1 = f32[8,1024,256]{2,1,0:T(8,128)S(1)} copy-done((f32[8,1024,256]{2,1,0:T(8,128)S(1)}, f32[8,1024,256]{2,1,0:T(8,128)}, u32[]{:S(2)}) %copy-start.1) | copy-done | bytes 8388632
  15.4 7.8 %own.1 = (f32[8,1024]{1,0:T(8,128)S(1)}, bf16[2,4,256,256]{3,2,1,0:T(8,128)(2,1)S(1)}, f32[8,1024,256]{2,1,0:T(8,128)S(1)}) custom-call(f32[65]{0:T(128)S(1)} %copy-done.3, f32[8,1024]{1,0:T(8,128)S(1)} %pad.4.refs_1_, f32[8,1024,256]{2,1,0:T(8,128)S(1)} %copy-done.1), custom_call_target="tpu_custom_call" | custom-call | tf_op jit(solution)/shard_map/own/own/pallas_call | solution.py:279
  23.1 9.6 %collective-permute-done.left_ref = f32[8,256,128]{2,1,0:T(8,128)S(1)} collective-permute-done((f32[8,256,128]{2,1,0:T(8,128)}, f32[8,256,128]{2,1,0:T(8,128)S(1)}, u32[]{:S(2)}, u32[]{:S(2)}) %collective-permute-start) | collective-permute-done | bytes 1048608 | tf_op jit(solution)/shard_map/edges/ppermute | solution.py:274
  32.7 3.9 %collective-permute-done.1.right_ref = f32[8,256,128]{2,1,0:T(8,128)S(1)} collective-permute-done((f32[8,256,128]{2,1,0:T(8,128)S(1)}, f32[8,256,128]{2,1,0:T(8,128)S(1)}, u32[]{:S(2)}, u32[]{:S(2)}) %collective-permute-start.1) | collective-permute-done | bytes 1048608 | tf_op jit(solution)/shard_map/edges/ppermute | solution.py:275
  36.6 8.6 %edge.1 = (bf16[8,1024,256]{2,1,0:T(8,128)(2,1)S(1)}, bf16[8,1024,256]{2,1,0:T(8,128)(2,1)S(1)}, bf16[8,1024,256]{2,1,0:T(8,128)(2,1)S(1)}, f32[8,1024]{1,0:T(8,128)S(1)}) custom-call(f32[8,1024]{1,0:T(8,128)S(1)} %get-tuple-element.14.basis_ref, bf16[2,4,256,256]{3,2,1,0:T(8,128)(2,1)S(1)} %get-tuple-element.15.fix_ref, ...), custom_call_target="tpu_custom_call" | custom-call | tf_op jit(solution)/shard_map/filtered/edge/pallas_call | solution.py:293
  45.2 1.2 collective-permute-done.2
  46.4 1.6 collective-permute-start.3
  48.0 2.9 %collective-permute-start.4 = (f32[8,1024]{1,0:T(8,128)S(1)}, f32[8,1024]{1,0:T(8,128)S(1)}, u32[]{:S(2)}, u32[]{:S(2)}) collective-permute-start(f32[8,1024]{1,0:T(8,128)S(1)} %add.100), channel_id=1, source_target_pairs={{0,4},{2,6},{4,0},{6,2},{1,5},{3,7},{5,1},{7,3},{8,12},{10,14},{12... | collective-permute-start | bytes 98312 | tf_op jit(solution)/shard_map/iterations/ppermute | solution.py:247
  50.9 1.3 collective-permute-start.5
  52.3 1.2 collective-permute-done.4
  53.4 1.4 collective-permute-done.5
  54.8 1.5 collective-permute-start.6
  56.3 5.2 %collective-permute-start.7 = (f32[8,1024]{1,0:T(8,128)S(1)}, f32[8,1024]{1,0:T(8,128)S(1)}, u32[]{:S(2)}, u32[]{:S(2)}) collective-permute-start(f32[8,1024]{1,0:T(8,128)S(1)} %add_add_fusion.8), channel_id=1, source_target_pairs={{0,16},{8,24},{16,0},{24,8},{1,17},{9,25},{17,1},{25,9},{2,18},{10... | collective-permute-start | bytes 98312 | tf_op jit(solution)/shard_map/iterations/ppermute | solution.py:247
  61.5 0.4 collective-permute-done.6
  62.0 1.8 collective-permute-done.7
  63.8 1.7 collective-permute-done.8
  65.5 3.7 %collective-permute-start.10 = (f32[8,1024]{1,0:T(8,128)S(1)}, f32[8,1024]{1,0:T(8,128)S(1)}, u32[]{:S(2)}, u32[]{:S(2)}) collective-permute-start(f32[8,1024]{1,0:T(8,128)S(1)} %add_add_fusion.7), channel_id=1, source_target_pairs={{0,64},{32,96},{64,0},{96,32},{1,65},{33,97},{65,1},{97,33},{2,66}... | collective-permute-start | bytes 98312 | tf_op jit(solution)/shard_map/iterations/ppermute | solution.py:247
  69.1 1.0 collective-permute-start.11
  70.1 1.0 collective-permute-start.9
  71.1 1.9 collective-permute-done.11
  73.0 2.2 collective-permute-done.9
  75.3 3.9 %step.2 = f32[8,1024]{1,0:T(8,128)S(1)} custom-call(f32[8,1024]{1,0:T(8,128)S(1)} %add_add_fusion.6.sums_ref, bf16[8,1024,256]{2,1,0:T(8,128)(2,1)S(1)} %get-tuple-element.20.high_ref, bf16[8,1024,256]{2,1,0:T(8,128)(2,1)S(1)} %get-tuple-element.21.mid_ref), custom_call_target="tpu_custom_call" | custom-call | tf_op jit(solution)/shard_map/iterations/step/pallas_call | solution.py:302
  79.2 1.2 collective-permute-done.12
  80.6 3.8 %collective-permute-start.14 = (f32[8,1024]{1,0:T(8,128)S(1)}, f32[8,1024]{1,0:T(8,128)S(1)}, u32[]{:S(2)}, u32[]{:S(2)}) collective-permute-start(f32[8,1024]{1,0:T(8,128)S(1)} %add.110), channel_id=1, source_target_pairs={{0,4},{2,6},{4,0},{6,2},{1,5},{3,7},{5,1},{7,3},{8,12},{10,14},{12... | collective-permute-start | bytes 98312 | tf_op jit(solution)/shard_map/iterations/ppermute | solution.py:247
  84.6 1.0 collective-permute-done.13
  85.6 1.1 collective-permute-done.14
  86.7 1.7 collective-permute-done.15
  88.4 2.7 %collective-permute-start.17 = (f32[8,1024]{1,0:T(8,128)S(1)}, f32[8,1024]{1,0:T(8,128)S(1)}, u32[]{:S(2)}, u32[]{:S(2)}) collective-permute-start(f32[8,1024]{1,0:T(8,128)S(1)} %add_add_fusion.5), channel_id=1, source_target_pairs={{0,16},{8,24},{16,0},{24,8},{1,17},{9,25},{17,1},{25,9},{2,18},{10... | collective-permute-start | bytes 98312 | tf_op jit(solution)/shard_map/iterations/ppermute | solution.py:247
  91.1 1.5 collective-permute-start.18
  92.6 1.0 collective-permute-done.16
  93.9 1.1 collective-permute-done.18
  95.3 1.5 collective-permute-start.20
  96.8 1.8 collective-permute-start.21
  98.5 1.9 collective-permute-done.19
  100.4 0.4 collective-permute-done.20
  100.8 0.8 collective-permute-done.21
  101.7 3.9 %step.3 = f32[8,1024]{1,0:T(8,128)S(1)} custom-call(f32[8,1024]{1,0:T(8,128)S(1)} %add_add_fusion.3.sums_ref, bf16[8,1024,256]{2,1,0:T(8,128)(2,1)S(1)} %get-tuple-element.20.high_ref, bf16[8,1024,256]{2,1,0:T(8,128)(2,1)S(1)} %get-tuple-element.21.mid_ref), custom_call_target="tpu_custom_call" | custom-call | tf_op jit(solution)/shard_map/iterations/step/pallas_call | solution.py:302
  105.6 1.2 collective-permute-done.22
  106.9 2.7 %collective-permute-start.24 = (f32[8,1024]{1,0:T(8,128)S(1)}, f32[8,1024]{1,0:T(8,128)S(1)}, u32[]{:S(2)}, u32[]{:S(2)}) collective-permute-start(f32[8,1024]{1,0:T(8,128)S(1)} %add.120), channel_id=1, source_target_pairs={{0,4},{2,6},{4,0},{6,2},{1,5},{3,7},{5,1},{7,3},{8,12},{10,14},{12... | collective-permute-start | bytes 98312 | tf_op jit(solution)/shard_map/iterations/ppermute | solution.py:247
  109.6 1.3 collective-permute-start.25
  110.9 1.5 collective-permute-done.23
  112.4 1.1 collective-permute-done.25
  113.5 1.5 collective-permute-start.26
  115.0 2.7 %collective-permute-start.27 = (f32[8,1024]{1,0:T(8,128)S(1)}, f32[8,1024]{1,0:T(8,128)S(1)}, u32[]{:S(2)}, u32[]{:S(2)}) collective-permute-start(f32[8,1024]{1,0:T(8,128)S(1)} %add_add_fusion.2), channel_id=1, source_target_pairs={{0,16},{8,24},{16,0},{24,8},{1,17},{9,25},{17,1},{25,9},{2,18},{10... | collective-permute-start | bytes 98312 | tf_op jit(solution)/shard_map/iterations/ppermute | solution.py:247
  117.8 0.9 collective-permute-done.26
  118.7 1.7 collective-permute-done.27
  120.4 1.2 collective-permute-done.28
  121.7 1.7 collective-permute-start.29
  123.4 2.2 collective-permute-start.30
  125.6 0.6 collective-permute-start.31
  126.2 0.7 collective-permute-done.29
  126.9 2.0 collective-permute-done.30
  128.8 0.7 collective-permute-done.31
  129.5 7.8 %clean.1 = bf16[32,16,32,128]{3,2,1,0:T(8,128)(2,1)S(1)} custom-call(f32[8,1024]{1,0:T(8,128)S(1)} %add_add_fusion.sums_ref, f32[8,1,256]{2,1,0:T(1,128)S(1)} %reshape.55.weight_ref, bf16[8,1024,256]{2,1,0:T(8,128)(2,1)S(1)} %get-tuple-element.20.high_ref, bf16[8,1024,256]{2,1,0:T(8,128)(2,1)S(1)} %get-tuple-element.21.mid_ref, ...), custom_call_target="tpu_custom_call" | custom-call | tf_op jit(solution)/shard_map/cleaned/clean/pallas_call | solution.py:306
  137.3 2.0 copy-done.2
  139.3 5.3 %all-to-all-start = ((bf16[32,16,32,128]{3,2,1,0:T(8,128)(2,1)}), bf16[32,16,32,128]{3,2,1,0:T(8,128)(2,1)}, u32[]{:S(2)}, u32[]{:S(2)}) async-start(bf16[32,16,32,128]{3,2,1,0:T(8,128)(2,1)} %copy-done.2), calls=%async_computation | async-start | bytes 8388608 | tf_op jit(solution)/shard_map/channels/all_to_all | solution.py:312
  144.7 52.8 %all-to-all-done.blocks_ref = bf16[32,16,32,128]{3,2,1,0:T(8,128)(2,1)} async-done(((bf16[32,16,32,128]{3,2,1,0:T(8,128)(2,1)}), bf16[32,16,32,128]{3,2,1,0:T(8,128)(2,1)}, u32[]{:S(2)}, u32[]{:S(2)}) %all-to-all-start) | async-done | bytes 4194336 | tf_op jit(solution)/shard_map/channels/all_to_all | solution.py:312
  197.4 8.0 %bin.1 = f32[16,32,256]{2,1,0:T(8,128)S(1)} custom-call(s32[1024]{0:T(1024)S(1)} %bitcast.5, bf16[32,16,32,128]{3,2,1,0:T(8,128)(2,1)} %all-to-all-done.blocks_ref), custom_call_target="tpu_custom_call" | custom-call | tf_op jit(solution)/shard_map/binning/bin/pallas_call | solution.py:315
  205.5 15.7 %all_to_all.10 = f32[16,32,256]{2,1,0:T(8,128)S(1)} all-to-all(f32[16,32,256]{2,1,0:T(8,128)S(1)} %bin.1), channel_id=1, replica_groups=mesh['z'=4,'x'=4,'y'=4,'c'=2] {'z','x'}, dimensions={0} | all-to-all | bytes 1048576 | tf_op jit(solution)/shard_map/tiles/all_to_all | solution.py:320
  221.1 0.7 bitcast_reduce_fusion
  (50 shorter events, 1.9 us)
Async XLA Ops:
  0.0 3.4 %copy-start = (f32[8,1024,256]{2,1,0:T(8,128)S(1)}, f32[8,1024,256]{2,1,0:T(8,128)}, u32[]{:S(2)}) copy-start(f32[8,1024,256]{2,1,0:T(8,128)} %refs_0_.3) | copy-start | bytes 25165828
  3.4 8.0 %copy-start.6 = (s32[8,2]{0,1:T(2,128)S(1)}, s32[8,2]{0,1:T(2,128)}, u32[]{:S(2)}) copy-start(s32[8,2]{0,1:T(2,128)} %param.10) | copy-start | bytes 196
  3.4 8.2 %copy-start.7 = (s32[8,2]{0,1:T(2,128)S(1)}, s32[8,2]{0,1:T(2,128)}, u32[]{:S(2)}) copy-start(s32[8,2]{0,1:T(2,128)} %param.11) | copy-start | bytes 196
  3.4 8.6 %copy-start.4 = (f32[6,1024]{1,0:T(8,128)S(1)}, f32[6,1024]{1,0:T(8,128)}, u32[]{:S(2)}) copy-start(f32[6,1024]{1,0:T(8,128)} %param.8) | copy-start | bytes 73732
  3.4 8.6 %copy-start.3 = (f32[65]{0:T(128)S(1)}, f32[65]{0:T(128)}, u32[]{:S(2)}) copy-start(f32[65]{0:T(128)} %refs_0_.2) | copy-start | bytes 784
  6.5 26.2 %collective-permute-start = (f32[8,256,128]{2,1,0:T(8,128)}, f32[8,256,128]{2,1,0:T(8,128)S(1)}, u32[]{:S(2)}, u32[]{:S(2)}) collective-permute-start(f32[8,256,128]{2,1,0:T(8,128)} %get-tuple-element.17), channel_id=1, source_target_pairs={{0,8},{8,16},{16,24},{24,32},{32,40},{40,48},{48,56},{56,64},{64,7... | collective-permute-start | bytes 3145736 | tf_op jit(solution)/shard_map/edges/ppermute | solution.py:274
  10.1 26.5 %collective-permute-start.1 = (f32[8,256,128]{2,1,0:T(8,128)S(1)}, f32[8,256,128]{2,1,0:T(8,128)S(1)}, u32[]{:S(2)}, u32[]{:S(2)}) collective-permute-start(f32[8,256,128]{2,1,0:T(8,128)S(1)} %get-tuple-element.18), channel_id=1, source_target_pairs={{8,0},{16,8},{24,16},{32,24},{40,32},{48,40},{56,48},{64,56},{72,6... | collective-permute-start | bytes 3145736 | tf_op jit(solution)/shard_map/edges/ppermute | solution.py:275
  12.0 3.4 %copy-start.1 = (f32[8,1024,256]{2,1,0:T(8,128)S(1)}, f32[8,1024,256]{2,1,0:T(8,128)}, u32[]{:S(2)}) copy-start(f32[8,1024,256]{2,1,0:T(8,128)} %refs_0_.3) | copy-start | bytes 25165828
  45.2 1.2 collective-permute-start.2
  46.4 5.8 %collective-permute-start.3 = (f32[8,1024]{1,0:T(8,128)S(1)}, f32[8,1024]{1,0:T(8,128)S(1)}, u32[]{:S(2)}, u32[]{:S(2)}) collective-permute-start(f32[8,1024]{1,0:T(8,128)S(1)} %add.100), channel_id=1, source_target_pairs={{0,2},{2,4},{4,6},{6,0},{1,3},{3,5},{5,7},{7,1},{8,10},{10,12},{12... | collective-permute-start | bytes 98312 | tf_op jit(solution)/shard_map/iterations/ppermute | solution.py:247
  48.0 5.4 %collective-permute-start.4 = (f32[8,1024]{1,0:T(8,128)S(1)}, f32[8,1024]{1,0:T(8,128)S(1)}, u32[]{:S(2)}, u32[]{:S(2)}) collective-permute-start(f32[8,1024]{1,0:T(8,128)S(1)} %add.100), channel_id=1, source_target_pairs={{0,4},{2,6},{4,0},{6,2},{1,5},{3,7},{5,1},{7,3},{8,12},{10,14},{12... | collective-permute-start | bytes 98312 | tf_op jit(solution)/shard_map/iterations/ppermute | solution.py:247
  50.9 3.9 %collective-permute-start.5 = (f32[8,1024]{1,0:T(8,128)S(1)}, f32[8,1024]{1,0:T(8,128)S(1)}, u32[]{:S(2)}, u32[]{:S(2)}) collective-permute-start(f32[8,1024]{1,0:T(8,128)S(1)} %add.100), channel_id=1, source_target_pairs={{0,6},{2,0},{4,2},{6,4},{1,7},{3,1},{5,3},{7,5},{8,14},{10,8},{12,... | collective-permute-start | bytes 98312 | tf_op jit(solution)/shard_map/iterations/ppermute | solution.py:247
  54.8 7.1 %collective-permute-start.6 = (f32[8,1024]{1,0:T(8,128)S(1)}, f32[8,1024]{1,0:T(8,128)S(1)}, u32[]{:S(2)}, u32[]{:S(2)}) collective-permute-start(f32[8,1024]{1,0:T(8,128)S(1)} %add_add_fusion.8), channel_id=1, source_target_pairs={{0,8},{8,16},{16,24},{24,0},{1,9},{9,17},{17,25},{25,1},{2,10},{10... | collective-permute-start | bytes 98312 | tf_op jit(solution)/shard_map/iterations/ppermute | solution.py:247
  56.3 7.4 %collective-permute-start.7 = (f32[8,1024]{1,0:T(8,128)S(1)}, f32[8,1024]{1,0:T(8,128)S(1)}, u32[]{:S(2)}, u32[]{:S(2)}) collective-permute-start(f32[8,1024]{1,0:T(8,128)S(1)} %add_add_fusion.8), channel_id=1, source_target_pairs={{0,16},{8,24},{16,0},{24,8},{1,17},{9,25},{17,1},{25,9},{2,18},{10... | collective-permute-start | bytes 98312 | tf_op jit(solution)/shard_map/iterations/ppermute | solution.py:247
  61.5 3.9 %collective-permute-start.8 = (f32[8,1024]{1,0:T(8,128)S(1)}, f32[8,1024]{1,0:T(8,128)S(1)}, u32[]{:S(2)}, u32[]{:S(2)}) collective-permute-start(f32[8,1024]{1,0:T(8,128)S(1)} %add_add_fusion.8), channel_id=1, source_target_pairs={{0,24},{8,0},{16,8},{24,16},{1,25},{9,1},{17,9},{25,17},{2,26},{10... | collective-permute-start | bytes 98312 | tf_op jit(solution)/shard_map/iterations/ppermute | solution.py:247
  65.5 5.7 %collective-permute-start.10 = (f32[8,1024]{1,0:T(8,128)S(1)}, f32[8,1024]{1,0:T(8,128)S(1)}, u32[]{:S(2)}, u32[]{:S(2)}) collective-permute-start(f32[8,1024]{1,0:T(8,128)S(1)} %add_add_fusion.7), channel_id=1, source_target_pairs={{0,64},{32,96},{64,0},{96,32},{1,65},{33,97},{65,1},{97,33},{2,66}... | collective-permute-start | bytes 98312 | tf_op jit(solution)/shard_map/iterations/ppermute | solution.py:247
  69.1 3.9 %collective-permute-start.11 = (f32[8,1024]{1,0:T(8,128)S(1)}, f32[8,1024]{1,0:T(8,128)S(1)}, u32[]{:S(2)}, u32[]{:S(2)}) collective-permute-start(f32[8,1024]{1,0:T(8,128)S(1)} %add_add_fusion.7), channel_id=1, source_target_pairs={{0,96},{32,0},{64,32},{96,64},{1,97},{33,1},{65,33},{97,65},{2,98}... | collective-permute-start | bytes 98312 | tf_op jit(solution)/shard_map/iterations/ppermute | solution.py:247
  70.1 5.1 %collective-permute-start.9 = (f32[8,1024]{1,0:T(8,128)S(1)}, f32[8,1024]{1,0:T(8,128)S(1)}, u32[]{:S(2)}, u32[]{:S(2)}) collective-permute-start(f32[8,1024]{1,0:T(8,128)S(1)} %add_add_fusion.7), channel_id=1, source_target_pairs={{0,32},{32,64},{64,96},{96,0},{1,33},{33,65},{65,97},{97,1},{2,34}... | collective-permute-start | bytes 98312 | tf_op jit(solution)/shard_map/iterations/ppermute | solution.py:247
  79.2 1.2 collective-permute-start.12
  80.4 5.1 %collective-permute-start.13 = (f32[8,1024]{1,0:T(8,128)S(1)}, f32[8,1024]{1,0:T(8,128)S(1)}, u32[]{:S(2)}, u32[]{:S(2)}) collective-permute-start(f32[8,1024]{1,0:T(8,128)S(1)} %add.110), channel_id=1, source_target_pairs={{0,2},{2,4},{4,6},{6,0},{1,3},{3,5},{5,7},{7,1},{8,10},{10,12},{12... | collective-permute-start | bytes 98312 | tf_op jit(solution)/shard_map/iterations/ppermute | solution.py:247
  80.6 6.1 %collective-permute-start.14 = (f32[8,1024]{1,0:T(8,128)S(1)}, f32[8,1024]{1,0:T(8,128)S(1)}, u32[]{:S(2)}, u32[]{:S(2)}) collective-permute-start(f32[8,1024]{1,0:T(8,128)S(1)} %add.110), channel_id=1, source_target_pairs={{0,4},{2,6},{4,0},{6,2},{1,5},{3,7},{5,1},{7,3},{8,12},{10,14},{12... | collective-permute-start | bytes 98312 | tf_op jit(solution)/shard_map/iterations/ppermute | solution.py:247
  84.4 3.9 %collective-permute-start.15 = (f32[8,1024]{1,0:T(8,128)S(1)}, f32[8,1024]{1,0:T(8,128)S(1)}, u32[]{:S(2)}, u32[]{:S(2)}) collective-permute-start(f32[8,1024]{1,0:T(8,128)S(1)} %add.110), channel_id=1, source_target_pairs={{0,6},{2,0},{4,2},{6,4},{1,7},{3,1},{5,3},{7,5},{8,14},{10,8},{12,... | collective-permute-start | bytes 98312 | tf_op jit(solution)/shard_map/iterations/ppermute | solution.py:247
  88.4 5.2 %collective-permute-start.16 = (f32[8,1024]{1,0:T(8,128)S(1)}, f32[8,1024]{1,0:T(8,128)S(1)}, u32[]{:S(2)}, u32[]{:S(2)}) collective-permute-start(f32[8,1024]{1,0:T(8,128)S(1)} %add_add_fusion.5), channel_id=1, source_target_pairs={{0,8},{8,16},{16,24},{24,0},{1,9},{9,17},{17,25},{25,1},{2,10},{10... | collective-permute-start | bytes 98312 | tf_op jit(solution)/shard_map/iterations/ppermute | solution.py:247
  88.4 5.5 %collective-permute-start.17 = (f32[8,1024]{1,0:T(8,128)S(1)}, f32[8,1024]{1,0:T(8,128)S(1)}, u32[]{:S(2)}, u32[]{:S(2)}) collective-permute-start(f32[8,1024]{1,0:T(8,128)S(1)} %add_add_fusion.5), channel_id=1, source_target_pairs={{0,16},{8,24},{16,0},{24,8},{1,17},{9,25},{17,1},{25,9},{2,18},{10... | collective-permute-start | bytes 98312 | tf_op jit(solution)/shard_map/iterations/ppermute | solution.py:247
  91.1 3.9 %collective-permute-start.18 = (f32[8,1024]{1,0:T(8,128)S(1)}, f32[8,1024]{1,0:T(8,128)S(1)}, u32[]{:S(2)}, u32[]{:S(2)}) collective-permute-start(f32[8,1024]{1,0:T(8,128)S(1)} %add_add_fusion.5), channel_id=1, source_target_pairs={{0,24},{8,0},{16,8},{24,16},{1,25},{9,1},{17,9},{25,17},{2,26},{10... | collective-permute-start | bytes 98312 | tf_op jit(solution)/shard_map/iterations/ppermute | solution.py:247
  95.0 5.4 %collective-permute-start.19 = (f32[8,1024]{1,0:T(8,128)S(1)}, f32[8,1024]{1,0:T(8,128)S(1)}, u32[]{:S(2)}, u32[]{:S(2)}) collective-permute-start(f32[8,1024]{1,0:T(8,128)S(1)} %add_add_fusion.4), channel_id=1, source_target_pairs={{0,32},{32,64},{64,96},{96,0},{1,33},{33,65},{65,97},{97,1},{2,34}... | collective-permute-start | bytes 98312 | tf_op jit(solution)/shard_map/iterations/ppermute | solution.py:247
  95.3 5.5 %collective-permute-start.20 = (f32[8,1024]{1,0:T(8,128)S(1)}, f32[8,1024]{1,0:T(8,128)S(1)}, u32[]{:S(2)}, u32[]{:S(2)}) collective-permute-start(f32[8,1024]{1,0:T(8,128)S(1)} %add_add_fusion.4), channel_id=1, source_target_pairs={{0,64},{32,96},{64,0},{96,32},{1,65},{33,97},{65,1},{97,33},{2,66}... | collective-permute-start | bytes 98312 | tf_op jit(solution)/shard_map/iterations/ppermute | solution.py:247
  96.8 4.9 %collective-permute-start.21 = (f32[8,1024]{1,0:T(8,128)S(1)}, f32[8,1024]{1,0:T(8,128)S(1)}, u32[]{:S(2)}, u32[]{:S(2)}) collective-permute-start(f32[8,1024]{1,0:T(8,128)S(1)} %add_add_fusion.4), channel_id=1, source_target_pairs={{0,96},{32,0},{64,32},{96,64},{1,97},{33,1},{65,33},{97,65},{2,98}... | collective-permute-start | bytes 98312 | tf_op jit(solution)/shard_map/iterations/ppermute | solution.py:247
  101.6 24.5 %copy-start.5 = (f32[8,256]{1,0:T(8,128)S(1)}, f32[8,256]{1,0:T(8,128)}, u32[]{:S(2)}) copy-start(f32[8,256]{1,0:T(8,128)} %param.9) | copy-start | bytes 24580
  105.6 1.2 collective-permute-start.22
  106.8 5.6 %collective-permute-start.23 = (f32[8,1024]{1,0:T(8,128)S(1)}, f32[8,1024]{1,0:T(8,128)S(1)}, u32[]{:S(2)}, u32[]{:S(2)}) collective-permute-start(f32[8,1024]{1,0:T(8,128)S(1)} %add.120), channel_id=1, source_target_pairs={{0,2},{2,4},{4,6},{6,0},{1,3},{3,5},{5,7},{7,1},{8,10},{10,12},{12... | collective-permute-start | bytes 98312 | tf_op jit(solution)/shard_map/iterations/ppermute | solution.py:247
  106.9 5.5 %collective-permute-start.24 = (f32[8,1024]{1,0:T(8,128)S(1)}, f32[8,1024]{1,0:T(8,128)S(1)}, u32[]{:S(2)}, u32[]{:S(2)}) collective-permute-start(f32[8,1024]{1,0:T(8,128)S(1)} %add.120), channel_id=1, source_target_pairs={{0,4},{2,6},{4,0},{6,2},{1,5},{3,7},{5,1},{7,3},{8,12},{10,14},{12... | collective-permute-start | bytes 98312 | tf_op jit(solution)/shard_map/iterations/ppermute | solution.py:247
  109.6 3.9 %collective-permute-start.25 = (f32[8,1024]{1,0:T(8,128)S(1)}, f32[8,1024]{1,0:T(8,128)S(1)}, u32[]{:S(2)}, u32[]{:S(2)}) collective-permute-start(f32[8,1024]{1,0:T(8,128)S(1)} %add.120), channel_id=1, source_target_pairs={{0,6},{2,0},{4,2},{6,4},{1,7},{3,1},{5,3},{7,5},{8,14},{10,8},{12,... | collective-permute-start | bytes 98312 | tf_op jit(solution)/shard_map/iterations/ppermute | solution.py:247
  113.5 5.2 %collective-permute-start.26 = (f32[8,1024]{1,0:T(8,128)S(1)}, f32[8,1024]{1,0:T(8,128)S(1)}, u32[]{:S(2)}, u32[]{:S(2)}) collective-permute-start(f32[8,1024]{1,0:T(8,128)S(1)} %add_add_fusion.2), channel_id=1, source_target_pairs={{0,8},{8,16},{16,24},{24,0},{1,9},{9,17},{17,25},{25,1},{2,10},{10... | collective-permute-start | bytes 98312 | tf_op jit(solution)/shard_map/iterations/ppermute | solution.py:247
  115.0 5.4 %collective-permute-start.27 = (f32[8,1024]{1,0:T(8,128)S(1)}, f32[8,1024]{1,0:T(8,128)S(1)}, u32[]{:S(2)}, u32[]{:S(2)}) collective-permute-start(f32[8,1024]{1,0:T(8,128)S(1)} %add_add_fusion.2), channel_id=1, source_target_pairs={{0,16},{8,24},{16,0},{24,8},{1,17},{9,25},{17,1},{25,9},{2,18},{10... | collective-permute-start | bytes 98312 | tf_op jit(solution)/shard_map/iterations/ppermute | solution.py:247
  117.7 3.9 %collective-permute-start.28 = (f32[8,1024]{1,0:T(8,128)S(1)}, f32[8,1024]{1,0:T(8,128)S(1)}, u32[]{:S(2)}, u32[]{:S(2)}) collective-permute-start(f32[8,1024]{1,0:T(8,128)S(1)} %add_add_fusion.2), channel_id=1, source_target_pairs={{0,24},{8,0},{16,8},{24,16},{1,25},{9,1},{17,9},{25,17},{2,26},{10... | collective-permute-start | bytes 98312 | tf_op jit(solution)/shard_map/iterations/ppermute | solution.py:247
  121.7 5.2 %collective-permute-start.29 = (f32[8,1024]{1,0:T(8,128)S(1)}, f32[8,1024]{1,0:T(8,128)S(1)}, u32[]{:S(2)}, u32[]{:S(2)}) collective-permute-start(f32[8,1024]{1,0:T(8,128)S(1)} %add_add_fusion.1), channel_id=1, source_target_pairs={{0,32},{32,64},{64,96},{96,0},{1,33},{33,65},{65,97},{97,1},{2,34}... | collective-permute-start | bytes 98312 | tf_op jit(solution)/shard_map/iterations/ppermute | solution.py:247
  123.4 5.4 %collective-permute-start.30 = (f32[8,1024]{1,0:T(8,128)S(1)}, f32[8,1024]{1,0:T(8,128)S(1)}, u32[]{:S(2)}, u32[]{:S(2)}) collective-permute-start(f32[8,1024]{1,0:T(8,128)S(1)} %add_add_fusion.1), channel_id=1, source_target_pairs={{0,64},{32,96},{64,0},{96,32},{1,65},{33,97},{65,1},{97,33},{2,66}... | collective-permute-start | bytes 98312 | tf_op jit(solution)/shard_map/iterations/ppermute | solution.py:247
  125.6 3.9 %collective-permute-start.31 = (f32[8,1024]{1,0:T(8,128)S(1)}, f32[8,1024]{1,0:T(8,128)S(1)}, u32[]{:S(2)}, u32[]{:S(2)}) collective-permute-start(f32[8,1024]{1,0:T(8,128)S(1)} %add_add_fusion.1), channel_id=1, source_target_pairs={{0,96},{32,0},{64,32},{96,64},{1,97},{33,1},{65,33},{97,65},{2,98}... | collective-permute-start | bytes 98312 | tf_op jit(solution)/shard_map/iterations/ppermute | solution.py:247
  137.3 2.0 copy-start.2
  139.3 58.1 %all-to-all-start = ((bf16[32,16,32,128]{3,2,1,0:T(8,128)(2,1)}), bf16[32,16,32,128]{3,2,1,0:T(8,128)(2,1)}, u32[]{:S(2)}, u32[]{:S(2)}) async-start(bf16[32,16,32,128]{3,2,1,0:T(8,128)(2,1)} %copy-done.2), calls=%async_computation | async-start | bytes 8388608 | tf_op jit(solution)/shard_map/channels/all_to_all | solution.py:312

commit v2 on v1

--- a/solution.py
+++ b/solution.py
@@ -15,7 +15,7 @@
 CORES = 2
 F32 = jnp.float32
 BF16 = jnp.bfloat16
-PARAMS = pltpu.CompilerParams(vmem_limit_bytes=24 * 1024 * 1024)
+PARAMS = pltpu.CompilerParams(vmem_limit_bytes=16 * 1024 * 1024)
 VMEM = pl.BlockSpec(memory_space=pltpu.VMEM)
 SMEM = pl.BlockSpec(memory_space=pltpu.SMEM)
 LAST = (((1,), (1,)), ((), ()))
@@ -50,15 +50,15 @@
 
 
 def orth(rows):
-    row = lax.broadcasted_iota(jnp.int32, rows.shape, 0)
+    row = lax.broadcasted_iota(jnp.int32, (rows.shape[0], 1), 0)
+    squares = jnp.ones((rows.shape[0], 1), F32)
     for index in range(MODES):
         vector = rows[index:index + 1]
         inner = jnp.sum(rows * vector, axis=1, keepdims=True)
         square = inner[index:index + 1]
-        later = rows - (inner / square) * vector
-        unit = vector / jnp.sqrt(square)
-        rows = jnp.where(row == index, unit, jnp.where(row > index, later, rows))
-    return jnp.where(row < MODES, rows, 0.0)
+        squares = jnp.where(row == index, square, squares)
+        rows = rows - jnp.where(row > index, inner / square, 0.0) * vector
+    return jnp.where(row < MODES, rows / jnp.sqrt(squares), 0.0)
 
 
 def pack_kernel(reach, tod_ref, head_ref, tail_ref):
@@ -173,67 +173,84 @@
     total_ref[...] = step(orth(sums_ref[...]), high_ref, mid_ref)
 
 
-def clean_kernel(sums_ref, weight_ref, high_ref, mid_ref, low_ref, out_ref):
+def clean_kernel(sums_ref, weight_ref, high_ref, mid_ref, low_ref, out_ref,
+                 weighted_ref, sems, amounts_ref, spread_ref):
     dishes, chans, tdev = high_ref.shape
     basis = split(orth(sums_ref[...]), 3)
-    left = rows_of(basis)
-    spread = rows_of([basis[i] for i in (0, 0, 0, 1, 1, 2)])
+    left = rows_of(basis[:2])
+    wide = [basis[i].astype(F32) for i in (0, 0, 0, 1, 1, 2)]
+    spread_ref[...] = jnp.concatenate(wide, axis=0).T.astype(BF16)
+    for dish in range(dishes):
+        product = folded(mxu(left, high_ref[dish]) + mxu(left, mid_ref[dish]), 2)
+        amounts = split(product, 3)
+        amounts_ref[dish] = rows_of([amounts[i] for i in (0, 1, 2, 0, 1, 0)])
     per_dish = tdev // BLOCK
     owned = chans // (CHIPS * CORES)
     part = owned // CHIPS
 
+    def copy_of(dish):
+        blocks = pl.ds(dish * per_dish, per_dish)
+        return pltpu.make_async_copy(
+            weighted_ref.at[dish], out_ref.at[:, blocks], sems.at[dish]
+        )
+
     def body(dish, carry):
-        product = mxu(left, low_ref[dish]) + mxu(left, mid_ref[dish]) + mxu(left, high_ref[dish])
-        amounts = split(folded(product, 3), 3)
-        right = rows_of([amounts[i] for i in (0, 1, 2, 0, 1, 0)])
+        removed = mxu(spread_ref[...], amounts_ref[dish])
         weight = weight_ref[dish]
-        for group in range(CHIPS * CORES):
-            rows = pl.ds(group * owned, owned)
-            filtered = (low_ref[dish, rows, :].astype(F32) + mid_ref[dish, rows, :].astype(F32)
-                        ) + high_ref[dish, rows, :].astype(F32)
-            removed = lax.dot_general(
-                spread[:, group * owned:(group + 1) * owned], right,
-                (((0,), (0,)), ((), ())), preferred_element_type=F32,
-            )
-            weighted = (weight * (filtered - removed)).astype(BF16)
-            for chip in range(CHIPS):
+        for chip in range(CHIPS):
+            for group in range(CHIPS * CORES):
+                first = group * owned + chip * part
+                rows = pl.ds(first, part)
+                filtered = (low_ref[dish, rows, :].astype(F32)
+                            + mid_ref[dish, rows, :].astype(F32)
+                            ) + high_ref[dish, rows, :].astype(F32)
+                weighted = (weight * (filtered - removed[first:first + part])).astype(BF16)
                 for block in range(per_dish):
-                    out_ref[chip * CHIPS * CORES + group, dish * per_dish + block] = weighted[
-                        chip * part:(chip + 1) * part, block * BLOCK:(block + 1) * BLOCK
+                    weighted_ref[dish, chip * CHIPS * CORES + group, block] = weighted[
+                        :, block * BLOCK:(block + 1) * BLOCK
                     ]
+        copy_of(dish).start()
         return carry
 
     lax.fori_loop(0, dishes, body, 0)
-
-
-def bin_kernel(pointing_ref, blocks_ref, sky_ref):
-    sky_ref[...] = jnp.zeros_like(sky_ref)
+    for dish in range(dishes):
+        copy_of(dish).wait()
+
+
+def bin_kernel(pointing_ref, blocks_ref, sky_ref, *others):
+    totals = (sky_ref,) + others
+    for ref in totals:
+        ref[...] = jnp.zeros_like(ref)
     sources, count, chans, width = blocks_ref.shape
     lane = lax.broadcasted_iota(jnp.int32, (chans, width), 1)
 
     def body(source, carry):
         for block in range(count):
+            ref = totals[block % len(totals)]
             where = source * 2 * count + block
             tile = pointing_ref[where]
             offset = pointing_ref[where + count]
-            half = offset // width
-            shift = offset - half * width
+            half = offset >> (width.bit_length() - 1)
+            shift = offset & (width - 1)
             moved = pltpu.roll(blocks_ref[source, block].astype(F32), shift, 1)
             first = jnp.where((lane >= shift) == (half == 0), moved, 0.0)
-            sky_ref[tile, :, 0:width] += first
-            sky_ref[tile, :, width:2 * width] += moved - first
+            ref[tile, :, 0:width] += first
+            ref[tile, :, width:2 * width] += moved - first
         return carry
 
     lax.fori_loop(0, sources, body, 0)
-
-
-def call(kernel, name, out_shape, in_specs, scratch=()):
+    sky_ref[...] = (totals[0][...] + totals[1][...]) + (totals[2][...] + totals[3][...])
+
+
+def call(kernel, name, out_shape, in_specs, scratch=(), out_specs=None):
     several = isinstance(out_shape, (list, tuple))
+    if out_specs is None:
+        out_specs = [VMEM] * len(out_shape) if several else VMEM
     return pl.pallas_call(
         kernel,
         out_shape=out_shape,
         in_specs=in_specs,
-        out_specs=[VMEM] * len(out_shape) if several else VMEM,
+        out_specs=out_specs,
         scratch_shapes=scratch,
         compiler_params=PARAMS,
         name=name,
@@ -305,7 +322,11 @@
     with jax.named_scope("cleaned"):
         blocks = call(
             clean_kernel, "clean",
-            jax.ShapeDtypeStruct((sharers, dishes * per_dish, part, BLOCK), BF16), [VMEM] * 5,
+            pltpu.HBM((sharers, dishes * per_dish, part, BLOCK), BF16), [VMEM] * 5,
+            [pltpu.VMEM((dishes, sharers, per_dish, part, BLOCK), BF16),
+             pltpu.SemaphoreType.DMA((dishes,)),
+             pltpu.VMEM((dishes, 6 * ROWS, tdev), BF16), pltpu.VMEM((chans, 6 * ROWS), BF16)],
+            pl.BlockSpec(memory_space=pl.ANY),
         )(sums, weights.reshape(dishes, 1, tdev), high, mid, low)
 
     with jax.named_scope("channels"):
@@ -313,7 +334,8 @@
 
     with jax.named_scope("binning"):
         sky = call(
-            bin_kernel, "bin", jax.ShapeDtypeStruct((times, part, PIX), F32), [SMEM, VMEM]
+            bin_kernel, "bin", jax.ShapeDtypeStruct((times, part, PIX), F32), [SMEM, VMEM],
+            [pltpu.VMEM((times, part, PIX), F32)] * 3,
         )(pointing, arrived)
 
     with jax.named_scope("tiles"):

time: 223 us -> 216 us (0.969)
  Pallas kernels: 43.1 us -> 38.9 us
    pallas_call x1, Pallas kernels: 7.8 us -> 5.44 us  [shards(): call(clean_kernel, 'clean', pltpu.HBM((sharers, dishes * per_dish, part,...]
    unnamed x18 -> x16, local copies, waits for them, and re-layouts: 8.97 us -> 6.94 us
  transfers between devices with their start and end apart: 33 -> 33, of which waited for: 30 -> 30; matrix products, arithmetic and copies ran while one was open for 0% -> 0% of each run, Pallas kernels for 3% -> 4%
where the time goes in v2:
time: 216 us
  waiting for transfers between devices  99.5 us (46%)
  starting transfers between devices  53.1 us (25%)
  Pallas kernels  38.9 us (18%)
  blocking collectives  15.7 us (7%)
  local copies, waits for them, and re-layouts  7.2 us (3%)
    all_to_all x1, waiting for transfers between devices, shards(): arrived = lax.all_to_all(blocks, ('x', 'y', 'c'), 0, 0, tiled=True)  52.8 us
    ppermute x30, starting transfers between devices, total_over(): lax.ppermute(value, axis, [(i, (i + s) % count) for i in range(count)])  43 us
    ppermute x30, waiting for transfers between devices, total_over(): lax.ppermute(value, axis, [(i, (i + s) % count) for i in range(count)])  33.3 us
    all_to_all x1, blocking collectives, shards(): parts = lax.all_to_all(sky, ('z', 'x'), 0, 0, tiled=True)  15.7 us
    ppermute x1, waiting for transfers between devices, shards(): lax.ppermute(tail, ('z', 'x'), [(i, i + 1) for i in range(ends)])  9.61 us
    pallas_call x1, Pallas kernels, shards(): call(edge_kernel, 'edge', [piece, piece, piece, rows_f32], [VMEM] * 6)  8.62 us
    pallas_call x2, Pallas kernels, shards(): sums = call(step_kernel, 'step', rows_f32, [VMEM] * 3)(sums, high, mid)  7.77 us
    pallas_call x1, Pallas kernels, shards(): call(lambda *refs: own_kernel(reach, *refs), 'own', [rows_f32, jax.ShapeD...  7.73 us
  transfers between devices with their start and end apart: 33, of which 30 were waited for; matrix products, arithmetic and copies ran while one was open for 0% of the time, Pallas kernels for 4%

profile of v2, /device:TPU:0, one launch (start us, length us, event | category | flops | bytes accessed | tf_op | source)
XLA Modules:
  0.0 215.6 jit_solution(607768185633605077)
XLA Ops:
  0.0 3.4 %copy-done = f32[8,1024,256]{2,1,0:T(8,128)S(1)} copy-done((f32[8,1024,256]{2,1,0:T(8,128)S(1)}, f32[8,1024,256]{2,1,0:T(8,128)}, u32[]{:S(2)}) %copy-start) | copy-done | bytes 8388632
  3.4 3.1 %pack.1 = (f32[8,256,128]{2,1,0:T(8,128)S(1)}, f32[8,256,128]{2,1,0:T(8,128)}) custom-call(f32[8,1024,256]{2,1,0:T(8,128)S(1)} %copy-done), custom_call_target="tpu_custom_call" | custom-call | tf_op jit(solution)/shard_map/edges/pack/pallas_call | solution.py:287
  6.5 3.5 %collective-permute-start = (f32[8,256,128]{2,1,0:T(8,128)}, f32[8,256,128]{2,1,0:T(8,128)S(1)}, u32[]{:S(2)}, u32[]{:S(2)}) collective-permute-start(f32[8,256,128]{2,1,0:T(8,128)} %get-tuple-element.17), channel_id=1, source_target_pairs={{0,8},{8,16},{16,24},{24,32},{32,40},{40,48},{48,56},{56,64},{64,7... | collective-permute-start | bytes 3145736 | tf_op jit(solution)/shard_map/edges/ppermute | solution.py:291
  10.1 1.3 collective-permute-start.1
  12.0 3.4 %copy-done.1 = f32[8,1024,256]{2,1,0:T(8,128)S(1)} copy-done((f32[8,1024,256]{2,1,0:T(8,128)S(1)}, f32[8,1024,256]{2,1,0:T(8,128)}, u32[]{:S(2)}) %copy-start.1) | copy-done | bytes 8388632
  15.4 7.7 %own.1 = (f32[8,1024]{1,0:T(8,128)S(1)}, bf16[2,4,256,256]{3,2,1,0:T(8,128)(2,1)S(1)}, f32[8,1024,256]{2,1,0:T(8,128)S(1)}) custom-call(f32[65]{0:T(128)S(1)} %copy-done.2, f32[8,1024]{1,0:T(8,128)S(1)} %pad.4.refs_1_, f32[8,1024,256]{2,1,0:T(8,128)S(1)} %copy-done.1), custom_call_target="tpu_custom_call" | custom-call | tf_op jit(solution)/shard_map/own/own/pallas_call | solution.py:296
  23.1 9.6 %collective-permute-done.left_ref = f32[8,256,128]{2,1,0:T(8,128)S(1)} collective-permute-done((f32[8,256,128]{2,1,0:T(8,128)}, f32[8,256,128]{2,1,0:T(8,128)S(1)}, u32[]{:S(2)}, u32[]{:S(2)}) %collective-permute-start) | collective-permute-done | bytes 1048608 | tf_op jit(solution)/shard_map/edges/ppermute | solution.py:291
  32.7 3.9 %collective-permute-done.1.right_ref = f32[8,256,128]{2,1,0:T(8,128)S(1)} collective-permute-done((f32[8,256,128]{2,1,0:T(8,128)S(1)}, f32[8,256,128]{2,1,0:T(8,128)S(1)}, u32[]{:S(2)}, u32[]{:S(2)}) %collective-permute-start.1) | collective-permute-done | bytes 1048608 | tf_op jit(solution)/shard_map/edges/ppermute | solution.py:292
  36.6 8.6 %edge.1 = (bf16[8,1024,256]{2,1,0:T(8,128)(2,1)S(1)}, bf16[8,1024,256]{2,1,0:T(8,128)(2,1)S(1)}, bf16[8,1024,256]{2,1,0:T(8,128)(2,1)S(1)}, f32[8,1024]{1,0:T(8,128)S(1)}) custom-call(f32[8,1024]{1,0:T(8,128)S(1)} %get-tuple-element.14.basis_ref, bf16[2,4,256,256]{3,2,1,0:T(8,128)(2,1)S(1)} %get-tuple-element.15.fix_ref, ...), custom_call_target="tpu_custom_call" | custom-call | tf_op jit(solution)/shard_map/filtered/edge/pallas_call | solution.py:310
  45.2 1.2 collective-permute-done.2
  46.4 1.6 collective-permute-start.3
  48.0 2.9 %collective-permute-start.4 = (f32[8,1024]{1,0:T(8,128)S(1)}, f32[8,1024]{1,0:T(8,128)S(1)}, u32[]{:S(2)}, u32[]{:S(2)}) collective-permute-start(f32[8,1024]{1,0:T(8,128)S(1)} %add.100), channel_id=1, source_target_pairs={{0,4},{2,6},{4,0},{6,2},{1,5},{3,7},{5,1},{7,3},{8,12},{10,14},{12... | collective-permute-start | bytes 98312 | tf_op jit(solution)/shard_map/iterations/ppermute | solution.py:264
  50.9 1.3 collective-permute-start.5
  52.3 1.2 collective-permute-done.4
  53.4 1.4 collective-permute-done.5
  54.8 1.5 collective-permute-start.6
  56.3 5.2 %collective-permute-start.7 = (f32[8,1024]{1,0:T(8,128)S(1)}, f32[8,1024]{1,0:T(8,128)S(1)}, u32[]{:S(2)}, u32[]{:S(2)}) collective-permute-start(f32[8,1024]{1,0:T(8,128)S(1)} %add_add_fusion.8), channel_id=1, source_target_pairs={{0,16},{8,24},{16,0},{24,8},{1,17},{9,25},{17,1},{25,9},{2,18},{10... | collective-permute-start | bytes 98312 | tf_op jit(solution)/shard_map/iterations/ppermute | solution.py:264
  61.5 0.4 collective-permute-done.6
  62.0 1.8 collective-permute-done.7
  63.8 1.7 collective-permute-done.8
  65.4 3.7 %collective-permute-start.10 = (f32[8,1024]{1,0:T(8,128)S(1)}, f32[8,1024]{1,0:T(8,128)S(1)}, u32[]{:S(2)}, u32[]{:S(2)}) collective-permute-start(f32[8,1024]{1,0:T(8,128)S(1)} %add_add_fusion.7), channel_id=1, source_target_pairs={{0,64},{32,96},{64,0},{96,32},{1,65},{33,97},{65,1},{97,33},{2,66}... | collective-permute-start | bytes 98312 | tf_op jit(solution)/shard_map/iterations/ppermute | solution.py:264
  69.1 1.0 collective-permute-start.11
  70.1 1.0 collective-permute-start.9
  71.1 1.9 collective-permute-done.11
  73.0 2.2 %collective-permute-done.9 = f32[8,1024]{1,0:T(8,128)S(1)} collective-permute-done((f32[8,1024]{1,0:T(8,128)S(1)}, f32[8,1024]{1,0:T(8,128)S(1)}, u32[]{:S(2)}, u32[]{:S(2)}) %collective-permute-start.9) | collective-permute-done | bytes 32800 | tf_op jit(solution)/shard_map/iterations/ppermute | solution.py:264
  75.3 3.9 %step.2 = f32[8,1024]{1,0:T(8,128)S(1)} custom-call(f32[8,1024]{1,0:T(8,128)S(1)} %add_add_fusion.6.sums_ref, bf16[8,1024,256]{2,1,0:T(8,128)(2,1)S(1)} %get-tuple-element.20.high_ref, bf16[8,1024,256]{2,1,0:T(8,128)(2,1)S(1)} %get-tuple-element.21.mid_ref), custom_call_target="tpu_custom_call" | custom-call | tf_op jit(solution)/shard_map/iterations/step/pallas_call | solution.py:319
  79.2 1.2 collective-permute-done.12
  80.6 3.8 %collective-permute-start.14 = (f32[8,1024]{1,0:T(8,128)S(1)}, f32[8,1024]{1,0:T(8,128)S(1)}, u32[]{:S(2)}, u32[]{:S(2)}) collective-permute-start(f32[8,1024]{1,0:T(8,128)S(1)} %add.110), channel_id=1, source_target_pairs={{0,4},{2,6},{4,0},{6,2},{1,5},{3,7},{5,1},{7,3},{8,12},{10,14},{12... | collective-permute-start | bytes 98312 | tf_op jit(solution)/shard_map/iterations/ppermute | solution.py:264
  84.5 1.0 collective-permute-done.13
  85.5 1.1 collective-permute-done.14
  86.6 1.7 collective-permute-done.15
  88.4 2.7 %collective-permute-start.17 = (f32[8,1024]{1,0:T(8,128)S(1)}, f32[8,1024]{1,0:T(8,128)S(1)}, u32[]{:S(2)}, u32[]{:S(2)}) collective-permute-start(f32[8,1024]{1,0:T(8,128)S(1)} %add_add_fusion.5), channel_id=1, source_target_pairs={{0,16},{8,24},{16,0},{24,8},{1,17},{9,25},{17,1},{25,9},{2,18},{10... | collective-permute-start | bytes 98312 | tf_op jit(solution)/shard_map/iterations/ppermute | solution.py:264
  91.1 1.5 collective-permute-start.18
  92.5 1.0 collective-permute-done.16
  93.5 0.4 collective-permute-done.17
  93.9 1.1 collective-permute-done.18
  95.3 1.5 collective-permute-start.20
  96.7 1.8 collective-permute-start.21
  98.5 1.9 collective-permute-done.19
  100.4 0.4 collective-permute-done.20
  100.8 0.8 collective-permute-done.21
  101.6 3.9 %step.3 = f32[8,1024]{1,0:T(8,128)S(1)} custom-call(f32[8,1024]{1,0:T(8,128)S(1)} %add_add_fusion.3.sums_ref, bf16[8,1024,256]{2,1,0:T(8,128)(2,1)S(1)} %get-tuple-element.20.high_ref, bf16[8,1024,256]{2,1,0:T(8,128)(2,1)S(1)} %get-tuple-element.21.mid_ref), custom_call_target="tpu_custom_call" | custom-call | tf_op jit(solution)/shard_map/iterations/step/pallas_call | solution.py:319
  105.5 1.2 collective-permute-done.22
  106.8 2.7 %collective-permute-start.24 = (f32[8,1024]{1,0:T(8,128)S(1)}, f32[8,1024]{1,0:T(8,128)S(1)}, u32[]{:S(2)}, u32[]{:S(2)}) collective-permute-start(f32[8,1024]{1,0:T(8,128)S(1)} %add.120), channel_id=1, source_target_pairs={{0,4},{2,6},{4,0},{6,2},{1,5},{3,7},{5,1},{7,3},{8,12},{10,14},{12... | collective-permute-start | bytes 98312 | tf_op jit(solution)/shard_map/iterations/ppermute | solution.py:264
  109.5 1.3 collective-permute-start.25
  110.9 1.5 collective-permute-done.23
  112.4 1.1 collective-permute-done.25
  113.5 1.5 collective-permute-start.26
  114.9 2.7 %collective-permute-start.27 = (f32[8,1024]{1,0:T(8,128)S(1)}, f32[8,1024]{1,0:T(8,128)S(1)}, u32[]{:S(2)}, u32[]{:S(2)}) collective-permute-start(f32[8,1024]{1,0:T(8,128)S(1)} %add_add_fusion.2), channel_id=1, source_target_pairs={{0,16},{8,24},{16,0},{24,8},{1,17},{9,25},{17,1},{25,9},{2,18},{10... | collective-permute-start | bytes 98312 | tf_op jit(solution)/shard_map/iterations/ppermute | solution.py:264
  117.7 0.9 collective-permute-done.26
  118.7 1.7 collective-permute-done.27
  120.4 1.2 collective-permute-done.28
  121.6 1.7 collective-permute-start.29
  123.3 2.2 %collective-permute-start.30 = (f32[8,1024]{1,0:T(8,128)S(1)}, f32[8,1024]{1,0:T(8,128)S(1)}, u32[]{:S(2)}, u32[]{:S(2)}) collective-permute-start(f32[8,1024]{1,0:T(8,128)S(1)} %add_add_fusion.1), channel_id=1, source_target_pairs={{0,64},{32,96},{64,0},{96,32},{1,65},{33,97},{65,1},{97,33},{2,66}... | collective-permute-start | bytes 98312 | tf_op jit(solution)/shard_map/iterations/ppermute | solution.py:264
  125.5 0.6 collective-permute-start.31
  126.1 0.7 collective-permute-done.29
  126.8 2.0 collective-permute-done.30
  128.8 0.7 collective-permute-done.31
  129.4 5.4 %clean.1 = bf16[32,16,32,128]{3,2,1,0:T(8,128)(2,1)} custom-call(f32[8,1024]{1,0:T(8,128)S(1)} %add_add_fusion.sums_ref, f32[8,1,256]{2,1,0:T(1,128)S(1)} %reshape.55.weight_ref, bf16[8,1024,256]{2,1,0:T(8,128)(2,1)S(1)} %get-tuple-element.20.high_ref, bf16[8,1024,256]{2,1,0:T(8,128)(2,1)S(1)} %get-tuple-element.21.mid_ref, ...), custom_call_target="tpu_custom_call" | custom-call | tf_op jit(solution)/shard_map/cleaned/clean/pallas_call | solution.py:323
  134.9 5.3 %all-to-all-start = ((bf16[32,16,32,128]{3,2,1,0:T(8,128)(2,1)}), bf16[32,16,32,128]{3,2,1,0:T(8,128)(2,1)}, u32[]{:S(2)}, u32[]{:S(2)}) async-start(bf16[32,16,32,128]{3,2,1,0:T(8,128)(2,1)} %clean.1), calls=%async_computation | async-start | bytes 8388608 | tf_op jit(solution)/shard_map/channels/all_to_all | solution.py:333
  140.2 52.8 %all-to-all-done.blocks_ref = bf16[32,16,32,128]{3,2,1,0:T(8,128)(2,1)} async-done(((bf16[32,16,32,128]{3,2,1,0:T(8,128)(2,1)}), bf16[32,16,32,128]{3,2,1,0:T(8,128)(2,1)}, u32[]{:S(2)}, u32[]{:S(2)}) %all-to-all-start) | async-done | bytes 4194336 | tf_op jit(solution)/shard_map/channels/all_to_all | solution.py:333
  193.0 6.2 %bin.1 = f32[16,32,256]{2,1,0:T(8,128)S(1)} custom-call(s32[1024]{0:T(1024)S(1)} %bitcast.5, bf16[32,16,32,128]{3,2,1,0:T(8,128)(2,1)} %all-to-all-done.blocks_ref), custom_call_target="tpu_custom_call" | custom-call | tf_op jit(solution)/shard_map/binning/bin/pallas_call | solution.py:336
  199.2 15.7 %all_to_all.10 = f32[16,32,256]{2,1,0:T(8,128)S(1)} all-to-all(f32[16,32,256]{2,1,0:T(8,128)S(1)} %bin.1), channel_id=1, replica_groups=mesh['z'=4,'x'=4,'y'=4,'c'=2] {'z','x'}, dimensions={0} | all-to-all | bytes 1048576 | tf_op jit(solution)/shard_map/tiles/all_to_all | solution.py:342
  214.9 0.7 bitcast_reduce_fusion
  (48 shorter events, 1.6 us)
Async XLA Ops:
  0.0 3.4 %copy-start = (f32[8,1024,256]{2,1,0:T(8,128)S(1)}, f32[8,1024,256]{2,1,0:T(8,128)}, u32[]{:S(2)}) copy-start(f32[8,1024,256]{2,1,0:T(8,128)} %refs_0_.3) | copy-start | bytes 25165828
  3.4 8.0 %copy-start.5 = (s32[8,2]{0,1:T(2,128)S(1)}, s32[8,2]{0,1:T(2,128)}, u32[]{:S(2)}) copy-start(s32[8,2]{0,1:T(2,128)} %param.10) | copy-start | bytes 196
  3.4 8.2 %copy-start.6 = (s32[8,2]{0,1:T(2,128)S(1)}, s32[8,2]{0,1:T(2,128)}, u32[]{:S(2)}) copy-start(s32[8,2]{0,1:T(2,128)} %param.11) | copy-start | bytes 196
  3.4 8.6 %copy-start.3 = (f32[6,1024]{1,0:T(8,128)S(1)}, f32[6,1024]{1,0:T(8,128)}, u32[]{:S(2)}) copy-start(f32[6,1024]{1,0:T(8,128)} %param.8) | copy-start | bytes 73732
  3.4 8.6 %copy-start.2 = (f32[65]{0:T(128)S(1)}, f32[65]{0:T(128)}, u32[]{:S(2)}) copy-start(f32[65]{0:T(128)} %refs_0_.2) | copy-start | bytes 784
  6.5 26.2 %collective-permute-start = (f32[8,256,128]{2,1,0:T(8,128)}, f32[8,256,128]{2,1,0:T(8,128)S(1)}, u32[]{:S(2)}, u32[]{:S(2)}) collective-permute-start(f32[8,256,128]{2,1,0:T(8,128)} %get-tuple-element.17), channel_id=1, source_target_pairs={{0,8},{8,16},{16,24},{24,32},{32,40},{40,48},{48,56},{56,64},{64,7... | collective-permute-start | bytes 3145736 | tf_op jit(solution)/shard_map/edges/ppermute | solution.py:291
  10.1 26.5 %collective-permute-start.1 = (f32[8,256,128]{2,1,0:T(8,128)S(1)}, f32[8,256,128]{2,1,0:T(8,128)S(1)}, u32[]{:S(2)}, u32[]{:S(2)}) collective-permute-start(f32[8,256,128]{2,1,0:T(8,128)S(1)} %get-tuple-element.18), channel_id=1, source_target_pairs={{8,0},{16,8},{24,16},{32,24},{40,32},{48,40},{56,48},{64,56},{72,6... | collective-permute-start | bytes 3145736 | tf_op jit(solution)/shard_map/edges/ppermute | solution.py:292
  12.0 3.4 %copy-start.1 = (f32[8,1024,256]{2,1,0:T(8,128)S(1)}, f32[8,1024,256]{2,1,0:T(8,128)}, u32[]{:S(2)}) copy-start(f32[8,1024,256]{2,1,0:T(8,128)} %refs_0_.3) | copy-start | bytes 25165828
  45.2 1.2 collective-permute-start.2
  46.4 5.8 %collective-permute-start.3 = (f32[8,1024]{1,0:T(8,128)S(1)}, f32[8,1024]{1,0:T(8,128)S(1)}, u32[]{:S(2)}, u32[]{:S(2)}) collective-permute-start(f32[8,1024]{1,0:T(8,128)S(1)} %add.100), channel_id=1, source_target_pairs={{0,2},{2,4},{4,6},{6,0},{1,3},{3,5},{5,7},{7,1},{8,10},{10,12},{12... | collective-permute-start | bytes 98312 | tf_op jit(solution)/shard_map/iterations/ppermute | solution.py:264
  48.0 5.4 %collective-permute-start.4 = (f32[8,1024]{1,0:T(8,128)S(1)}, f32[8,1024]{1,0:T(8,128)S(1)}, u32[]{:S(2)}, u32[]{:S(2)}) collective-permute-start(f32[8,1024]{1,0:T(8,128)S(1)} %add.100), channel_id=1, source_target_pairs={{0,4},{2,6},{4,0},{6,2},{1,5},{3,7},{5,1},{7,3},{8,12},{10,14},{12... | collective-permute-start | bytes 98312 | tf_op jit(solution)/shard_map/iterations/ppermute | solution.py:264
  50.9 3.9 %collective-permute-start.5 = (f32[8,1024]{1,0:T(8,128)S(1)}, f32[8,1024]{1,0:T(8,128)S(1)}, u32[]{:S(2)}, u32[]{:S(2)}) collective-permute-start(f32[8,1024]{1,0:T(8,128)S(1)} %add.100), channel_id=1, source_target_pairs={{0,6},{2,0},{4,2},{6,4},{1,7},{3,1},{5,3},{7,5},{8,14},{10,8},{12,... | collective-permute-start | bytes 98312 | tf_op jit(solution)/shard_map/iterations/ppermute | solution.py:264
  54.8 7.1 %collective-permute-start.6 = (f32[8,1024]{1,0:T(8,128)S(1)}, f32[8,1024]{1,0:T(8,128)S(1)}, u32[]{:S(2)}, u32[]{:S(2)}) collective-permute-start(f32[8,1024]{1,0:T(8,128)S(1)} %add_add_fusion.8), channel_id=1, source_target_pairs={{0,8},{8,16},{16,24},{24,0},{1,9},{9,17},{17,25},{25,1},{2,10},{10... | collective-permute-start | bytes 98312 | tf_op jit(solution)/shard_map/iterations/ppermute | solution.py:264
  56.3 7.4 %collective-permute-start.7 = (f32[8,1024]{1,0:T(8,128)S(1)}, f32[8,1024]{1,0:T(8,128)S(1)}, u32[]{:S(2)}, u32[]{:S(2)}) collective-permute-start(f32[8,1024]{1,0:T(8,128)S(1)} %add_add_fusion.8), channel_id=1, source_target_pairs={{0,16},{8,24},{16,0},{24,8},{1,17},{9,25},{17,1},{25,9},{2,18},{10... | collective-permute-start | bytes 98312 | tf_op jit(solution)/shard_map/iterations/ppermute | solution.py:264
  61.5 3.9 %collective-permute-start.8 = (f32[8,1024]{1,0:T(8,128)S(1)}, f32[8,1024]{1,0:T(8,128)S(1)}, u32[]{:S(2)}, u32[]{:S(2)}) collective-permute-start(f32[8,1024]{1,0:T(8,128)S(1)} %add_add_fusion.8), channel_id=1, source_target_pairs={{0,24},{8,0},{16,8},{24,16},{1,25},{9,1},{17,9},{25,17},{2,26},{10... | collective-permute-start | bytes 98312 | tf_op jit(solution)/shard_map/iterations/ppermute | solution.py:264
  65.4 5.7 %collective-permute-start.10 = (f32[8,1024]{1,0:T(8,128)S(1)}, f32[8,1024]{1,0:T(8,128)S(1)}, u32[]{:S(2)}, u32[]{:S(2)}) collective-permute-start(f32[8,1024]{1,0:T(8,128)S(1)} %add_add_fusion.7), channel_id=1, source_target_pairs={{0,64},{32,96},{64,0},{96,32},{1,65},{33,97},{65,1},{97,33},{2,66}... | collective-permute-start | bytes 98312 | tf_op jit(solution)/shard_map/iterations/ppermute | solution.py:264
  69.1 3.9 %collective-permute-start.11 = (f32[8,1024]{1,0:T(8,128)S(1)}, f32[8,1024]{1,0:T(8,128)S(1)}, u32[]{:S(2)}, u32[]{:S(2)}) collective-permute-start(f32[8,1024]{1,0:T(8,128)S(1)} %add_add_fusion.7), channel_id=1, source_target_pairs={{0,96},{32,0},{64,32},{96,64},{1,97},{33,1},{65,33},{97,65},{2,98}... | collective-permute-start | bytes 98312 | tf_op jit(solution)/shard_map/iterations/ppermute | solution.py:264
  70.1 5.1 %collective-permute-start.9 = (f32[8,1024]{1,0:T(8,128)S(1)}, f32[8,1024]{1,0:T(8,128)S(1)}, u32[]{:S(2)}, u32[]{:S(2)}) collective-permute-start(f32[8,1024]{1,0:T(8,128)S(1)} %add_add_fusion.7), channel_id=1, source_target_pairs={{0,32},{32,64},{64,96},{96,0},{1,33},{33,65},{65,97},{97,1},{2,34}... | collective-permute-start | bytes 98312 | tf_op jit(solution)/shard_map/iterations/ppermute | solution.py:264
  79.1 1.2 collective-permute-start.12
  80.4 5.1 %collective-permute-start.13 = (f32[8,1024]{1,0:T(8,128)S(1)}, f32[8,1024]{1,0:T(8,128)S(1)}, u32[]{:S(2)}, u32[]{:S(2)}) collective-permute-start(f32[8,1024]{1,0:T(8,128)S(1)} %add.110), channel_id=1, source_target_pairs={{0,2},{2,4},{4,6},{6,0},{1,3},{3,5},{5,7},{7,1},{8,10},{10,12},{12... | collective-permute-start | bytes 98312 | tf_op jit(solution)/shard_map/iterations/ppermute | solution.py:264
  80.6 6.1 %collective-permute-start.14 = (f32[8,1024]{1,0:T(8,128)S(1)}, f32[8,1024]{1,0:T(8,128)S(1)}, u32[]{:S(2)}, u32[]{:S(2)}) collective-permute-start(f32[8,1024]{1,0:T(8,128)S(1)} %add.110), channel_id=1, source_target_pairs={{0,4},{2,6},{4,0},{6,2},{1,5},{3,7},{5,1},{7,3},{8,12},{10,14},{12... | collective-permute-start | bytes 98312 | tf_op jit(solution)/shard_map/iterations/ppermute | solution.py:264
  84.4 3.9 %collective-permute-start.15 = (f32[8,1024]{1,0:T(8,128)S(1)}, f32[8,1024]{1,0:T(8,128)S(1)}, u32[]{:S(2)}, u32[]{:S(2)}) collective-permute-start(f32[8,1024]{1,0:T(8,128)S(1)} %add.110), channel_id=1, source_target_pairs={{0,6},{2,0},{4,2},{6,4},{1,7},{3,1},{5,3},{7,5},{8,14},{10,8},{12,... | collective-permute-start | bytes 98312 | tf_op jit(solution)/shard_map/iterations/ppermute | solution.py:264
  88.3 5.2 %collective-permute-start.16 = (f32[8,1024]{1,0:T(8,128)S(1)}, f32[8,1024]{1,0:T(8,128)S(1)}, u32[]{:S(2)}, u32[]{:S(2)}) collective-permute-start(f32[8,1024]{1,0:T(8,128)S(1)} %add_add_fusion.5), channel_id=1, source_target_pairs={{0,8},{8,16},{16,24},{24,0},{1,9},{9,17},{17,25},{25,1},{2,10},{10... | collective-permute-start | bytes 98312 | tf_op jit(solution)/shard_map/iterations/ppermute | solution.py:264
  88.4 5.5 %collective-permute-start.17 = (f32[8,1024]{1,0:T(8,128)S(1)}, f32[8,1024]{1,0:T(8,128)S(1)}, u32[]{:S(2)}, u32[]{:S(2)}) collective-permute-start(f32[8,1024]{1,0:T(8,128)S(1)} %add_add_fusion.5), channel_id=1, source_target_pairs={{0,16},{8,24},{16,0},{24,8},{1,17},{9,25},{17,1},{25,9},{2,18},{10... | collective-permute-start | bytes 98312 | tf_op jit(solution)/shard_map/iterations/ppermute | solution.py:264
  91.1 3.9 %collective-permute-start.18 = (f32[8,1024]{1,0:T(8,128)S(1)}, f32[8,1024]{1,0:T(8,128)S(1)}, u32[]{:S(2)}, u32[]{:S(2)}) collective-permute-start(f32[8,1024]{1,0:T(8,128)S(1)} %add_add_fusion.5), channel_id=1, source_target_pairs={{0,24},{8,0},{16,8},{24,16},{1,25},{9,1},{17,9},{25,17},{2,26},{10... | collective-permute-start | bytes 98312 | tf_op jit(solution)/shard_map/iterations/ppermute | solution.py:264
  95.0 5.4 %collective-permute-start.19 = (f32[8,1024]{1,0:T(8,128)S(1)}, f32[8,1024]{1,0:T(8,128)S(1)}, u32[]{:S(2)}, u32[]{:S(2)}) collective-permute-start(f32[8,1024]{1,0:T(8,128)S(1)} %add_add_fusion.4), channel_id=1, source_target_pairs={{0,32},{32,64},{64,96},{96,0},{1,33},{33,65},{65,97},{97,1},{2,34}... | collective-permute-start | bytes 98312 | tf_op jit(solution)/shard_map/iterations/ppermute | solution.py:264
  95.3 5.5 %collective-permute-start.20 = (f32[8,1024]{1,0:T(8,128)S(1)}, f32[8,1024]{1,0:T(8,128)S(1)}, u32[]{:S(2)}, u32[]{:S(2)}) collective-permute-start(f32[8,1024]{1,0:T(8,128)S(1)} %add_add_fusion.4), channel_id=1, source_target_pairs={{0,64},{32,96},{64,0},{96,32},{1,65},{33,97},{65,1},{97,33},{2,66}... | collective-permute-start | bytes 98312 | tf_op jit(solution)/shard_map/iterations/ppermute | solution.py:264
  96.7 4.9 %collective-permute-start.21 = (f32[8,1024]{1,0:T(8,128)S(1)}, f32[8,1024]{1,0:T(8,128)S(1)}, u32[]{:S(2)}, u32[]{:S(2)}) collective-permute-start(f32[8,1024]{1,0:T(8,128)S(1)} %add_add_fusion.4), channel_id=1, source_target_pairs={{0,96},{32,0},{64,32},{96,64},{1,97},{33,1},{65,33},{97,65},{2,98}... | collective-permute-start | bytes 98312 | tf_op jit(solution)/shard_map/iterations/ppermute | solution.py:264
  101.6 24.5 %copy-start.4 = (f32[8,256]{1,0:T(8,128)S(1)}, f32[8,256]{1,0:T(8,128)}, u32[]{:S(2)}) copy-start(f32[8,256]{1,0:T(8,128)} %param.9) | copy-start | bytes 24580
  105.5 1.2 collective-permute-start.22
  106.7 5.6 %collective-permute-start.23 = (f32[8,1024]{1,0:T(8,128)S(1)}, f32[8,1024]{1,0:T(8,128)S(1)}, u32[]{:S(2)}, u32[]{:S(2)}) collective-permute-start(f32[8,1024]{1,0:T(8,128)S(1)} %add.120), channel_id=1, source_target_pairs={{0,2},{2,4},{4,6},{6,0},{1,3},{3,5},{5,7},{7,1},{8,10},{10,12},{12... | collective-permute-start | bytes 98312 | tf_op jit(solution)/shard_map/iterations/ppermute | solution.py:264
  106.8 5.5 %collective-permute-start.24 = (f32[8,1024]{1,0:T(8,128)S(1)}, f32[8,1024]{1,0:T(8,128)S(1)}, u32[]{:S(2)}, u32[]{:S(2)}) collective-permute-start(f32[8,1024]{1,0:T(8,128)S(1)} %add.120), channel_id=1, source_target_pairs={{0,4},{2,6},{4,0},{6,2},{1,5},{3,7},{5,1},{7,3},{8,12},{10,14},{12... | collective-permute-start | bytes 98312 | tf_op jit(solution)/shard_map/iterations/ppermute | solution.py:264
  109.5 3.9 %collective-permute-start.25 = (f32[8,1024]{1,0:T(8,128)S(1)}, f32[8,1024]{1,0:T(8,128)S(1)}, u32[]{:S(2)}, u32[]{:S(2)}) collective-permute-start(f32[8,1024]{1,0:T(8,128)S(1)} %add.120), channel_id=1, source_target_pairs={{0,6},{2,0},{4,2},{6,4},{1,7},{3,1},{5,3},{7,5},{8,14},{10,8},{12,... | collective-permute-start | bytes 98312 | tf_op jit(solution)/shard_map/iterations/ppermute | solution.py:264
  113.5 5.2 %collective-permute-start.26 = (f32[8,1024]{1,0:T(8,128)S(1)}, f32[8,1024]{1,0:T(8,128)S(1)}, u32[]{:S(2)}, u32[]{:S(2)}) collective-permute-start(f32[8,1024]{1,0:T(8,128)S(1)} %add_add_fusion.2), channel_id=1, source_target_pairs={{0,8},{8,16},{16,24},{24,0},{1,9},{9,17},{17,25},{25,1},{2,10},{10... | collective-permute-start | bytes 98312 | tf_op jit(solution)/shard_map/iterations/ppermute | solution.py:264
  114.9 5.4 %collective-permute-start.27 = (f32[8,1024]{1,0:T(8,128)S(1)}, f32[8,1024]{1,0:T(8,128)S(1)}, u32[]{:S(2)}, u32[]{:S(2)}) collective-permute-start(f32[8,1024]{1,0:T(8,128)S(1)} %add_add_fusion.2), channel_id=1, source_target_pairs={{0,16},{8,24},{16,0},{24,8},{1,17},{9,25},{17,1},{25,9},{2,18},{10... | collective-permute-start | bytes 98312 | tf_op jit(solution)/shard_map/iterations/ppermute | solution.py:264
  117.7 3.9 %collective-permute-start.28 = (f32[8,1024]{1,0:T(8,128)S(1)}, f32[8,1024]{1,0:T(8,128)S(1)}, u32[]{:S(2)}, u32[]{:S(2)}) collective-permute-start(f32[8,1024]{1,0:T(8,128)S(1)} %add_add_fusion.2), channel_id=1, source_target_pairs={{0,24},{8,0},{16,8},{24,16},{1,25},{9,1},{17,9},{25,17},{2,26},{10... | collective-permute-start | bytes 98312 | tf_op jit(solution)/shard_map/iterations/ppermute | solution.py:264
  121.6 5.2 %collective-permute-start.29 = (f32[8,1024]{1,0:T(8,128)S(1)}, f32[8,1024]{1,0:T(8,128)S(1)}, u32[]{:S(2)}, u32[]{:S(2)}) collective-permute-start(f32[8,1024]{1,0:T(8,128)S(1)} %add_add_fusion.1), channel_id=1, source_target_pairs={{0,32},{32,64},{64,96},{96,0},{1,33},{33,65},{65,97},{97,1},{2,34}... | collective-permute-start | bytes 98312 | tf_op jit(solution)/shard_map/iterations/ppermute | solution.py:264
  123.3 5.4 %collective-permute-start.30 = (f32[8,1024]{1,0:T(8,128)S(1)}, f32[8,1024]{1,0:T(8,128)S(1)}, u32[]{:S(2)}, u32[]{:S(2)}) collective-permute-start(f32[8,1024]{1,0:T(8,128)S(1)} %add_add_fusion.1), channel_id=1, source_target_pairs={{0,64},{32,96},{64,0},{96,32},{1,65},{33,97},{65,1},{97,33},{2,66}... | collective-permute-start | bytes 98312 | tf_op jit(solution)/shard_map/iterations/ppermute | solution.py:264
  125.5 3.9 %collective-permute-start.31 = (f32[8,1024]{1,0:T(8,128)S(1)}, f32[8,1024]{1,0:T(8,128)S(1)}, u32[]{:S(2)}, u32[]{:S(2)}) collective-permute-start(f32[8,1024]{1,0:T(8,128)S(1)} %add_add_fusion.1), channel_id=1, source_target_pairs={{0,96},{32,0},{64,32},{96,64},{1,97},{33,1},{65,33},{97,65},{2,98}... | collective-permute-start | bytes 98312 | tf_op jit(solution)/shard_map/iterations/ppermute | solution.py:264
  134.9 58.1 %all-to-all-start = ((bf16[32,16,32,128]{3,2,1,0:T(8,128)(2,1)}), bf16[32,16,32,128]{3,2,1,0:T(8,128)(2,1)}, u32[]{:S(2)}, u32[]{:S(2)}) async-start(bf16[32,16,32,128]{3,2,1,0:T(8,128)(2,1)} %clean.1), calls=%async_computation | async-start | bytes 8388608 | tf_op jit(solution)/shard_map/channels/all_to_all | solution.py:333

commit v3 on v2

--- a/solution.py
+++ b/solution.py
@@ -18,6 +18,7 @@
 PARAMS = pltpu.CompilerParams(vmem_limit_bytes=16 * 1024 * 1024)
 VMEM = pl.BlockSpec(memory_space=pltpu.VMEM)
 SMEM = pl.BlockSpec(memory_space=pltpu.SMEM)
+HBM = pl.BlockSpec(memory_space=pltpu.HBM)
 LAST = (((1,), (1,)), ((), ()))
 
 
@@ -61,19 +62,26 @@
     return jnp.where(row < MODES, rows / jnp.sqrt(squares), 0.0)
 
 
-def pack_kernel(reach, tod_ref, head_ref, tail_ref):
+def pack_kernel(reach, tod_ref, head_ref, tail_ref, series_ref, sems):
     groups = BLOCK // reach
     dishes, chans, tdev = tod_ref.shape
     size = chans // groups
     lane = lax.broadcasted_iota(jnp.int32, (size, BLOCK), 1) // reach
 
+    def copy_of(dish):
+        return pltpu.make_async_copy(tod_ref.at[dish], series_ref.at[dish], sems.at[dish])
+
+    for dish in range(dishes):
+        copy_of(dish).start()
+
     def body(dish, carry):
+        copy_of(dish).wait()
         head = jnp.zeros((size, BLOCK), F32)
         tail = jnp.zeros((size, BLOCK), F32)
         for group in range(groups):
             rows = pl.ds(group * size, size)
-            first = tod_ref[dish, rows, 0:BLOCK]
-            last = tod_ref[dish, rows, tdev - BLOCK:tdev]
+            first = series_ref[dish, rows, 0:BLOCK]
+            last = series_ref[dish, rows, tdev - BLOCK:tdev]
             if group:
                 first = pltpu.roll(first, group * reach, 1)
             move = (group * reach + reach) % BLOCK
@@ -146,25 +154,27 @@
 
 def edge_kernel(basis_ref, fix_ref, own_ref, left_ref, right_ref, pointing_ref,
                 high_ref, mid_ref, low_ref, total_ref):
-    dishes, chans = own_ref.shape[0], own_ref.shape[1]
+    dishes, chans, tdev = own_ref.shape
     groups = fix_ref.shape[1]
     size = chans // groups
-
-    def body(dish, carry):
-        edges = jnp.concatenate([left_ref[dish], right_ref[dish]], axis=1)
-        high, low = split(edges, 2)
+    several = 4
+
+    def body(index, carry):
+        some = pl.ds(index * several, several)
+        edges = jnp.concatenate([left_ref[some], right_ref[some]], axis=2)
+        high, low = split(edges.reshape(several * size, tdev), 2)
         for group in range(groups):
             rows = pl.ds(group * size, size)
             lowpass = mxu(high, fix_ref[0, group]) + (
                 mxu(high, fix_ref[1, group]) + mxu(low, fix_ref[0, group])
             )
-            pieces = split(own_ref[dish, rows, :] - lowpass, 3)
-            high_ref[dish, rows, :] = pieces[0]
-            mid_ref[dish, rows, :] = pieces[1]
-            low_ref[dish, rows, :] = pieces[2]
-        return carry
-
-    lax.fori_loop(0, dishes, body, 0)
+            pieces = split(own_ref[some, rows, :] - lowpass.reshape(several, size, tdev), 3)
+            high_ref[some, rows, :] = pieces[0]
+            mid_ref[some, rows, :] = pieces[1]
+            low_ref[some, rows, :] = pieces[2]
+        return carry
+
+    lax.fori_loop(0, dishes // several, body, 0)
     total_ref[...] = step(basis_ref[...], high_ref, mid_ref)
     total_ref[MODES:MODES + 1] = pointing_ref[...]
 
@@ -217,14 +227,23 @@
         copy_of(dish).wait()
 
 
-def bin_kernel(pointing_ref, blocks_ref, sky_ref, *others):
+def bin_kernel(pointing_ref, arrived_ref, sky_ref, blocks_ref, sems, *others):
+    sources, count, chans, width = arrived_ref.shape
+    pieces = sems.shape[0]
+    several = sources // pieces
+
+    def copy_of(piece):
+        some = pl.ds(piece * several, several)
+        return pltpu.make_async_copy(arrived_ref.at[some], blocks_ref.at[some], sems.at[piece])
+
+    for piece in range(pieces):
+        copy_of(piece).start()
     totals = (sky_ref,) + others
     for ref in totals:
         ref[...] = jnp.zeros_like(ref)
-    sources, count, chans, width = blocks_ref.shape
     lane = lax.broadcasted_iota(jnp.int32, (chans, width), 1)
 
-    def body(source, carry):
+    def one(source, carry):
         for block in range(count):
             ref = totals[block % len(totals)]
             where = source * 2 * count + block
@@ -238,7 +257,11 @@
             ref[tile, :, width:2 * width] += moved - first
         return carry
 
-    lax.fori_loop(0, sources, body, 0)
+    def body(piece, carry):
+        copy_of(piece).wait()
+        return lax.fori_loop(piece * several, (piece + 1) * several, one, carry)
+
+    lax.fori_loop(0, pieces, body, 0)
     sky_ref[...] = (totals[0][...] + totals[1][...]) + (totals[2][...] + totals[3][...])
 
 
@@ -285,8 +308,9 @@
 
     with jax.named_scope("edges"):
         head, tail = call(
-            lambda *refs: pack_kernel(reach, *refs), "pack", [edge_f32] * 2, [VMEM]
-        )(tod)
+            lambda *refs: pack_kernel(reach, *refs), "pack", [edge_f32] * 2, [HBM],
+            [pltpu.VMEM((dishes, chans, tdev), F32), pltpu.SemaphoreType.DMA((dishes,))],
+        )(pltpu.with_memory_space_constraint(tod, pltpu.HBM))
         ends = times - 1
         from_left = lax.ppermute(tail, ("z", "x"), [(i, i + 1) for i in range(ends)])
         from_right = lax.ppermute(head, ("z", "x"), [(i + 1, i) for i in range(ends)])
@@ -326,7 +350,7 @@
             [pltpu.VMEM((dishes, sharers, per_dish, part, BLOCK), BF16),
              pltpu.SemaphoreType.DMA((dishes,)),
              pltpu.VMEM((dishes, 6 * ROWS, tdev), BF16), pltpu.VMEM((chans, 6 * ROWS), BF16)],
-            pl.BlockSpec(memory_space=pl.ANY),
+            HBM,
         )(sums, weights.reshape(dishes, 1, tdev), high, mid, low)
 
     with jax.named_scope("channels"):
@@ -334,8 +358,9 @@
 
     with jax.named_scope("binning"):
         sky = call(
-            bin_kernel, "bin", jax.ShapeDtypeStruct((times, part, PIX), F32), [SMEM, VMEM],
-            [pltpu.VMEM((times, part, PIX), F32)] * 3,
+            bin_kernel, "bin", jax.ShapeDtypeStruct((times, part, PIX), F32), [SMEM, HBM],
+            [pltpu.VMEM(blocks.shape, BF16), pltpu.SemaphoreType.DMA((8,))]
+            + [pltpu.VMEM((times, part, PIX), F32)] * 3,
         )(pointing, arrived)
 
     with jax.named_scope("tiles"):

time: 216 us -> 213 us (0.986)
  local copies, waits for them, and re-layouts: 7.2 us -> 3.82 us
    unnamed x16 -> x14, local copies, waits for them, and re-layouts: 6.94 us -> 3.56 us
where the time goes in v3:
time: 213 us; the launch traced here: 212 us
  waiting for transfers between devices  99.5 us (47%)
  starting transfers between devices  53.2 us (25%)
  Pallas kernels  39.1 us (18%)
  blocking collectives  15.6 us (7%)
  local copies, waits for them, and re-layouts  3.82 us (2%)
    all_to_all x1, waiting for transfers between devices, shards(): arrived = lax.all_to_all(blocks, ('x', 'y', 'c'), 0, 0, tiled=True)  52.8 us
    ppermute x30, starting transfers between devices, total_over(): lax.ppermute(value, axis, [(i, (i + s) % count) for i in range(count)])  43 us
    ppermute x30, waiting for transfers between devices, total_over(): lax.ppermute(value, axis, [(i, (i + s) % count) for i in range(count)])  33.3 us
    all_to_all x1, blocking collectives, shards(): parts = lax.all_to_all(sky, ('z', 'x'), 0, 0, tiled=True)  15.6 us
    ppermute x1, waiting for transfers between devices, shards(): lax.ppermute(tail, ('z', 'x'), [(i, i + 1) for i in range(ends)])  9.61 us
    pallas_call x2, Pallas kernels, shards(): sums = call(step_kernel, 'step', rows_f32, [VMEM] * 3)(sums, high, mid)  7.77 us
    pallas_call x1, Pallas kernels, shards(): call(edge_kernel, 'edge', [piece, piece, piece, rows_f32], [VMEM] * 6)  7.77 us
    pallas_call x1, Pallas kernels, shards(): call(lambda *refs: own_kernel(reach, *refs), 'own', [rows_f32, jax.ShapeD...  7.73 us
  transfers between devices with their start and end apart: 33, of which 30 were waited for; matrix products, arithmetic and copies ran while one was open for 0% of the time, Pallas kernels for 4%

profile of v3, /device:TPU:0, one launch (start us, length us, event | category | flops | bytes accessed | tf_op | source)
XLA Modules:
  0.0 212.4 jit_solution(11305458254079248016)
XLA Ops:
  0.0 4.7 %pack.1 = (f32[8,256,128]{2,1,0:T(8,128)S(1)}, f32[8,256,128]{2,1,0:T(8,128)}) custom-call(f32[8,1024,256]{2,1,0:T(8,128)} %refs_0_.3), custom_call_target="tpu_custom_call" | custom-call | tf_op jit(solution)/shard_map/edges/pack/pallas_call | solution.py:310
  4.7 3.6 %collective-permute-start = (f32[8,256,128]{2,1,0:T(8,128)}, f32[8,256,128]{2,1,0:T(8,128)S(1)}, u32[]{:S(2)}, u32[]{:S(2)}) collective-permute-start(f32[8,256,128]{2,1,0:T(8,128)} %get-tuple-element.17), channel_id=1, source_target_pairs={{0,8},{8,16},{16,24},{24,32},{32,40},{40,48},{48,56},{56,64},{64,7... | collective-permute-start | bytes 3145736 | tf_op jit(solution)/shard_map/edges/ppermute | solution.py:315
  8.3 1.3 collective-permute-start.1
  10.2 3.4 %copy-done = f32[8,1024,256]{2,1,0:T(8,128)S(1)} copy-done((f32[8,1024,256]{2,1,0:T(8,128)S(1)}, f32[8,1024,256]{2,1,0:T(8,128)}, u32[]{:S(2)}) %copy-start) | copy-done | bytes 8388632
  13.6 7.7 %own.1 = (f32[8,1024]{1,0:T(8,128)S(1)}, bf16[2,4,256,256]{3,2,1,0:T(8,128)(2,1)S(1)}, f32[8,1024,256]{2,1,0:T(8,128)S(1)}) custom-call(f32[65]{0:T(128)S(1)} %copy-done.1, f32[8,1024]{1,0:T(8,128)S(1)} %pad.4.refs_1_, f32[8,1024,256]{2,1,0:T(8,128)S(1)} %copy-done), custom_call_target="tpu_custom_call" | custom-call | tf_op jit(solution)/shard_map/own/own/pallas_call | solution.py:320
  21.3 9.6 %collective-permute-done.left_ref = f32[8,256,128]{2,1,0:T(8,128)S(1)} collective-permute-done((f32[8,256,128]{2,1,0:T(8,128)}, f32[8,256,128]{2,1,0:T(8,128)S(1)}, u32[]{:S(2)}, u32[]{:S(2)}) %collective-permute-start) | collective-permute-done | bytes 1048608 | tf_op jit(solution)/shard_map/edges/ppermute | solution.py:315
  30.9 3.9 %collective-permute-done.1.right_ref = f32[8,256,128]{2,1,0:T(8,128)S(1)} collective-permute-done((f32[8,256,128]{2,1,0:T(8,128)S(1)}, f32[8,256,128]{2,1,0:T(8,128)S(1)}, u32[]{:S(2)}, u32[]{:S(2)}) %collective-permute-start.1) | collective-permute-done | bytes 1048608 | tf_op jit(solution)/shard_map/edges/ppermute | solution.py:316
  34.8 7.8 %edge.1 = (bf16[8,1024,256]{2,1,0:T(8,128)(2,1)S(1)}, bf16[8,1024,256]{2,1,0:T(8,128)(2,1)S(1)}, bf16[8,1024,256]{2,1,0:T(8,128)(2,1)S(1)}, f32[8,1024]{1,0:T(8,128)S(1)}) custom-call(f32[8,1024]{1,0:T(8,128)S(1)} %get-tuple-element.14.basis_ref, bf16[2,4,256,256]{3,2,1,0:T(8,128)(2,1)S(1)} %get-tuple-element.15.fix_ref, ...), custom_call_target="tpu_custom_call" | custom-call | tf_op jit(solution)/shard_map/filtered/edge/pallas_call | solution.py:334
  42.6 1.2 collective-permute-done.2
  43.8 1.6 collective-permute-start.3
  45.4 2.9 %collective-permute-start.4 = (f32[8,1024]{1,0:T(8,128)S(1)}, f32[8,1024]{1,0:T(8,128)S(1)}, u32[]{:S(2)}, u32[]{:S(2)}) collective-permute-start(f32[8,1024]{1,0:T(8,128)S(1)} %add.100), channel_id=1, source_target_pairs={{0,4},{2,6},{4,0},{6,2},{1,5},{3,7},{5,1},{7,3},{8,12},{10,14},{12... | collective-permute-start | bytes 98312 | tf_op jit(solution)/shard_map/iterations/ppermute | solution.py:287
  48.3 1.3 collective-permute-start.5
  49.6 1.2 collective-permute-done.4
  50.8 1.4 collective-permute-done.5
  52.2 1.5 collective-permute-start.6
  53.7 5.2 %collective-permute-start.7 = (f32[8,1024]{1,0:T(8,128)S(1)}, f32[8,1024]{1,0:T(8,128)S(1)}, u32[]{:S(2)}, u32[]{:S(2)}) collective-permute-start(f32[8,1024]{1,0:T(8,128)S(1)} %add_add_fusion.8), channel_id=1, source_target_pairs={{0,16},{8,24},{16,0},{24,8},{1,17},{9,25},{17,1},{25,9},{2,18},{10... | collective-permute-start | bytes 98312 | tf_op jit(solution)/shard_map/iterations/ppermute | solution.py:287
  58.9 0.4 collective-permute-done.6
  59.3 1.8 collective-permute-done.7
  61.1 1.7 collective-permute-done.8
  62.8 3.7 %collective-permute-start.10 = (f32[8,1024]{1,0:T(8,128)S(1)}, f32[8,1024]{1,0:T(8,128)S(1)}, u32[]{:S(2)}, u32[]{:S(2)}) collective-permute-start(f32[8,1024]{1,0:T(8,128)S(1)} %add_add_fusion.7), channel_id=1, source_target_pairs={{0,64},{32,96},{64,0},{96,32},{1,65},{33,97},{65,1},{97,33},{2,66}... | collective-permute-start | bytes 98312 | tf_op jit(solution)/shard_map/iterations/ppermute | solution.py:287
  66.5 1.0 collective-permute-start.11
  67.5 1.0 collective-permute-start.9
  68.5 1.9 collective-permute-done.11
  70.4 2.2 %collective-permute-done.9 = f32[8,1024]{1,0:T(8,128)S(1)} collective-permute-done((f32[8,1024]{1,0:T(8,128)S(1)}, f32[8,1024]{1,0:T(8,128)S(1)}, u32[]{:S(2)}, u32[]{:S(2)}) %collective-permute-start.9) | collective-permute-done | bytes 32800 | tf_op jit(solution)/shard_map/iterations/ppermute | solution.py:287
  72.6 3.9 %step.2 = f32[8,1024]{1,0:T(8,128)S(1)} custom-call(f32[8,1024]{1,0:T(8,128)S(1)} %add_add_fusion.6.sums_ref, bf16[8,1024,256]{2,1,0:T(8,128)(2,1)S(1)} %get-tuple-element.20.high_ref, bf16[8,1024,256]{2,1,0:T(8,128)(2,1)S(1)} %get-tuple-element.21.mid_ref), custom_call_target="tpu_custom_call" | custom-call | tf_op jit(solution)/shard_map/iterations/step/pallas_call | solution.py:343
  76.6 1.2 collective-permute-done.12
  77.9 3.8 %collective-permute-start.14 = (f32[8,1024]{1,0:T(8,128)S(1)}, f32[8,1024]{1,0:T(8,128)S(1)}, u32[]{:S(2)}, u32[]{:S(2)}) collective-permute-start(f32[8,1024]{1,0:T(8,128)S(1)} %add.110), channel_id=1, source_target_pairs={{0,4},{2,6},{4,0},{6,2},{1,5},{3,7},{5,1},{7,3},{8,12},{10,14},{12... | collective-permute-start | bytes 98312 | tf_op jit(solution)/shard_map/iterations/ppermute | solution.py:287
  81.9 1.0 collective-permute-done.13
  82.9 1.1 collective-permute-done.14
  84.0 1.7 collective-permute-done.15
  85.7 0.3 collective-permute-start.16
  86.0 2.7 %collective-permute-start.17 = (f32[8,1024]{1,0:T(8,128)S(1)}, f32[8,1024]{1,0:T(8,128)S(1)}, u32[]{:S(2)}, u32[]{:S(2)}) collective-permute-start(f32[8,1024]{1,0:T(8,128)S(1)} %add_add_fusion.5), channel_id=1, source_target_pairs={{0,16},{8,24},{16,0},{24,8},{1,17},{9,25},{17,1},{25,9},{2,18},{10... | collective-permute-start | bytes 98312 | tf_op jit(solution)/shard_map/iterations/ppermute | solution.py:287
  88.6 1.5 collective-permute-start.18
  90.1 1.0 collective-permute-done.16
  91.1 0.4 collective-permute-done.17
  91.5 1.1 collective-permute-done.18
  92.6 1.5 collective-permute-start.20
  94.1 1.8 collective-permute-start.21
  95.9 1.9 collective-permute-done.19
  97.8 0.4 collective-permute-done.20
  98.1 0.8 collective-permute-done.21
  99.0 3.9 %step.3 = f32[8,1024]{1,0:T(8,128)S(1)} custom-call(f32[8,1024]{1,0:T(8,128)S(1)} %add_add_fusion.3.sums_ref, bf16[8,1024,256]{2,1,0:T(8,128)(2,1)S(1)} %get-tuple-element.20.high_ref, bf16[8,1024,256]{2,1,0:T(8,128)(2,1)S(1)} %get-tuple-element.21.mid_ref), custom_call_target="tpu_custom_call" | custom-call | tf_op jit(solution)/shard_map/iterations/step/pallas_call | solution.py:343
  102.9 1.2 collective-permute-done.22
  104.2 2.7 %collective-permute-start.24 = (f32[8,1024]{1,0:T(8,128)S(1)}, f32[8,1024]{1,0:T(8,128)S(1)}, u32[]{:S(2)}, u32[]{:S(2)}) collective-permute-start(f32[8,1024]{1,0:T(8,128)S(1)} %add.120), channel_id=1, source_target_pairs={{0,4},{2,6},{4,0},{6,2},{1,5},{3,7},{5,1},{7,3},{8,12},{10,14},{12... | collective-permute-start | bytes 98312 | tf_op jit(solution)/shard_map/iterations/ppermute | solution.py:287
  106.9 1.3 collective-permute-start.25
  108.3 1.5 collective-permute-done.23
  109.7 1.1 collective-permute-done.25
  110.8 1.5 collective-permute-start.26
  112.3 2.7 %collective-permute-start.27 = (f32[8,1024]{1,0:T(8,128)S(1)}, f32[8,1024]{1,0:T(8,128)S(1)}, u32[]{:S(2)}, u32[]{:S(2)}) collective-permute-start(f32[8,1024]{1,0:T(8,128)S(1)} %add_add_fusion.2), channel_id=1, source_target_pairs={{0,16},{8,24},{16,0},{24,8},{1,17},{9,25},{17,1},{25,9},{2,18},{10... | collective-permute-start | bytes 98312 | tf_op jit(solution)/shard_map/iterations/ppermute | solution.py:287
  115.1 0.9 collective-permute-done.26
  116.0 1.7 collective-permute-done.27
  117.7 1.2 collective-permute-done.28
  119.0 1.7 collective-permute-start.29
  120.7 2.2 %collective-permute-start.30 = (f32[8,1024]{1,0:T(8,128)S(1)}, f32[8,1024]{1,0:T(8,128)S(1)}, u32[]{:S(2)}, u32[]{:S(2)}) collective-permute-start(f32[8,1024]{1,0:T(8,128)S(1)} %add_add_fusion.1), channel_id=1, source_target_pairs={{0,64},{32,96},{64,0},{96,32},{1,65},{33,97},{65,1},{97,33},{2,66}... | collective-permute-start | bytes 98312 | tf_op jit(solution)/shard_map/iterations/ppermute | solution.py:287
  122.9 0.6 collective-permute-start.31
  123.5 0.7 collective-permute-done.29
  124.2 2.0 collective-permute-done.30
  126.1 0.7 collective-permute-done.31
  126.8 5.5 %clean.1 = bf16[32,16,32,128]{3,2,1,0:T(8,128)(2,1)} custom-call(f32[8,1024]{1,0:T(8,128)S(1)} %add_add_fusion.sums_ref, f32[8,1,256]{2,1,0:T(1,128)S(1)} %reshape.55.weight_ref, bf16[8,1024,256]{2,1,0:T(8,128)(2,1)S(1)} %get-tuple-element.20.high_ref, bf16[8,1024,256]{2,1,0:T(8,128)(2,1)S(1)} %get-tuple-element.21.mid_ref, ...), custom_call_target="tpu_custom_call" | custom-call | tf_op jit(solution)/shard_map/cleaned/clean/pallas_call | solution.py:347
  132.3 5.3 %all-to-all-start = ((bf16[32,16,32,128]{3,2,1,0:T(8,128)(2,1)}), bf16[32,16,32,128]{3,2,1,0:T(8,128)(2,1)}, u32[]{:S(2)}, u32[]{:S(2)}) async-start(bf16[32,16,32,128]{3,2,1,0:T(8,128)(2,1)} %clean.1), calls=%async_computation | async-start | bytes 8388608 | tf_op jit(solution)/shard_map/channels/all_to_all | solution.py:357
  137.7 52.8 %all-to-all-done.arrived_ref = bf16[32,16,32,128]{3,2,1,0:T(8,128)(2,1)} async-done(((bf16[32,16,32,128]{3,2,1,0:T(8,128)(2,1)}), bf16[32,16,32,128]{3,2,1,0:T(8,128)(2,1)}, u32[]{:S(2)}, u32[]{:S(2)}) %all-to-all-start) | async-done | bytes 4194336 | tf_op jit(solution)/shard_map/channels/all_to_all | solution.py:357
  190.4 5.6 %bin.1 = f32[16,32,256]{2,1,0:T(8,128)S(1)} custom-call(s32[1024]{0:T(1024)S(1)} %bitcast.5, bf16[32,16,32,128]{3,2,1,0:T(8,128)(2,1)} %all-to-all-done.arrived_ref), custom_call_target="tpu_custom_call" | custom-call | tf_op jit(solution)/shard_map/binning/bin/pallas_call | solution.py:360
  196.1 15.6 %all_to_all.10 = f32[16,32,256]{2,1,0:T(8,128)S(1)} all-to-all(f32[16,32,256]{2,1,0:T(8,128)S(1)} %bin.1), channel_id=1, replica_groups=mesh['z'=4,'x'=4,'y'=4,'c'=2] {'z','x'}, dimensions={0} | all-to-all | bytes 1048576 | tf_op jit(solution)/shard_map/tiles/all_to_all | solution.py:367
  211.7 0.7 bitcast_reduce_fusion
  (46 shorter events, 1.3 us)
Async XLA Ops:
  0.0 9.6 %copy-start.4 = (s32[8,2]{0,1:T(2,128)S(1)}, s32[8,2]{0,1:T(2,128)}, u32[]{:S(2)}) copy-start(s32[8,2]{0,1:T(2,128)} %param.10) | copy-start | bytes 196
  0.0 9.8 %copy-start.5 = (s32[8,2]{0,1:T(2,128)S(1)}, s32[8,2]{0,1:T(2,128)}, u32[]{:S(2)}) copy-start(s32[8,2]{0,1:T(2,128)} %param.11) | copy-start | bytes 196
  0.0 10.2 %copy-start.2 = (f32[6,1024]{1,0:T(8,128)S(1)}, f32[6,1024]{1,0:T(8,128)}, u32[]{:S(2)}) copy-start(f32[6,1024]{1,0:T(8,128)} %param.8) | copy-start | bytes 73732
  0.0 10.2 %copy-start.1 = (f32[65]{0:T(128)S(1)}, f32[65]{0:T(128)}, u32[]{:S(2)}) copy-start(f32[65]{0:T(128)} %refs_0_.2) | copy-start | bytes 784
  4.7 26.2 %collective-permute-start = (f32[8,256,128]{2,1,0:T(8,128)}, f32[8,256,128]{2,1,0:T(8,128)S(1)}, u32[]{:S(2)}, u32[]{:S(2)}) collective-permute-start(f32[8,256,128]{2,1,0:T(8,128)} %get-tuple-element.17), channel_id=1, source_target_pairs={{0,8},{8,16},{16,24},{24,32},{32,40},{40,48},{48,56},{56,64},{64,7... | collective-permute-start | bytes 3145736 | tf_op jit(solution)/shard_map/edges/ppermute | solution.py:315
  8.3 26.5 %collective-permute-start.1 = (f32[8,256,128]{2,1,0:T(8,128)S(1)}, f32[8,256,128]{2,1,0:T(8,128)S(1)}, u32[]{:S(2)}, u32[]{:S(2)}) collective-permute-start(f32[8,256,128]{2,1,0:T(8,128)S(1)} %get-tuple-element.18), channel_id=1, source_target_pairs={{8,0},{16,8},{24,16},{32,24},{40,32},{48,40},{56,48},{64,56},{72,6... | collective-permute-start | bytes 3145736 | tf_op jit(solution)/shard_map/edges/ppermute | solution.py:316
  10.2 3.4 %copy-start = (f32[8,1024,256]{2,1,0:T(8,128)S(1)}, f32[8,1024,256]{2,1,0:T(8,128)}, u32[]{:S(2)}) copy-start(f32[8,1024,256]{2,1,0:T(8,128)} %refs_0_.3) | copy-start | bytes 25165828
  42.6 1.2 collective-permute-start.2
  43.8 5.8 %collective-permute-start.3 = (f32[8,1024]{1,0:T(8,128)S(1)}, f32[8,1024]{1,0:T(8,128)S(1)}, u32[]{:S(2)}, u32[]{:S(2)}) collective-permute-start(f32[8,1024]{1,0:T(8,128)S(1)} %add.100), channel_id=1, source_target_pairs={{0,2},{2,4},{4,6},{6,0},{1,3},{3,5},{5,7},{7,1},{8,10},{10,12},{12... | collective-permute-start | bytes 98312 | tf_op jit(solution)/shard_map/iterations/ppermute | solution.py:287
  45.4 5.4 %collective-permute-start.4 = (f32[8,1024]{1,0:T(8,128)S(1)}, f32[8,1024]{1,0:T(8,128)S(1)}, u32[]{:S(2)}, u32[]{:S(2)}) collective-permute-start(f32[8,1024]{1,0:T(8,128)S(1)} %add.100), channel_id=1, source_target_pairs={{0,4},{2,6},{4,0},{6,2},{1,5},{3,7},{5,1},{7,3},{8,12},{10,14},{12... | collective-permute-start | bytes 98312 | tf_op jit(solution)/shard_map/iterations/ppermute | solution.py:287
  48.3 3.9 %collective-permute-start.5 = (f32[8,1024]{1,0:T(8,128)S(1)}, f32[8,1024]{1,0:T(8,128)S(1)}, u32[]{:S(2)}, u32[]{:S(2)}) collective-permute-start(f32[8,1024]{1,0:T(8,128)S(1)} %add.100), channel_id=1, source_target_pairs={{0,6},{2,0},{4,2},{6,4},{1,7},{3,1},{5,3},{7,5},{8,14},{10,8},{12,... | collective-permute-start | bytes 98312 | tf_op jit(solution)/shard_map/iterations/ppermute | solution.py:287
  52.2 7.1 %collective-permute-start.6 = (f32[8,1024]{1,0:T(8,128)S(1)}, f32[8,1024]{1,0:T(8,128)S(1)}, u32[]{:S(2)}, u32[]{:S(2)}) collective-permute-start(f32[8,1024]{1,0:T(8,128)S(1)} %add_add_fusion.8), channel_id=1, source_target_pairs={{0,8},{8,16},{16,24},{24,0},{1,9},{9,17},{17,25},{25,1},{2,10},{10... | collective-permute-start | bytes 98312 | tf_op jit(solution)/shard_map/iterations/ppermute | solution.py:287
  53.7 7.4 %collective-permute-start.7 = (f32[8,1024]{1,0:T(8,128)S(1)}, f32[8,1024]{1,0:T(8,128)S(1)}, u32[]{:S(2)}, u32[]{:S(2)}) collective-permute-start(f32[8,1024]{1,0:T(8,128)S(1)} %add_add_fusion.8), channel_id=1, source_target_pairs={{0,16},{8,24},{16,0},{24,8},{1,17},{9,25},{17,1},{25,9},{2,18},{10... | collective-permute-start | bytes 98312 | tf_op jit(solution)/shard_map/iterations/ppermute | solution.py:287
  58.9 3.9 %collective-permute-start.8 = (f32[8,1024]{1,0:T(8,128)S(1)}, f32[8,1024]{1,0:T(8,128)S(1)}, u32[]{:S(2)}, u32[]{:S(2)}) collective-permute-start(f32[8,1024]{1,0:T(8,128)S(1)} %add_add_fusion.8), channel_id=1, source_target_pairs={{0,24},{8,0},{16,8},{24,16},{1,25},{9,1},{17,9},{25,17},{2,26},{10... | collective-permute-start | bytes 98312 | tf_op jit(solution)/shard_map/iterations/ppermute | solution.py:287
  62.8 5.7 %collective-permute-start.10 = (f32[8,1024]{1,0:T(8,128)S(1)}, f32[8,1024]{1,0:T(8,128)S(1)}, u32[]{:S(2)}, u32[]{:S(2)}) collective-permute-start(f32[8,1024]{1,0:T(8,128)S(1)} %add_add_fusion.7), channel_id=1, source_target_pairs={{0,64},{32,96},{64,0},{96,32},{1,65},{33,97},{65,1},{97,33},{2,66}... | collective-permute-start | bytes 98312 | tf_op jit(solution)/shard_map/iterations/ppermute | solution.py:287
  66.5 3.9 %collective-permute-start.11 = (f32[8,1024]{1,0:T(8,128)S(1)}, f32[8,1024]{1,0:T(8,128)S(1)}, u32[]{:S(2)}, u32[]{:S(2)}) collective-permute-start(f32[8,1024]{1,0:T(8,128)S(1)} %add_add_fusion.7), channel_id=1, source_target_pairs={{0,96},{32,0},{64,32},{96,64},{1,97},{33,1},{65,33},{97,65},{2,98}... | collective-permute-start | bytes 98312 | tf_op jit(solution)/shard_map/iterations/ppermute | solution.py:287
  67.5 5.1 %collective-permute-start.9 = (f32[8,1024]{1,0:T(8,128)S(1)}, f32[8,1024]{1,0:T(8,128)S(1)}, u32[]{:S(2)}, u32[]{:S(2)}) collective-permute-start(f32[8,1024]{1,0:T(8,128)S(1)} %add_add_fusion.7), channel_id=1, source_target_pairs={{0,32},{32,64},{64,96},{96,0},{1,33},{33,65},{65,97},{97,1},{2,34}... | collective-permute-start | bytes 98312 | tf_op jit(solution)/shard_map/iterations/ppermute | solution.py:287
  76.5 1.2 collective-permute-start.12
  77.8 5.1 %collective-permute-start.13 = (f32[8,1024]{1,0:T(8,128)S(1)}, f32[8,1024]{1,0:T(8,128)S(1)}, u32[]{:S(2)}, u32[]{:S(2)}) collective-permute-start(f32[8,1024]{1,0:T(8,128)S(1)} %add.110), channel_id=1, source_target_pairs={{0,2},{2,4},{4,6},{6,0},{1,3},{3,5},{5,7},{7,1},{8,10},{10,12},{12... | collective-permute-start | bytes 98312 | tf_op jit(solution)/shard_map/iterations/ppermute | solution.py:287
  77.9 6.1 %collective-permute-start.14 = (f32[8,1024]{1,0:T(8,128)S(1)}, f32[8,1024]{1,0:T(8,128)S(1)}, u32[]{:S(2)}, u32[]{:S(2)}) collective-permute-start(f32[8,1024]{1,0:T(8,128)S(1)} %add.110), channel_id=1, source_target_pairs={{0,4},{2,6},{4,0},{6,2},{1,5},{3,7},{5,1},{7,3},{8,12},{10,14},{12... | collective-permute-start | bytes 98312 | tf_op jit(solution)/shard_map/iterations/ppermute | solution.py:287
  81.8 3.9 %collective-permute-start.15 = (f32[8,1024]{1,0:T(8,128)S(1)}, f32[8,1024]{1,0:T(8,128)S(1)}, u32[]{:S(2)}, u32[]{:S(2)}) collective-permute-start(f32[8,1024]{1,0:T(8,128)S(1)} %add.110), channel_id=1, source_target_pairs={{0,6},{2,0},{4,2},{6,4},{1,7},{3,1},{5,3},{7,5},{8,14},{10,8},{12,... | collective-permute-start | bytes 98312 | tf_op jit(solution)/shard_map/iterations/ppermute | solution.py:287
  85.7 5.4 %collective-permute-start.16 = (f32[8,1024]{1,0:T(8,128)S(1)}, f32[8,1024]{1,0:T(8,128)S(1)}, u32[]{:S(2)}, u32[]{:S(2)}) collective-permute-start(f32[8,1024]{1,0:T(8,128)S(1)} %add_add_fusion.5), channel_id=1, source_target_pairs={{0,8},{8,16},{16,24},{24,0},{1,9},{9,17},{17,25},{25,1},{2,10},{10... | collective-permute-start | bytes 98312 | tf_op jit(solution)/shard_map/iterations/ppermute | solution.py:287
  86.0 5.5 %collective-permute-start.17 = (f32[8,1024]{1,0:T(8,128)S(1)}, f32[8,1024]{1,0:T(8,128)S(1)}, u32[]{:S(2)}, u32[]{:S(2)}) collective-permute-start(f32[8,1024]{1,0:T(8,128)S(1)} %add_add_fusion.5), channel_id=1, source_target_pairs={{0,16},{8,24},{16,0},{24,8},{1,17},{9,25},{17,1},{25,9},{2,18},{10... | collective-permute-start | bytes 98312 | tf_op jit(solution)/shard_map/iterations/ppermute | solution.py:287
  88.6 3.9 %collective-permute-start.18 = (f32[8,1024]{1,0:T(8,128)S(1)}, f32[8,1024]{1,0:T(8,128)S(1)}, u32[]{:S(2)}, u32[]{:S(2)}) collective-permute-start(f32[8,1024]{1,0:T(8,128)S(1)} %add_add_fusion.5), channel_id=1, source_target_pairs={{0,24},{8,0},{16,8},{24,16},{1,25},{9,1},{17,9},{25,17},{2,26},{10... | collective-permute-start | bytes 98312 | tf_op jit(solution)/shard_map/iterations/ppermute | solution.py:287
  92.6 5.2 %collective-permute-start.19 = (f32[8,1024]{1,0:T(8,128)S(1)}, f32[8,1024]{1,0:T(8,128)S(1)}, u32[]{:S(2)}, u32[]{:S(2)}) collective-permute-start(f32[8,1024]{1,0:T(8,128)S(1)} %add_add_fusion.4), channel_id=1, source_target_pairs={{0,32},{32,64},{64,96},{96,0},{1,33},{33,65},{65,97},{97,1},{2,34}... | collective-permute-start | bytes 98312 | tf_op jit(solution)/shard_map/iterations/ppermute | solution.py:287
  92.6 5.5 %collective-permute-start.20 = (f32[8,1024]{1,0:T(8,128)S(1)}, f32[8,1024]{1,0:T(8,128)S(1)}, u32[]{:S(2)}, u32[]{:S(2)}) collective-permute-start(f32[8,1024]{1,0:T(8,128)S(1)} %add_add_fusion.4), channel_id=1, source_target_pairs={{0,64},{32,96},{64,0},{96,32},{1,65},{33,97},{65,1},{97,33},{2,66}... | collective-permute-start | bytes 98312 | tf_op jit(solution)/shard_map/iterations/ppermute | solution.py:287
  94.1 4.9 %collective-permute-start.21 = (f32[8,1024]{1,0:T(8,128)S(1)}, f32[8,1024]{1,0:T(8,128)S(1)}, u32[]{:S(2)}, u32[]{:S(2)}) collective-permute-start(f32[8,1024]{1,0:T(8,128)S(1)} %add_add_fusion.4), channel_id=1, source_target_pairs={{0,96},{32,0},{64,32},{96,64},{1,97},{33,1},{65,33},{97,65},{2,98}... | collective-permute-start | bytes 98312 | tf_op jit(solution)/shard_map/iterations/ppermute | solution.py:287
  99.0 24.5 %copy-start.3 = (f32[8,256]{1,0:T(8,128)S(1)}, f32[8,256]{1,0:T(8,128)}, u32[]{:S(2)}) copy-start(f32[8,256]{1,0:T(8,128)} %param.9) | copy-start | bytes 24580
  102.9 1.2 collective-permute-start.22
  104.1 5.6 %collective-permute-start.23 = (f32[8,1024]{1,0:T(8,128)S(1)}, f32[8,1024]{1,0:T(8,128)S(1)}, u32[]{:S(2)}, u32[]{:S(2)}) collective-permute-start(f32[8,1024]{1,0:T(8,128)S(1)} %add.120), channel_id=1, source_target_pairs={{0,2},{2,4},{4,6},{6,0},{1,3},{3,5},{5,7},{7,1},{8,10},{10,12},{12... | collective-permute-start | bytes 98312 | tf_op jit(solution)/shard_map/iterations/ppermute | solution.py:287
  104.2 5.5 %collective-permute-start.24 = (f32[8,1024]{1,0:T(8,128)S(1)}, f32[8,1024]{1,0:T(8,128)S(1)}, u32[]{:S(2)}, u32[]{:S(2)}) collective-permute-start(f32[8,1024]{1,0:T(8,128)S(1)} %add.120), channel_id=1, source_target_pairs={{0,4},{2,6},{4,0},{6,2},{1,5},{3,7},{5,1},{7,3},{8,12},{10,14},{12... | collective-permute-start | bytes 98312 | tf_op jit(solution)/shard_map/iterations/ppermute | solution.py:287
  106.9 3.9 %collective-permute-start.25 = (f32[8,1024]{1,0:T(8,128)S(1)}, f32[8,1024]{1,0:T(8,128)S(1)}, u32[]{:S(2)}, u32[]{:S(2)}) collective-permute-start(f32[8,1024]{1,0:T(8,128)S(1)} %add.120), channel_id=1, source_target_pairs={{0,6},{2,0},{4,2},{6,4},{1,7},{3,1},{5,3},{7,5},{8,14},{10,8},{12,... | collective-permute-start | bytes 98312 | tf_op jit(solution)/shard_map/iterations/ppermute | solution.py:287
  110.8 5.2 %collective-permute-start.26 = (f32[8,1024]{1,0:T(8,128)S(1)}, f32[8,1024]{1,0:T(8,128)S(1)}, u32[]{:S(2)}, u32[]{:S(2)}) collective-permute-start(f32[8,1024]{1,0:T(8,128)S(1)} %add_add_fusion.2), channel_id=1, source_target_pairs={{0,8},{8,16},{16,24},{24,0},{1,9},{9,17},{17,25},{25,1},{2,10},{10... | collective-permute-start | bytes 98312 | tf_op jit(solution)/shard_map/iterations/ppermute | solution.py:287
  112.3 5.4 %collective-permute-start.27 = (f32[8,1024]{1,0:T(8,128)S(1)}, f32[8,1024]{1,0:T(8,128)S(1)}, u32[]{:S(2)}, u32[]{:S(2)}) collective-permute-start(f32[8,1024]{1,0:T(8,128)S(1)} %add_add_fusion.2), channel_id=1, source_target_pairs={{0,16},{8,24},{16,0},{24,8},{1,17},{9,25},{17,1},{25,9},{2,18},{10... | collective-permute-start | bytes 98312 | tf_op jit(solution)/shard_map/iterations/ppermute | solution.py:287
  115.0 3.9 %collective-permute-start.28 = (f32[8,1024]{1,0:T(8,128)S(1)}, f32[8,1024]{1,0:T(8,128)S(1)}, u32[]{:S(2)}, u32[]{:S(2)}) collective-permute-start(f32[8,1024]{1,0:T(8,128)S(1)} %add_add_fusion.2), channel_id=1, source_target_pairs={{0,24},{8,0},{16,8},{24,16},{1,25},{9,1},{17,9},{25,17},{2,26},{10... | collective-permute-start | bytes 98312 | tf_op jit(solution)/shard_map/iterations/ppermute | solution.py:287
  119.0 5.2 %collective-permute-start.29 = (f32[8,1024]{1,0:T(8,128)S(1)}, f32[8,1024]{1,0:T(8,128)S(1)}, u32[]{:S(2)}, u32[]{:S(2)}) collective-permute-start(f32[8,1024]{1,0:T(8,128)S(1)} %add_add_fusion.1), channel_id=1, source_target_pairs={{0,32},{32,64},{64,96},{96,0},{1,33},{33,65},{65,97},{97,1},{2,34}... | collective-permute-start | bytes 98312 | tf_op jit(solution)/shard_map/iterations/ppermute | solution.py:287
  120.7 5.4 %collective-permute-start.30 = (f32[8,1024]{1,0:T(8,128)S(1)}, f32[8,1024]{1,0:T(8,128)S(1)}, u32[]{:S(2)}, u32[]{:S(2)}) collective-permute-start(f32[8,1024]{1,0:T(8,128)S(1)} %add_add_fusion.1), channel_id=1, source_target_pairs={{0,64},{32,96},{64,0},{96,32},{1,65},{33,97},{65,1},{97,33},{2,66}... | collective-permute-start | bytes 98312 | tf_op jit(solution)/shard_map/iterations/ppermute | solution.py:287
  122.9 3.9 %collective-permute-start.31 = (f32[8,1024]{1,0:T(8,128)S(1)}, f32[8,1024]{1,0:T(8,128)S(1)}, u32[]{:S(2)}, u32[]{:S(2)}) collective-permute-start(f32[8,1024]{1,0:T(8,128)S(1)} %add_add_fusion.1), channel_id=1, source_target_pairs={{0,96},{32,0},{64,32},{96,64},{1,97},{33,1},{65,33},{97,65},{2,98}... | collective-permute-start | bytes 98312 | tf_op jit(solution)/shard_map/iterations/ppermute | solution.py:287
  132.3 58.1 %all-to-all-start = ((bf16[32,16,32,128]{3,2,1,0:T(8,128)(2,1)}), bf16[32,16,32,128]{3,2,1,0:T(8,128)(2,1)}, u32[]{:S(2)}, u32[]{:S(2)}) async-start(bf16[32,16,32,128]{3,2,1,0:T(8,128)(2,1)} %clean.1), calls=%async_computation | async-start | bytes 8388608 | tf_op jit(solution)/shard_map/channels/all_to_all | solution.py:357

commit v4 on v3

--- a/solution.py
+++ b/solution.py
@@ -15,7 +15,7 @@
 CORES = 2
 F32 = jnp.float32
 BF16 = jnp.bfloat16
-PARAMS = pltpu.CompilerParams(vmem_limit_bytes=16 * 1024 * 1024)
+PARAMS = pltpu.CompilerParams(vmem_limit_bytes=14 * 1024 * 1024)
 VMEM = pl.BlockSpec(memory_space=pltpu.VMEM)
 SMEM = pl.BlockSpec(memory_space=pltpu.SMEM)
 HBM = pl.BlockSpec(memory_space=pltpu.HBM)
@@ -179,12 +179,14 @@
     total_ref[MODES:MODES + 1] = pointing_ref[...]
 
 
-def step_kernel(sums_ref, high_ref, mid_ref, total_ref):
+def step_kernel(sums_ref, high_ref, mid_ref, note_ref, total_ref):
     total_ref[...] = step(orth(sums_ref[...]), high_ref, mid_ref)
-
-
-def clean_kernel(sums_ref, weight_ref, high_ref, mid_ref, low_ref, out_ref,
-                 weighted_ref, sems, amounts_ref, spread_ref):
+    total_ref[MODES:MODES + 1] = note_ref[...]
+
+
+def clean_kernel(place_ref, sums_ref, weight_ref, high_ref, mid_ref, low_ref, *refs):
+    out_refs = refs[:1 + CHIPS]
+    flat_ref, ring_ref, sems, amounts_ref, spread_ref, removed_ref = refs[1 + CHIPS:]
     dishes, chans, tdev = high_ref.shape
     basis = split(orth(sums_ref[...]), 3)
     left = rows_of(basis[:2])
@@ -195,39 +197,67 @@
         amounts = split(product, 3)
         amounts_ref[dish] = rows_of([amounts[i] for i in (0, 1, 2, 0, 1, 0)])
     per_dish = tdev // BLOCK
-    owned = chans // (CHIPS * CORES)
-    part = owned // CHIPS
-
-    def copy_of(dish):
+    groups = CHIPS * CORES
+    owned = chans // groups
+    half = owned // 2
+    part = half // CHIPS
+    z, core = place_ref[0], place_ref[3]
+
+    def copies_of(dish):
         blocks = pl.ds(dish * per_dish, per_dish)
-        return pltpu.make_async_copy(
-            weighted_ref.at[dish], out_ref.at[:, blocks], sems.at[dish]
-        )
+        sources = [flat_ref.at[dish]] + [ring_ref.at[dish, s] for s in range(CHIPS)]
+        return [
+            pltpu.make_async_copy(source, out.at[:, blocks], sems.at[dish, index])
+            for index, (source, out) in enumerate(zip(sources, out_refs))
+        ]
 
     def body(dish, carry):
-        removed = mxu(spread_ref[...], amounts_ref[dish])
+        removed_ref[...] = mxu(spread_ref[...], amounts_ref[dish])
         weight = weight_ref[dish]
-        for chip in range(CHIPS):
-            for group in range(CHIPS * CORES):
-                first = group * owned + chip * part
-                rows = pl.ds(first, part)
-                filtered = (low_ref[dish, rows, :].astype(F32)
-                            + mid_ref[dish, rows, :].astype(F32)
-                            ) + high_ref[dish, rows, :].astype(F32)
-                weighted = (weight * (filtered - removed[first:first + part])).astype(BF16)
+
+        def weighted_of(first, length):
+            rows = pl.ds(first, length)
+            filtered = (low_ref[dish, rows, :].astype(F32) + mid_ref[dish, rows, :].astype(F32)
+                        ) + high_ref[dish, rows, :].astype(F32)
+            return (weight * (filtered - removed_ref[rows, :])).astype(BF16)
+
+        for group in range(groups):
+            weighted = weighted_of(group * owned, half)
+            for chip in range(CHIPS):
                 for block in range(per_dish):
-                    weighted_ref[dish, chip * CHIPS * CORES + group, block] = weighted[
-                        :, block * BLOCK:(block + 1) * BLOCK
+                    flat_ref[dish, chip * groups + group, block] = weighted[
+                        chip * part:(chip + 1) * part, block * BLOCK:(block + 1) * BLOCK
                     ]
-        copy_of(dish).start()
+        for shift in range(CHIPS):
+            for other in range(CORES):
+                inner = half + ((z + shift) & (CHIPS - 1)) * part
+                for chip in range(CHIPS):
+                    group = chip * CORES + (core + other) % CORES
+                    weighted = weighted_of(pl.multiple_of(group * owned + inner, part), part)
+                    for block in range(per_dish):
+                        ring_ref[dish, shift, other, block, chip * part:(chip + 1) * part] = (
+                            weighted[:, block * BLOCK:(block + 1) * BLOCK]
+                        )
+        for copy in copies_of(dish):
+            copy.start()
         return carry
 
     lax.fori_loop(0, dishes, body, 0)
     for dish in range(dishes):
-        copy_of(dish).wait()
-
-
-def bin_kernel(pointing_ref, arrived_ref, sky_ref, blocks_ref, sems, *others):
+        for copy in copies_of(dish):
+            copy.wait()
+
+
+def add_block(ref, place, lane, offset, block):
+    half = offset >> (BLOCK.bit_length() - 1)
+    shift = offset & (BLOCK - 1)
+    moved = pltpu.roll(block.astype(F32), shift, 1)
+    first = jnp.where((lane >= shift) == (half == 0), moved, 0.0)
+    ref[place, :, 0:BLOCK] += first
+    ref[place, :, BLOCK:2 * BLOCK] += moved - first
+
+
+def flat_bin_kernel(pointing_ref, arrived_ref, sky_ref, blocks_ref, sems, *others):
     sources, count, chans, width = arrived_ref.shape
     pieces = sems.shape[0]
     several = sources // pieces
@@ -245,16 +275,9 @@
 
     def one(source, carry):
         for block in range(count):
-            ref = totals[block % len(totals)]
             where = source * 2 * count + block
-            tile = pointing_ref[where]
-            offset = pointing_ref[where + count]
-            half = offset >> (width.bit_length() - 1)
-            shift = offset & (width - 1)
-            moved = pltpu.roll(blocks_ref[source, block].astype(F32), shift, 1)
-            first = jnp.where((lane >= shift) == (half == 0), moved, 0.0)
-            ref[tile, :, 0:width] += first
-            ref[tile, :, width:2 * width] += moved - first
+            add_block(totals[block % len(totals)], pointing_ref[where], lane,
+                      pointing_ref[where + count], blocks_ref[source, block])
         return carry
 
     def body(piece, carry):
@@ -263,6 +286,34 @@
 
     lax.fori_loop(0, pieces, body, 0)
     sky_ref[...] = (totals[0][...] + totals[1][...]) + (totals[2][...] + totals[3][...])
+
+
+def ring_bin_kernel(place_ref, pointing_ref, *refs):
+    near, far, outs, totals = (refs[i * CHIPS:(i + 1) * CHIPS] for i in range(4))
+    count, chans, width = far[0].shape
+    part = chans // CHIPS
+    z, y, core = place_ref[0], place_ref[2], place_ref[3]
+    for ref in totals:
+        ref[...] = jnp.zeros_like(ref)
+    lane = lax.broadcasted_iota(jnp.int32, (chans, width), 1)
+    last = CHIPS - 1
+
+    def body(block, carry):
+        for shift in range(CHIPS):
+            for other in range(CORES):
+                source = ((z - shift) & last) * CORES + (core + other) % CORES
+                where = source * 2 * count + block
+                value = far[shift][block] if other else near[shift][0, block]
+                add_block(totals[shift], pointing_ref[where], lane,
+                          pointing_ref[where + count], value)
+        return carry
+
+    lax.fori_loop(0, count, body, 0)
+    for shift in range(CHIPS):
+        rows = pl.ds(pl.multiple_of(((y + shift) & last) * part, part), part)
+        outs[shift][...] = (totals[0][:, rows, :] + totals[1][:, rows, :]) + (
+            totals[2][:, rows, :] + totals[3][:, rows, :]
+        )
 
 
 def call(kernel, name, out_shape, in_specs, scratch=(), out_specs=None):
@@ -301,7 +352,9 @@
     per_dish = tdev // BLOCK
     times = CHIPS * CHIPS
     sharers = CHIPS * CHIPS * CORES
-    part = chans // sharers
+    half = chans // (CHIPS * CORES) // 2
+    part = half // CHIPS
+    count = dishes * per_dish
     rows_f32 = jax.ShapeDtypeStruct((ROWS, chans), F32)
     edge_f32 = jax.ShapeDtypeStruct((dishes, size, BLOCK), F32)
     piece = pltpu.VMEM((dishes, chans, tdev), BF16)
@@ -327,46 +380,83 @@
 
     with jax.named_scope("pointing"):
         mine = jnp.concatenate([block_tile.reshape(-1), block_offset.reshape(-1)]).astype(F32)
-        slot = jnp.arange(sharers, dtype=jnp.int32)[:, None] == lax.axis_index(("x", "y", "c"))
-        pointing = jnp.where(slot, mine[None, :], 0.0).reshape(1, sharers * mine.shape[0])
+        slots = jnp.arange(sharers, dtype=jnp.int32)[:, None]
+        note, ring_note = [
+            jnp.where(slots == lax.axis_index(axes), mine[None, :], 0.0).reshape(1, chans)
+            for axes in (("x", "y", "c"), ("z", "c"))
+        ]
+        place = jnp.stack([lax.axis_index(axis) for axis in ("z", "x", "y", "c")])
 
     with jax.named_scope("filtered"):
+        note, ring_note, no_note, place, own = lax.optimization_barrier(
+            (note, ring_note, jnp.zeros_like(note), place, own)
+        )
         high, mid, low, sums = call(
             edge_kernel, "edge", [piece, piece, piece, rows_f32], [VMEM] * 6
-        )(basis, fix, own, from_left, from_right, pointing)
+        )(basis, fix, own, from_left, from_right, note)
 
     with jax.named_scope("iterations"):
         sums = total_over(sums, ("c", "y", "x"))
         pointing = sums[MODES].astype(jnp.int32)
         sums = total_over(sums, ("z",))
-        for _ in range(ITERS - 1):
-            sums = call(step_kernel, "step", rows_f32, [VMEM] * 3)(sums, high, mid)
+        sums = call(step_kernel, "step", rows_f32, [VMEM] * 4)(sums, high, mid, ring_note)
+        sums = total_over(sums, ("c", "z"))
+        ring_pointing = sums[MODES].astype(jnp.int32)
+        sums = total_over(sums, ("y", "x"))
+        for _ in range(ITERS - 2):
+            sums = call(step_kernel, "step", rows_f32, [VMEM] * 4)(
+                sums, high, mid, no_note
+            )
             sums = total_over(sums, ("c", "y", "x", "z"))
 
     with jax.named_scope("cleaned"):
-        blocks = call(
+        ring_shape = (CORES, count, half, BLOCK)
+        flat, *ring = call(
             clean_kernel, "clean",
-            pltpu.HBM((sharers, dishes * per_dish, part, BLOCK), BF16), [VMEM] * 5,
+            [pltpu.HBM((sharers, count, part, BLOCK), BF16)]
+            + [pltpu.HBM(ring_shape, BF16)] * CHIPS,
+            [SMEM] + [VMEM] * 5,
             [pltpu.VMEM((dishes, sharers, per_dish, part, BLOCK), BF16),
-             pltpu.SemaphoreType.DMA((dishes,)),
-             pltpu.VMEM((dishes, 6 * ROWS, tdev), BF16), pltpu.VMEM((chans, 6 * ROWS), BF16)],
-            HBM,
-        )(sums, weights.reshape(dishes, 1, tdev), high, mid, low)
+             pltpu.VMEM((dishes, CHIPS, CORES, per_dish, half, BLOCK), BF16),
+             pltpu.SemaphoreType.DMA((dishes, 1 + CHIPS)),
+             pltpu.VMEM((dishes, 6 * ROWS, tdev), BF16), pltpu.VMEM((chans, 6 * ROWS), BF16),
+             pltpu.VMEM((chans, tdev), F32)],
+            [HBM] * (1 + CHIPS),
+        )(place, sums, weights.reshape(dishes, 1, tdev), high, mid, low)
+
+    def along(value, axis, shift):
+        return lax.ppermute(value, axis, [(i, (i + shift) % CHIPS) for i in range(CHIPS)])
 
     with jax.named_scope("channels"):
-        arrived = lax.all_to_all(blocks, ("x", "y", "c"), 0, 0, tiled=True)
+        arrived = lax.all_to_all(flat, ("x", "y", "c"), 0, 0, tiled=True)
+        near = [ring[0]] + [along(ring[s], "z", s) for s in range(1, CHIPS)]
+        far = [lax.ppermute(value[1], "c", [(0, 1), (1, 0)]) for value in near]
 
     with jax.named_scope("binning"):
+        row_sums = call(
+            ring_bin_kernel, "ring_bin",
+            [jax.ShapeDtypeStruct((times, part, PIX), F32)] * CHIPS,
+            [SMEM, SMEM] + [VMEM] * (2 * CHIPS),
+            [pltpu.VMEM((times, half, PIX), F32)] * 4,
+        )(place, ring_pointing, *near, *far)
         sky = call(
-            bin_kernel, "bin", jax.ShapeDtypeStruct((times, part, PIX), F32), [SMEM, HBM],
-            [pltpu.VMEM(blocks.shape, BF16), pltpu.SemaphoreType.DMA((8,))]
+            flat_bin_kernel, "flat_bin", jax.ShapeDtypeStruct((times, part, PIX), F32),
+            [SMEM, HBM],
+            [pltpu.VMEM(flat.shape, BF16), pltpu.SemaphoreType.DMA((8,))]
             + [pltpu.VMEM((times, part, PIX), F32)] * 3,
         )(pointing, arrived)
 
     with jax.named_scope("tiles"):
-        parts = lax.all_to_all(sky, ("z", "x"), 0, 0, tiled=True)
-        parts = parts.reshape(CHIPS, CHIPS * part, PIX)
-        return jnp.sum(parts, axis=0, keepdims=True)
+        last, sky = lax.optimization_barrier((row_sums[-1], sky))
+        row_sums = [*row_sums[:-1], last]
+        rows = [row_sums[0]] + [along(row_sums[s], "y", s) for s in range(1, CHIPS)]
+        rows = (rows[0] + rows[1]) + (rows[2] + rows[3])
+        parts = lax.all_to_all(
+            jnp.concatenate([sky, rows], axis=1), ("z", "x"), 0, 0, tiled=True
+        ).reshape(CHIPS, CHIPS, 2, part, PIX)
+        flat_sky = jnp.sum(parts[:, :, 0], axis=0)
+        ring_sky = jnp.sum(parts[:, :, 1], axis=1)
+        return jnp.concatenate([flat_sky, ring_sky]).reshape(1, 2 * half, PIX)
 
 
 def solution(mesh):

time: 213 us -> 209 us (0.981)
  waiting for transfers between devices: 99.5 us -> 77.5 us
  starting transfers between devices: 53.2 us -> 63.8 us
  Pallas kernels: 39.1 us -> 43 us
    all_to_all x1, waiting for transfers between devices: 52.8 us -> 0.01 us  [shards(): arrived = lax.all_to_all(flat, ('x', 'y', 'c'), 0, 0, tiled=True)]
    ppermute x0 -> x10, waiting for transfers between devices: none -> 30.8 us  [the longest x6 29.3 us: along(): lax.ppermute(value, axis, [(i, (i + shift) % CHIPS) for i in range(CHIPS)])]
    ppermute x0 -> x10, starting transfers between devices: none -> 10.6 us  [the longest x6 10.1 us: along(): lax.ppermute(value, axis, [(i, (i + shift) % CHIPS) for i in range(CHIPS)])]
    pallas_call x4 -> x5, Pallas kernels: 18.9 us -> 22.5 us  [the longest x1 6.68 us: shards(): call(clean_kernel, 'clean', [pltpu.HBM((sharers, count, part, BLOCK), BF1...]
  transfers between devices with their start and end apart: 33 -> 43, of which waited for: 30 -> 35; matrix products, arithmetic and copies ran while one was open for 0% -> 0% of each run, Pallas kernels for 4% -> 8%
where the time goes in v4:
time: 209 us; the launch traced here: 208 us
  waiting for transfers between devices  77.5 us (37%)
  starting transfers between devices  63.8 us (31%)
  Pallas kernels  43 us (21%)
  blocking collectives  17.3 us (8%)
  local copies, waits for them, and re-layouts  3.99 us (2%)
  other arithmetic  2.21 us (1%)
    ppermute x30, starting transfers between devices, total_over(): lax.ppermute(value, axis, [(i, (i + s) % count) for i in range(count)])  43 us
    ppermute x30, waiting for transfers between devices, total_over(): lax.ppermute(value, axis, [(i, (i + s) % count) for i in range(count)])  33.2 us
    ppermute x6, waiting for transfers between devices, along(): lax.ppermute(value, axis, [(i, (i + shift) % CHIPS) for i in range(CHIPS)])  29.3 us
    all_to_all x1, blocking collectives, shards(): lax.all_to_all(jnp.concatenate([sky, rows], axis=1), ('z', 'x'), 0, 0, ti...  17.3 us
    ppermute x6, starting transfers between devices, along(): lax.ppermute(value, axis, [(i, (i + shift) % CHIPS) for i in range(CHIPS)])  10.1 us
    ppermute x1, waiting for transfers between devices, shards(): lax.ppermute(tail, ('z', 'x'), [(i, i + 1) for i in range(ends)])  9.4 us
    pallas_call x1, Pallas kernels, shards(): call(lambda *refs: own_kernel(reach, *refs), 'own', [rows_f32, jax.ShapeD...  7.76 us
    pallas_call x1, Pallas kernels, shards(): call(edge_kernel, 'edge', [piece, piece, piece, rows_f32], [VMEM] * 6)  7.74 us
  transfers between devices with their start and end apart: 43, of which 35 were waited for; matrix products, arithmetic and copies ran while one was open for 0% of the time, Pallas kernels for 8%

profile of v4, /device:TPU:0, one launch (start us, length us, event | category | flops | bytes accessed | tf_op | source)
XLA Modules:
  0.0 208.2 jit_solution(13261081445771949337)
XLA Ops:
  0.0 5.1 %pack.1 = (f32[8,256,128]{2,1,0:T(8,128)}, f32[8,256,128]{2,1,0:T(8,128)}) custom-call(f32[8,1024,256]{2,1,0:T(8,128)} %refs_0_.3), custom_call_target="tpu_custom_call" | custom-call | tf_op jit(solution)/shard_map/edges/pack/pallas_call | solution.py:363
  5.1 3.6 %collective-permute-start = (f32[8,256,128]{2,1,0:T(8,128)}, f32[8,256,128]{2,1,0:T(8,128)S(1)}, u32[]{:S(2)}, u32[]{:S(2)}) collective-permute-start(f32[8,256,128]{2,1,0:T(8,128)} %get-tuple-element.35), channel_id=1, source_target_pairs={{0,8},{8,16},{16,24},{24,32},{32,40},{40,48},{48,56},{56,64},{64,7... | collective-permute-start | bytes 3145736 | tf_op jit(solution)/shard_map/edges/ppermute | solution.py:368
  8.7 1.3 collective-permute-start.1
  10.7 3.4 %copy-done = f32[8,1024,256]{2,1,0:T(8,128)S(1)} copy-done((f32[8,1024,256]{2,1,0:T(8,128)S(1)}, f32[8,1024,256]{2,1,0:T(8,128)}, u32[]{:S(2)}) %copy-start) | copy-done | bytes 8388632
  14.1 7.8 %own.1 = (f32[8,1024]{1,0:T(8,128)S(1)}, bf16[2,4,256,256]{3,2,1,0:T(8,128)(2,1)S(1)}, f32[8,1024,256]{2,1,0:T(8,128)S(1)}) custom-call(f32[65]{0:T(128)S(1)} %copy-done.2, f32[8,1024]{1,0:T(8,128)S(1)} %pad.4.refs_1_, f32[8,1024,256]{2,1,0:T(8,128)S(1)} %copy-done), custom_call_target="tpu_custom_call" | custom-call | tf_op jit(solution)/shard_map/own/own/pallas_call | solution.py:373
  21.9 9.4 %collective-permute-done.left_ref = f32[8,256,128]{2,1,0:T(8,128)S(1)} collective-permute-done((f32[8,256,128]{2,1,0:T(8,128)}, f32[8,256,128]{2,1,0:T(8,128)S(1)}, u32[]{:S(2)}, u32[]{:S(2)}) %collective-permute-start) | collective-permute-done | bytes 1048608 | tf_op jit(solution)/shard_map/edges/ppermute | solution.py:368
  31.3 4.1 %collective-permute-done.1.right_ref = f32[8,256,128]{2,1,0:T(8,128)S(1)} collective-permute-done((f32[8,256,128]{2,1,0:T(8,128)}, f32[8,256,128]{2,1,0:T(8,128)S(1)}, u32[]{:S(2)}, u32[]{:S(2)}) %collective-permute-start.1) | collective-permute-done | bytes 1048608 | tf_op jit(solution)/shard_map/edges/ppermute | solution.py:369
  35.4 7.7 %edge.1 = (bf16[8,1024,256]{2,1,0:T(8,128)(2,1)S(1)}, bf16[8,1024,256]{2,1,0:T(8,128)(2,1)S(1)}, bf16[8,1024,256]{2,1,0:T(8,128)(2,1)S(1)}, f32[8,1024]{1,0:T(8,128)S(1)}) custom-call(f32[8,1024]{1,0:T(8,128)S(1)} %get-tuple-element.32.basis_ref, bf16[2,4,256,256]{3,2,1,0:T(8,128)(2,1)S(1)} %get-tuple-element.33.fix_ref, ...), custom_call_target="tpu_custom_call" | custom-call | tf_op jit(solution)/shard_map/filtered/edge/pallas_call | solution.py:394
  43.2 1.2 collective-permute-done.2
  44.4 1.6 collective-permute-start.3
  46.0 2.9 %collective-permute-start.4 = (f32[8,1024]{1,0:T(8,128)S(1)}, f32[8,1024]{1,0:T(8,128)S(1)}, u32[]{:S(2)}, u32[]{:S(2)}) collective-permute-start(f32[8,1024]{1,0:T(8,128)S(1)} %add.113), channel_id=1, source_target_pairs={{0,4},{2,6},{4,0},{6,2},{1,5},{3,7},{5,1},{7,3},{8,12},{10,14},{12... | collective-permute-start | bytes 98312 | tf_op jit(solution)/shard_map/iterations/ppermute | solution.py:338
  48.9 1.3 collective-permute-start.5
  50.2 1.2 collective-permute-done.4
  51.4 1.4 collective-permute-done.5
  52.8 1.5 collective-permute-start.6
  54.3 5.2 %collective-permute-start.7 = (f32[8,1024]{1,0:T(8,128)S(1)}, f32[8,1024]{1,0:T(8,128)S(1)}, u32[]{:S(2)}, u32[]{:S(2)}) collective-permute-start(f32[8,1024]{1,0:T(8,128)S(1)} %add_add_fusion.9), channel_id=1, source_target_pairs={{0,16},{8,24},{16,0},{24,8},{1,17},{9,25},{17,1},{25,9},{2,18},{10... | collective-permute-start | bytes 98312 | tf_op jit(solution)/shard_map/iterations/ppermute | solution.py:338
  59.9 1.8 collective-permute-done.7
  61.7 1.7 collective-permute-done.8
  63.4 3.7 %collective-permute-start.10 = (f32[8,1024]{1,0:T(8,128)S(1)}, f32[8,1024]{1,0:T(8,128)S(1)}, u32[]{:S(2)}, u32[]{:S(2)}) collective-permute-start(f32[8,1024]{1,0:T(8,128)S(1)} %add_add_fusion.8), channel_id=1, source_target_pairs={{0,64},{32,96},{64,0},{96,32},{1,65},{33,97},{65,1},{97,33},{2,66}... | collective-permute-start | bytes 98312 | tf_op jit(solution)/shard_map/iterations/ppermute | solution.py:338
  67.1 1.0 collective-permute-start.11
  68.1 1.0 collective-permute-start.9
  69.1 1.9 collective-permute-done.11
  71.0 2.2 %collective-permute-done.9 = f32[8,1024]{1,0:T(8,128)S(1)} collective-permute-done((f32[8,1024]{1,0:T(8,128)S(1)}, f32[8,1024]{1,0:T(8,128)S(1)}, u32[]{:S(2)}, u32[]{:S(2)}) %collective-permute-start.9) | collective-permute-done | bytes 32800 | tf_op jit(solution)/shard_map/iterations/ppermute | solution.py:338
  73.2 3.9 %step.2 = f32[8,1024]{1,0:T(8,128)S(1)} custom-call(f32[8,1024]{1,0:T(8,128)S(1)} %add_add_fusion.7.sums_ref, bf16[8,1024,256]{2,1,0:T(8,128)(2,1)S(1)} %get-tuple-element.39.high_ref, bf16[8,1024,256]{2,1,0:T(8,128)(2,1)S(1)} %get-tuple-element.40.mid_ref, f32[1,1024]{1,0:T(1,128)S(1)} %select_n.30.note_ref), custom_call_target="tpu_custom_call" | custom-call | tf_op jit(solution)/shard_map/iterations/step/pallas_call | solution.py:402
  77.1 1.2 collective-permute-done.12
  78.3 1.5 collective-permute-start.14
  79.8 1.8 collective-permute-start.15
  81.6 1.9 collective-permute-done.13
  85.1 3.8 %collective-permute-start.17 = (f32[8,1024]{1,0:T(8,128)S(1)}, f32[8,1024]{1,0:T(8,128)S(1)}, u32[]{:S(2)}, u32[]{:S(2)}) collective-permute-start(f32[8,1024]{1,0:T(8,128)S(1)} %add_add_fusion.6), channel_id=1, source_target_pairs={{0,4},{2,6},{4,0},{6,2},{1,5},{3,7},{5,1},{7,3},{8,12},{10,14},{12... | collective-permute-start | bytes 98312 | tf_op jit(solution)/shard_map/iterations/ppermute | solution.py:338
  89.1 1.0 collective-permute-done.16
  90.1 1.1 collective-permute-done.17
  91.2 1.7 collective-permute-done.18
  93.0 2.7 %collective-permute-start.20 = (f32[8,1024]{1,0:T(8,128)S(1)}, f32[8,1024]{1,0:T(8,128)S(1)}, u32[]{:S(2)}, u32[]{:S(2)}) collective-permute-start(f32[8,1024]{1,0:T(8,128)S(1)} %add_add_fusion.5), channel_id=1, source_target_pairs={{0,16},{8,24},{16,0},{24,8},{1,17},{9,25},{17,1},{25,9},{2,18},{10... | collective-permute-start | bytes 98312 | tf_op jit(solution)/shard_map/iterations/ppermute | solution.py:338
  95.6 1.5 collective-permute-start.21
  97.1 1.0 collective-permute-done.19
  98.5 1.1 collective-permute-done.21
  99.6 3.9 %step.3 = f32[8,1024]{1,0:T(8,128)S(1)} custom-call(f32[8,1024]{1,0:T(8,128)S(1)} %add_add_fusion.4.sums_ref, bf16[8,1024,256]{2,1,0:T(8,128)(2,1)S(1)} %get-tuple-element.39.high_ref, bf16[8,1024,256]{2,1,0:T(8,128)(2,1)S(1)} %get-tuple-element.40.mid_ref, f32[1,1024]{1,0:T(1,128)S(1)} %broadcast_in_dim.39.note_ref), custom_call_target="tpu_custom_call" | custom-call | tf_op jit(solution)/shard_map/iterations/step/pallas_call | solution.py:407
  103.5 1.2 collective-permute-done.22
  104.8 2.7 %collective-permute-start.24 = (f32[8,1024]{1,0:T(8,128)S(1)}, f32[8,1024]{1,0:T(8,128)S(1)}, u32[]{:S(2)}, u32[]{:S(2)}) collective-permute-start(f32[8,1024]{1,0:T(8,128)S(1)} %add.133), channel_id=1, source_target_pairs={{0,4},{2,6},{4,0},{6,2},{1,5},{3,7},{5,1},{7,3},{8,12},{10,14},{12... | collective-permute-start | bytes 98312 | tf_op jit(solution)/shard_map/iterations/ppermute | solution.py:338
  107.5 1.3 collective-permute-start.25
  108.9 1.5 collective-permute-done.23
  110.3 1.1 collective-permute-done.25
  111.4 1.5 collective-permute-start.26
  112.9 2.7 %collective-permute-start.27 = (f32[8,1024]{1,0:T(8,128)S(1)}, f32[8,1024]{1,0:T(8,128)S(1)}, u32[]{:S(2)}, u32[]{:S(2)}) collective-permute-start(f32[8,1024]{1,0:T(8,128)S(1)} %add_add_fusion.3), channel_id=1, source_target_pairs={{0,16},{8,24},{16,0},{24,8},{1,17},{9,25},{17,1},{25,9},{2,18},{10... | collective-permute-start | bytes 98312 | tf_op jit(solution)/shard_map/iterations/ppermute | solution.py:338
  115.7 0.9 collective-permute-done.26
  116.6 1.7 collective-permute-done.27
  118.3 1.2 collective-permute-done.28
  119.6 1.7 collective-permute-start.29
  121.3 2.2 %collective-permute-start.30 = (f32[8,1024]{1,0:T(8,128)S(1)}, f32[8,1024]{1,0:T(8,128)S(1)}, u32[]{:S(2)}, u32[]{:S(2)}) collective-permute-start(f32[8,1024]{1,0:T(8,128)S(1)} %add_add_fusion.2), channel_id=1, source_target_pairs={{0,64},{32,96},{64,0},{96,32},{1,65},{33,97},{65,1},{97,33},{2,66}... | collective-permute-start | bytes 98312 | tf_op jit(solution)/shard_map/iterations/ppermute | solution.py:338
  124.8 2.0 collective-permute-done.30
  127.4 6.7 %clean.1 = (bf16[32,16,16,128]{3,2,1,0:T(8,128)(2,1)}, bf16[2,16,64,128]{3,2,1,0:T(8,128)(2,1)}, bf16[2,16,64,128]{3,2,1,0:T(8,128)(2,1)}, bf16[2,16,64,128]{3,2,1,0:T(8,128)(2,1)}, bf16[2,16,64,128]{3,2,1,0:T(8,128)(2,1)}) custom-call(s32[4]{0:T(128)S(1)} %pad_add_fusion.place_ref, f32[8,1024]{1,0:T(8,128)S(1)} %add_add_fusion.1.sums_ref, ...), custom_call_target="tpu_custom_call" | custom-call | tf_op jit(solution)/shard_map/cleaned/clean/pallas_call | solution.py:414
  134.1 5.3 %all-to-all-start = ((bf16[32,16,16,128]{3,2,1,0:T(8,128)(2,1)}), bf16[32,16,16,128]{3,2,1,0:T(8,128)(2,1)S(1)}, u32[]{:S(2)}, u32[]{:S(2)}) async-start(bf16[32,16,16,128]{3,2,1,0:T(8,128)(2,1)} %get-tuple-element.49), calls=%async_computation | async-start | bytes 4194304 | tf_op jit(solution)/shard_map/channels/all_to_all | solution.py:431
  139.7 3.0 %collective-permute-start.33 = (bf16[2,16,64,128]{3,2,1,0:T(8,128)(2,1)}, bf16[2,16,64,128]{3,2,1,0:T(8,128)(2,1)S(1)}, u32[]{:S(2)}, u32[]{:S(2)}) collective-permute-start(bf16[2,16,64,128]{3,2,1,0:T(8,128)(2,1)} %get-tuple-element.46), channel_id=1, source_target_pairs={{0,64},{32,96},{64,0},{96,32},{1,65},{33,97},{65,1},{97,33},{2,66}... | collective-permute-start | bytes 1572872 | tf_op jit(solution)/shard_map/channels/ppermute | solution.py:428
  142.8 0.9 collective-permute-start.34
  143.8 11.9 %collective-permute-done.32.refs_1_ = bf16[2,16,64,128]{3,2,1,0:T(8,128)(2,1)S(1)} collective-permute-done((bf16[2,16,64,128]{3,2,1,0:T(8,128)(2,1)}, bf16[2,16,64,128]{3,2,1,0:T(8,128)(2,1)S(1)}, u32[]{:S(2)}, u32[]{:S(2)}) %collective-permute-start.32) | collective-permute-done | bytes 524320 | tf_op jit(solution)/shard_map/channels/ppermute | solution.py:428
  155.8 10.5 %collective-permute-done.33.refs_2_ = bf16[2,16,64,128]{3,2,1,0:T(8,128)(2,1)S(1)} collective-permute-done((bf16[2,16,64,128]{3,2,1,0:T(8,128)(2,1)}, bf16[2,16,64,128]{3,2,1,0:T(8,128)(2,1)S(1)}, u32[]{:S(2)}, u32[]{:S(2)}) %collective-permute-start.33) | collective-permute-done | bytes 524320 | tf_op jit(solution)/shard_map/channels/ppermute | solution.py:428
  168.7 3.7 %ring_bin.1 = (f32[16,16,256]{2,1,0:T(8,128)S(1)}, f32[16,16,256]{2,1,0:T(8,128)}, f32[16,16,256]{2,1,0:T(8,128)S(1)}, f32[16,16,256]{2,1,0:T(8,128)S(1)}) custom-call(s32[4]{0:T(128)S(1)} %pad_add_fusion.place_ref, s32[1024]{0:T(1024)S(1)} %bitcast.17, bf16[2,16,64,128]{3,2,1,0:T(8,128)(2,1)S(1)} %copy-done.1, ...), custom_call_target="tpu_custom_call" | custom-call | tf_op jit(solution)/shard_map/binning/ring_bin/pallas_call | solution.py:436
  172.5 1.7 collective-permute-start.39
  174.1 2.7 %collective-permute-start.40 = (f32[16,16,256]{2,1,0:T(8,128)S(1)}, f32[16,16,256]{2,1,0:T(8,128)}, u32[]{:S(2)}, u32[]{:S(2)}) collective-permute-start(f32[16,16,256]{2,1,0:T(8,128)S(1)} %get-tuple-element.53), channel_id=1, source_target_pairs={{0,4},{2,6},{4,0},{6,2},{1,5},{3,7},{5,1},{7,3},{8,12},{10,14},{12... | collective-permute-start | bytes 786440 | tf_op jit(solution)/shard_map/tiles/ppermute | solution.py:428
  176.8 4.3 %flat_bin.1 = f32[16,16,256]{2,1,0:T(8,128)S(1)} custom-call(s32[1024]{0:T(1024)S(1)} %bitcast.16, bf16[32,16,16,128]{3,2,1,0:T(8,128)(2,1)S(1)} %all-to-all-done.arrived_ref), custom_call_target="tpu_custom_call" | custom-call | tf_op jit(solution)/shard_map/binning/flat_bin/pallas_call | solution.py:442
  181.1 1.5 collective-permute-start.41
  182.6 6.4 %collective-permute-done.40 = f32[16,16,256]{2,1,0:T(8,128)} collective-permute-done((f32[16,16,256]{2,1,0:T(8,128)S(1)}, f32[16,16,256]{2,1,0:T(8,128)}, u32[]{:S(2)}, u32[]{:S(2)}) %collective-permute-start.40) | collective-permute-done | bytes 262176 | tf_op jit(solution)/shard_map/tiles/ppermute | solution.py:428
  189.1 1.1 add_add_fusion
  190.2 17.3 %all_to_all.10 = f32[16,32,256]{2,1,0:T(8,128)S(1)} all-to-all(f32[16,32,256]{2,1,0:T(8,128)S(1)} %pad_maximum_fusion), channel_id=1, replica_groups=mesh['z'=4,'x'=4,'y'=4,'c'=2] {'z','x'}, dimensions={0} | all-to-all | bytes 1048576 | tf_op jit(solution)/shard_map/tiles/all_to_all | solution.py:454
  (84 shorter events, 9.4 us)
Async XLA Ops:
  0.0 10.0 %copy-start.6 = (s32[8,2]{0,1:T(2,128)S(1)}, s32[8,2]{0,1:T(2,128)}, u32[]{:S(2)}) copy-start(s32[8,2]{0,1:T(2,128)} %param.10) | copy-start | bytes 196
  0.0 10.2 %copy-start.7 = (s32[8,2]{0,1:T(2,128)S(1)}, s32[8,2]{0,1:T(2,128)}, u32[]{:S(2)}) copy-start(s32[8,2]{0,1:T(2,128)} %param.11) | copy-start | bytes 196
  0.0 10.6 %copy-start.4 = (f32[6,1024]{1,0:T(8,128)S(1)}, f32[6,1024]{1,0:T(8,128)}, u32[]{:S(2)}) copy-start(f32[6,1024]{1,0:T(8,128)} %param.8) | copy-start | bytes 73732
  0.0 10.7 %copy-start.2 = (f32[65]{0:T(128)S(1)}, f32[65]{0:T(128)}, u32[]{:S(2)}) copy-start(f32[65]{0:T(128)} %refs_0_.2) | copy-start | bytes 784
  5.1 26.2 %collective-permute-start = (f32[8,256,128]{2,1,0:T(8,128)}, f32[8,256,128]{2,1,0:T(8,128)S(1)}, u32[]{:S(2)}, u32[]{:S(2)}) collective-permute-start(f32[8,256,128]{2,1,0:T(8,128)} %get-tuple-element.35), channel_id=1, source_target_pairs={{0,8},{8,16},{16,24},{24,32},{32,40},{40,48},{48,56},{56,64},{64,7... | collective-permute-start | bytes 3145736 | tf_op jit(solution)/shard_map/edges/ppermute | solution.py:368
  8.7 26.7 %collective-permute-start.1 = (f32[8,256,128]{2,1,0:T(8,128)}, f32[8,256,128]{2,1,0:T(8,128)S(1)}, u32[]{:S(2)}, u32[]{:S(2)}) collective-permute-start(f32[8,256,128]{2,1,0:T(8,128)} %get-tuple-element.36), channel_id=1, source_target_pairs={{8,0},{16,8},{24,16},{32,24},{40,32},{48,40},{56,48},{64,56},{72,6... | collective-permute-start | bytes 3145736 | tf_op jit(solution)/shard_map/edges/ppermute | solution.py:369
  10.7 3.4 %copy-start = (f32[8,1024,256]{2,1,0:T(8,128)S(1)}, f32[8,1024,256]{2,1,0:T(8,128)}, u32[]{:S(2)}) copy-start(f32[8,1024,256]{2,1,0:T(8,128)} %refs_0_.3) | copy-start | bytes 25165828
  43.1 1.2 collective-permute-start.2
  44.4 5.8 %collective-permute-start.3 = (f32[8,1024]{1,0:T(8,128)S(1)}, f32[8,1024]{1,0:T(8,128)S(1)}, u32[]{:S(2)}, u32[]{:S(2)}) collective-permute-start(f32[8,1024]{1,0:T(8,128)S(1)} %add.113), channel_id=1, source_target_pairs={{0,2},{2,4},{4,6},{6,0},{1,3},{3,5},{5,7},{7,1},{8,10},{10,12},{12... | collective-permute-start | bytes 98312 | tf_op jit(solution)/shard_map/iterations/ppermute | solution.py:338
  46.0 5.4 %collective-permute-start.4 = (f32[8,1024]{1,0:T(8,128)S(1)}, f32[8,1024]{1,0:T(8,128)S(1)}, u32[]{:S(2)}, u32[]{:S(2)}) collective-permute-start(f32[8,1024]{1,0:T(8,128)S(1)} %add.113), channel_id=1, source_target_pairs={{0,4},{2,6},{4,0},{6,2},{1,5},{3,7},{5,1},{7,3},{8,12},{10,14},{12... | collective-permute-start | bytes 98312 | tf_op jit(solution)/shard_map/iterations/ppermute | solution.py:338
  48.9 3.9 %collective-permute-start.5 = (f32[8,1024]{1,0:T(8,128)S(1)}, f32[8,1024]{1,0:T(8,128)S(1)}, u32[]{:S(2)}, u32[]{:S(2)}) collective-permute-start(f32[8,1024]{1,0:T(8,128)S(1)} %add.113), channel_id=1, source_target_pairs={{0,6},{2,0},{4,2},{6,4},{1,7},{3,1},{5,3},{7,5},{8,14},{10,8},{12,... | collective-permute-start | bytes 98312 | tf_op jit(solution)/shard_map/iterations/ppermute | solution.py:338
  52.8 7.1 %collective-permute-start.6 = (f32[8,1024]{1,0:T(8,128)S(1)}, f32[8,1024]{1,0:T(8,128)S(1)}, u32[]{:S(2)}, u32[]{:S(2)}) collective-permute-start(f32[8,1024]{1,0:T(8,128)S(1)} %add_add_fusion.9), channel_id=1, source_target_pairs={{0,8},{8,16},{16,24},{24,0},{1,9},{9,17},{17,25},{25,1},{2,10},{10... | collective-permute-start | bytes 98312 | tf_op jit(solution)/shard_map/iterations/ppermute | solution.py:338
  54.3 7.4 %collective-permute-start.7 = (f32[8,1024]{1,0:T(8,128)S(1)}, f32[8,1024]{1,0:T(8,128)S(1)}, u32[]{:S(2)}, u32[]{:S(2)}) collective-permute-start(f32[8,1024]{1,0:T(8,128)S(1)} %add_add_fusion.9), channel_id=1, source_target_pairs={{0,16},{8,24},{16,0},{24,8},{1,17},{9,25},{17,1},{25,9},{2,18},{10... | collective-permute-start | bytes 98312 | tf_op jit(solution)/shard_map/iterations/ppermute | solution.py:338
  59.5 3.9 %collective-permute-start.8 = (f32[8,1024]{1,0:T(8,128)S(1)}, f32[8,1024]{1,0:T(8,128)S(1)}, u32[]{:S(2)}, u32[]{:S(2)}) collective-permute-start(f32[8,1024]{1,0:T(8,128)S(1)} %add_add_fusion.9), channel_id=1, source_target_pairs={{0,24},{8,0},{16,8},{24,16},{1,25},{9,1},{17,9},{25,17},{2,26},{10... | collective-permute-start | bytes 98312 | tf_op jit(solution)/shard_map/iterations/ppermute | solution.py:338
  63.4 5.7 %collective-permute-start.10 = (f32[8,1024]{1,0:T(8,128)S(1)}, f32[8,1024]{1,0:T(8,128)S(1)}, u32[]{:S(2)}, u32[]{:S(2)}) collective-permute-start(f32[8,1024]{1,0:T(8,128)S(1)} %add_add_fusion.8), channel_id=1, source_target_pairs={{0,64},{32,96},{64,0},{96,32},{1,65},{33,97},{65,1},{97,33},{2,66}... | collective-permute-start | bytes 98312 | tf_op jit(solution)/shard_map/iterations/ppermute | solution.py:338
  67.1 3.9 %collective-permute-start.11 = (f32[8,1024]{1,0:T(8,128)S(1)}, f32[8,1024]{1,0:T(8,128)S(1)}, u32[]{:S(2)}, u32[]{:S(2)}) collective-permute-start(f32[8,1024]{1,0:T(8,128)S(1)} %add_add_fusion.8), channel_id=1, source_target_pairs={{0,96},{32,0},{64,32},{96,64},{1,97},{33,1},{65,33},{97,65},{2,98}... | collective-permute-start | bytes 98312 | tf_op jit(solution)/shard_map/iterations/ppermute | solution.py:338
  68.1 5.1 %collective-permute-start.9 = (f32[8,1024]{1,0:T(8,128)S(1)}, f32[8,1024]{1,0:T(8,128)S(1)}, u32[]{:S(2)}, u32[]{:S(2)}) collective-permute-start(f32[8,1024]{1,0:T(8,128)S(1)} %add_add_fusion.8), channel_id=1, source_target_pairs={{0,32},{32,64},{64,96},{96,0},{1,33},{33,65},{65,97},{97,1},{2,34}... | collective-permute-start | bytes 98312 | tf_op jit(solution)/shard_map/iterations/ppermute | solution.py:338
  77.1 1.2 collective-permute-start.12
  78.3 5.1 %collective-permute-start.13 = (f32[8,1024]{1,0:T(8,128)S(1)}, f32[8,1024]{1,0:T(8,128)S(1)}, u32[]{:S(2)}, u32[]{:S(2)}) collective-permute-start(f32[8,1024]{1,0:T(8,128)S(1)} %add.123), channel_id=1, source_target_pairs={{0,32},{32,64},{64,96},{96,0},{1,33},{33,65},{65,97},{97,1},{2,34}... | collective-permute-start | bytes 98312 | tf_op jit(solution)/shard_map/iterations/ppermute | solution.py:338
  78.3 5.5 %collective-permute-start.14 = (f32[8,1024]{1,0:T(8,128)S(1)}, f32[8,1024]{1,0:T(8,128)S(1)}, u32[]{:S(2)}, u32[]{:S(2)}) collective-permute-start(f32[8,1024]{1,0:T(8,128)S(1)} %add.123), channel_id=1, source_target_pairs={{0,64},{32,96},{64,0},{96,32},{1,65},{33,97},{65,1},{97,33},{2,66}... | collective-permute-start | bytes 98312 | tf_op jit(solution)/shard_map/iterations/ppermute | solution.py:338
  79.8 4.9 %collective-permute-start.15 = (f32[8,1024]{1,0:T(8,128)S(1)}, f32[8,1024]{1,0:T(8,128)S(1)}, u32[]{:S(2)}, u32[]{:S(2)}) collective-permute-start(f32[8,1024]{1,0:T(8,128)S(1)} %add.123), channel_id=1, source_target_pairs={{0,96},{32,0},{64,32},{96,64},{1,97},{33,1},{65,33},{97,65},{2,98}... | collective-permute-start | bytes 98312 | tf_op jit(solution)/shard_map/iterations/ppermute | solution.py:338
  84.7 5.4 %collective-permute-start.16 = (f32[8,1024]{1,0:T(8,128)S(1)}, f32[8,1024]{1,0:T(8,128)S(1)}, u32[]{:S(2)}, u32[]{:S(2)}) collective-permute-start(f32[8,1024]{1,0:T(8,128)S(1)} %add_add_fusion.6), channel_id=1, source_target_pairs={{0,2},{2,4},{4,6},{6,0},{1,3},{3,5},{5,7},{7,1},{8,10},{10,12},{12... | collective-permute-start | bytes 98312 | tf_op jit(solution)/shard_map/iterations/ppermute | solution.py:338
  85.1 6.1 %collective-permute-start.17 = (f32[8,1024]{1,0:T(8,128)S(1)}, f32[8,1024]{1,0:T(8,128)S(1)}, u32[]{:S(2)}, u32[]{:S(2)}) collective-permute-start(f32[8,1024]{1,0:T(8,128)S(1)} %add_add_fusion.6), channel_id=1, source_target_pairs={{0,4},{2,6},{4,0},{6,2},{1,5},{3,7},{5,1},{7,3},{8,12},{10,14},{12... | collective-permute-start | bytes 98312 | tf_op jit(solution)/shard_map/iterations/ppermute | solution.py:338
  89.0 3.9 %collective-permute-start.18 = (f32[8,1024]{1,0:T(8,128)S(1)}, f32[8,1024]{1,0:T(8,128)S(1)}, u32[]{:S(2)}, u32[]{:S(2)}) collective-permute-start(f32[8,1024]{1,0:T(8,128)S(1)} %add_add_fusion.6), channel_id=1, source_target_pairs={{0,6},{2,0},{4,2},{6,4},{1,7},{3,1},{5,3},{7,5},{8,14},{10,8},{12,... | collective-permute-start | bytes 98312 | tf_op jit(solution)/shard_map/iterations/ppermute | solution.py:338
  92.9 5.2 %collective-permute-start.19 = (f32[8,1024]{1,0:T(8,128)S(1)}, f32[8,1024]{1,0:T(8,128)S(1)}, u32[]{:S(2)}, u32[]{:S(2)}) collective-permute-start(f32[8,1024]{1,0:T(8,128)S(1)} %add_add_fusion.5), channel_id=1, source_target_pairs={{0,8},{8,16},{16,24},{24,0},{1,9},{9,17},{17,25},{25,1},{2,10},{10... | collective-permute-start | bytes 98312 | tf_op jit(solution)/shard_map/iterations/ppermute | solution.py:338
  93.0 5.5 %collective-permute-start.20 = (f32[8,1024]{1,0:T(8,128)S(1)}, f32[8,1024]{1,0:T(8,128)S(1)}, u32[]{:S(2)}, u32[]{:S(2)}) collective-permute-start(f32[8,1024]{1,0:T(8,128)S(1)} %add_add_fusion.5), channel_id=1, source_target_pairs={{0,16},{8,24},{16,0},{24,8},{1,17},{9,25},{17,1},{25,9},{2,18},{10... | collective-permute-start | bytes 98312 | tf_op jit(solution)/shard_map/iterations/ppermute | solution.py:338
  95.6 3.9 %collective-permute-start.21 = (f32[8,1024]{1,0:T(8,128)S(1)}, f32[8,1024]{1,0:T(8,128)S(1)}, u32[]{:S(2)}, u32[]{:S(2)}) collective-permute-start(f32[8,1024]{1,0:T(8,128)S(1)} %add_add_fusion.5), channel_id=1, source_target_pairs={{0,24},{8,0},{16,8},{24,16},{1,25},{9,1},{17,9},{25,17},{2,26},{10... | collective-permute-start | bytes 98312 | tf_op jit(solution)/shard_map/iterations/ppermute | solution.py:338
  99.6 24.5 %copy-start.5 = (f32[8,256]{1,0:T(8,128)S(1)}, f32[8,256]{1,0:T(8,128)}, u32[]{:S(2)}) copy-start(f32[8,256]{1,0:T(8,128)} %param.9) | copy-start | bytes 24580
  103.5 1.2 collective-permute-start.22
  104.7 5.6 %collective-permute-start.23 = (f32[8,1024]{1,0:T(8,128)S(1)}, f32[8,1024]{1,0:T(8,128)S(1)}, u32[]{:S(2)}, u32[]{:S(2)}) collective-permute-start(f32[8,1024]{1,0:T(8,128)S(1)} %add.133), channel_id=1, source_target_pairs={{0,2},{2,4},{4,6},{6,0},{1,3},{3,5},{5,7},{7,1},{8,10},{10,12},{12... | collective-permute-start | bytes 98312 | tf_op jit(solution)/shard_map/iterations/ppermute | solution.py:338
  104.8 5.5 %collective-permute-start.24 = (f32[8,1024]{1,0:T(8,128)S(1)}, f32[8,1024]{1,0:T(8,128)S(1)}, u32[]{:S(2)}, u32[]{:S(2)}) collective-permute-start(f32[8,1024]{1,0:T(8,128)S(1)} %add.133), channel_id=1, source_target_pairs={{0,4},{2,6},{4,0},{6,2},{1,5},{3,7},{5,1},{7,3},{8,12},{10,14},{12... | collective-permute-start | bytes 98312 | tf_op jit(solution)/shard_map/iterations/ppermute | solution.py:338
  107.5 3.9 %collective-permute-start.25 = (f32[8,1024]{1,0:T(8,128)S(1)}, f32[8,1024]{1,0:T(8,128)S(1)}, u32[]{:S(2)}, u32[]{:S(2)}) collective-permute-start(f32[8,1024]{1,0:T(8,128)S(1)} %add.133), channel_id=1, source_target_pairs={{0,6},{2,0},{4,2},{6,4},{1,7},{3,1},{5,3},{7,5},{8,14},{10,8},{12,... | collective-permute-start | bytes 98312 | tf_op jit(solution)/shard_map/iterations/ppermute | solution.py:338
  111.4 5.2 %collective-permute-start.26 = (f32[8,1024]{1,0:T(8,128)S(1)}, f32[8,1024]{1,0:T(8,128)S(1)}, u32[]{:S(2)}, u32[]{:S(2)}) collective-permute-start(f32[8,1024]{1,0:T(8,128)S(1)} %add_add_fusion.3), channel_id=1, source_target_pairs={{0,8},{8,16},{16,24},{24,0},{1,9},{9,17},{17,25},{25,1},{2,10},{10... | collective-permute-start | bytes 98312 | tf_op jit(solution)/shard_map/iterations/ppermute | solution.py:338
  112.9 5.4 %collective-permute-start.27 = (f32[8,1024]{1,0:T(8,128)S(1)}, f32[8,1024]{1,0:T(8,128)S(1)}, u32[]{:S(2)}, u32[]{:S(2)}) collective-permute-start(f32[8,1024]{1,0:T(8,128)S(1)} %add_add_fusion.3), channel_id=1, source_target_pairs={{0,16},{8,24},{16,0},{24,8},{1,17},{9,25},{17,1},{25,9},{2,18},{10... | collective-permute-start | bytes 98312 | tf_op jit(solution)/shard_map/iterations/ppermute | solution.py:338
  115.6 3.9 %collective-permute-start.28 = (f32[8,1024]{1,0:T(8,128)S(1)}, f32[8,1024]{1,0:T(8,128)S(1)}, u32[]{:S(2)}, u32[]{:S(2)}) collective-permute-start(f32[8,1024]{1,0:T(8,128)S(1)} %add_add_fusion.3), channel_id=1, source_target_pairs={{0,24},{8,0},{16,8},{24,16},{1,25},{9,1},{17,9},{25,17},{2,26},{10... | collective-permute-start | bytes 98312 | tf_op jit(solution)/shard_map/iterations/ppermute | solution.py:338
  119.6 5.2 %collective-permute-start.29 = (f32[8,1024]{1,0:T(8,128)S(1)}, f32[8,1024]{1,0:T(8,128)S(1)}, u32[]{:S(2)}, u32[]{:S(2)}) collective-permute-start(f32[8,1024]{1,0:T(8,128)S(1)} %add_add_fusion.2), channel_id=1, source_target_pairs={{0,32},{32,64},{64,96},{96,0},{1,33},{33,65},{65,97},{97,1},{2,34}... | collective-permute-start | bytes 98312 | tf_op jit(solution)/shard_map/iterations/ppermute | solution.py:338
  121.3 5.4 %collective-permute-start.30 = (f32[8,1024]{1,0:T(8,128)S(1)}, f32[8,1024]{1,0:T(8,128)S(1)}, u32[]{:S(2)}, u32[]{:S(2)}) collective-permute-start(f32[8,1024]{1,0:T(8,128)S(1)} %add_add_fusion.2), channel_id=1, source_target_pairs={{0,64},{32,96},{64,0},{96,32},{1,65},{33,97},{65,1},{97,33},{2,66}... | collective-permute-start | bytes 98312 | tf_op jit(solution)/shard_map/iterations/ppermute | solution.py:338
  123.5 3.9 %collective-permute-start.31 = (f32[8,1024]{1,0:T(8,128)S(1)}, f32[8,1024]{1,0:T(8,128)S(1)}, u32[]{:S(2)}, u32[]{:S(2)}) collective-permute-start(f32[8,1024]{1,0:T(8,128)S(1)} %add_add_fusion.2), channel_id=1, source_target_pairs={{0,96},{32,0},{64,32},{96,64},{1,97},{33,1},{65,33},{97,65},{2,98}... | collective-permute-start | bytes 98312 | tf_op jit(solution)/shard_map/iterations/ppermute | solution.py:338
  134.1 8.7 %copy-start.8 = (bf16[2,16,64,128]{3,2,1,0:T(8,128)(2,1)S(1)}, bf16[2,16,64,128]{3,2,1,0:T(8,128)(2,1)}, u32[]{:S(2)}) copy-start(bf16[2,16,64,128]{3,2,1,0:T(8,128)(2,1)} %get-tuple-element.47) | copy-start | bytes 1572868
  134.1 9.5 %copy-start.1 = (bf16[2,16,64,128]{3,2,1,0:T(8,128)(2,1)S(1)}, bf16[2,16,64,128]{3,2,1,0:T(8,128)(2,1)}, u32[]{:S(2)}) copy-start(bf16[2,16,64,128]{3,2,1,0:T(8,128)(2,1)} %get-tuple-element.44.refs_0_) | copy-start | bytes 1572868
  134.1 42.7 %all-to-all-start = ((bf16[32,16,16,128]{3,2,1,0:T(8,128)(2,1)}), bf16[32,16,16,128]{3,2,1,0:T(8,128)(2,1)S(1)}, u32[]{:S(2)}, u32[]{:S(2)}) async-start(bf16[32,16,16,128]{3,2,1,0:T(8,128)(2,1)} %get-tuple-element.49), calls=%async_computation | async-start | bytes 4194304 | tf_op jit(solution)/shard_map/channels/all_to_all | solution.py:431
  139.4 16.2 %collective-permute-start.32 = (bf16[2,16,64,128]{3,2,1,0:T(8,128)(2,1)}, bf16[2,16,64,128]{3,2,1,0:T(8,128)(2,1)S(1)}, u32[]{:S(2)}, u32[]{:S(2)}) collective-permute-start(bf16[2,16,64,128]{3,2,1,0:T(8,128)(2,1)} %get-tuple-element.45), channel_id=1, source_target_pairs={{0,32},{32,64},{64,96},{96,0},{1,33},{33,65},{65,97},{97,1},{2,34}... | collective-permute-start | bytes 1572872 | tf_op jit(solution)/shard_map/channels/ppermute | solution.py:428
  139.7 26.5 %collective-permute-start.33 = (bf16[2,16,64,128]{3,2,1,0:T(8,128)(2,1)}, bf16[2,16,64,128]{3,2,1,0:T(8,128)(2,1)S(1)}, u32[]{:S(2)}, u32[]{:S(2)}) collective-permute-start(bf16[2,16,64,128]{3,2,1,0:T(8,128)(2,1)} %get-tuple-element.46), channel_id=1, source_target_pairs={{0,64},{32,96},{64,0},{96,32},{1,65},{33,97},{65,1},{97,33},{2,66}... | collective-permute-start | bytes 1572872 | tf_op jit(solution)/shard_map/channels/ppermute | solution.py:428
  142.8 24.1 %collective-permute-start.34 = (bf16[2,16,64,128]{3,2,1,0:T(8,128)(2,1)S(1)}, bf16[2,16,64,128]{3,2,1,0:T(8,128)(2,1)S(1)}, u32[]{:S(2)}, u32[]{:S(2)}) collective-permute-start(bf16[2,16,64,128]{3,2,1,0:T(8,128)(2,1)S(1)} %copy-done.8), channel_id=1, source_target_pairs={{0,96},{32,0},{64,32},{96,64},{1,97},{33,1},{65,33},{97,65},{2,98}... | collective-permute-start | bytes 1572872 | tf_op jit(solution)/shard_map/channels/ppermute | solution.py:428
  143.7 23.6 %collective-permute-start.35 = (bf16[16,64,128]{2,1,0:T(8,128)(2,1)S(1)}, bf16[16,64,128]{2,1,0:T(8,128)(2,1)S(1)}, u32[]{:S(2)}, u32[]{:S(2)}) collective-permute-start(bf16[16,64,128]{2,1,0:T(8,128)(2,1)S(1)} %slice_bitcast_fusion.3), channel_id=1, source_target_pairs={{0,1},{1,0},{2,3},{3,2},{4,5},{5,4},{6,7},{7,6},{8,9},{9,8},{10,11... | collective-permute-start | bytes 786440 | tf_op jit(solution)/shard_map/channels/ppermute | solution.py:433
  155.7 11.6 %collective-permute-start.36 = (bf16[16,64,128]{2,1,0:T(8,128)(2,1)S(1)}, bf16[16,64,128]{2,1,0:T(8,128)(2,1)S(1)}, u32[]{:S(2)}, u32[]{:S(2)}) collective-permute-start(bf16[16,64,128]{2,1,0:T(8,128)(2,1)S(1)} %slice_bitcast_fusion.2), channel_id=1, source_target_pairs={{0,1},{1,0},{2,3},{3,2},{4,5},{5,4},{6,7},{7,6},{8,9},{9,8},{10,11... | collective-permute-start | bytes 786440 | tf_op jit(solution)/shard_map/channels/ppermute | solution.py:433
  166.3 1.6 collective-permute-start.37
  166.9 1.8 collective-permute-start.38
  172.5 10.2 %collective-permute-start.39 = (f32[16,16,256]{2,1,0:T(8,128)}, f32[16,16,256]{2,1,0:T(8,128)S(1)}, u32[]{:S(2)}, u32[]{:S(2)}) collective-permute-start(f32[16,16,256]{2,1,0:T(8,128)} %get-tuple-element.52), channel_id=1, source_target_pairs={{0,2},{2,4},{4,6},{6,0},{1,3},{3,5},{5,7},{7,1},{8,10},{10,12},{12... | collective-permute-start | bytes 786440 | tf_op jit(solution)/shard_map/tiles/ppermute | solution.py:428
  174.1 14.9 %collective-permute-start.40 = (f32[16,16,256]{2,1,0:T(8,128)S(1)}, f32[16,16,256]{2,1,0:T(8,128)}, u32[]{:S(2)}, u32[]{:S(2)}) collective-permute-start(f32[16,16,256]{2,1,0:T(8,128)S(1)} %get-tuple-element.53), channel_id=1, source_target_pairs={{0,4},{2,6},{4,0},{6,2},{1,5},{3,7},{5,1},{7,3},{8,12},{10,14},{12... | collective-permute-start | bytes 786440 | tf_op jit(solution)/shard_map/tiles/ppermute | solution.py:428
  181.1 8.0 %collective-permute-start.41 = (f32[16,16,256]{2,1,0:T(8,128)S(1)}, f32[16,16,256]{2,1,0:T(8,128)S(1)}, u32[]{:S(2)}, u32[]{:S(2)}) collective-permute-start(f32[16,16,256]{2,1,0:T(8,128)S(1)} %get-tuple-element.54), channel_id=1, source_target_pairs={{0,6},{2,0},{4,2},{6,4},{1,7},{3,1},{5,3},{7,5},{8,14},{10,8},{12,... | collective-permute-start | bytes 786440 | tf_op jit(solution)/shard_map/tiles/ppermute | solution.py:428
  182.6 6.4 %copy-start.3 = (f32[16,16,256]{2,1,0:T(8,128)}, f32[16,16,256]{2,1,0:T(8,128)S(1)}, u32[]{:S(2)}) copy-start(f32[16,16,256]{2,1,0:T(8,128)S(1)} %collective-permute-done.39) | copy-start | bytes 786436

commit v5 on v4

--- a/solution.py
+++ b/solution.py
@@ -186,7 +186,7 @@
 
 def clean_kernel(place_ref, sums_ref, weight_ref, high_ref, mid_ref, low_ref, *refs):
     out_refs = refs[:1 + CHIPS]
-    flat_ref, ring_ref, sems, amounts_ref, spread_ref, removed_ref = refs[1 + CHIPS:]
+    flat_ref, ring_ref, sems, amounts_ref, spread_ref = refs[1 + CHIPS:]
     dishes, chans, tdev = high_ref.shape
     basis = split(orth(sums_ref[...]), 3)
     left = rows_of(basis[:2])
@@ -212,32 +212,27 @@
         ]
 
     def body(dish, carry):
-        removed_ref[...] = mxu(spread_ref[...], amounts_ref[dish])
+        removed = mxu(spread_ref[...], amounts_ref[dish])
         weight = weight_ref[dish]
-
-        def weighted_of(first, length):
-            rows = pl.ds(first, length)
+        for group in range(groups):
+            chip, other = group // CORES, (group + core) % CORES
+            rows = pl.ds(group * owned, owned)
             filtered = (low_ref[dish, rows, :].astype(F32) + mid_ref[dish, rows, :].astype(F32)
                         ) + high_ref[dish, rows, :].astype(F32)
-            return (weight * (filtered - removed_ref[rows, :])).astype(BF16)
-
-        for group in range(groups):
-            weighted = weighted_of(group * owned, half)
-            for chip in range(CHIPS):
+            removed_here = removed[group * owned:(group + 1) * owned]
+            weighted = (weight * (filtered - removed_here)).astype(BF16)
+            for place in range(CHIPS):
+                shift = (place - z) & (CHIPS - 1)
                 for block in range(per_dish):
-                    flat_ref[dish, chip * groups + group, block] = weighted[
-                        chip * part:(chip + 1) * part, block * BLOCK:(block + 1) * BLOCK
+                    lanes = slice(block * BLOCK, (block + 1) * BLOCK)
+                    first = place * part
+                    flat_ref[dish, place * groups + group, block] = weighted[
+                        first:first + part, lanes
                     ]
-        for shift in range(CHIPS):
-            for other in range(CORES):
-                inner = half + ((z + shift) & (CHIPS - 1)) * part
-                for chip in range(CHIPS):
-                    group = chip * CORES + (core + other) % CORES
-                    weighted = weighted_of(pl.multiple_of(group * owned + inner, part), part)
-                    for block in range(per_dish):
-                        ring_ref[dish, shift, other, block, chip * part:(chip + 1) * part] = (
-                            weighted[:, block * BLOCK:(block + 1) * BLOCK]
-                        )
+                    first += half
+                    ring_ref[dish, shift, other, block, chip * part:(chip + 1) * part] = (
+                        weighted[first:first + part, lanes]
+                    )
         for copy in copies_of(dish):
             copy.start()
         return carry
@@ -290,6 +285,7 @@
 
 def ring_bin_kernel(place_ref, pointing_ref, *refs):
     near, far, outs, totals = (refs[i * CHIPS:(i + 1) * CHIPS] for i in range(4))
+    rest, totals = totals[0], refs[3 * CHIPS + 1:]
     count, chans, width = far[0].shape
     part = chans // CHIPS
     z, y, core = place_ref[0], place_ref[2], place_ref[3]
@@ -311,9 +307,13 @@
     lax.fori_loop(0, count, body, 0)
     for shift in range(CHIPS):
         rows = pl.ds(pl.multiple_of(((y + shift) & last) * part, part), part)
-        outs[shift][...] = (totals[0][:, rows, :] + totals[1][:, rows, :]) + (
+        total = (totals[0][:, rows, :] + totals[1][:, rows, :]) + (
             totals[2][:, rows, :] + totals[3][:, rows, :]
         )
+        tiles = outs[shift].shape[0]
+        outs[shift][...] = total[:tiles]
+        if tiles < total.shape[0]:
+            rest[...] = total[tiles:]
 
 
 def call(kernel, name, out_shape, in_specs, scratch=(), out_specs=None):
@@ -419,8 +419,7 @@
             [pltpu.VMEM((dishes, sharers, per_dish, part, BLOCK), BF16),
              pltpu.VMEM((dishes, CHIPS, CORES, per_dish, half, BLOCK), BF16),
              pltpu.SemaphoreType.DMA((dishes, 1 + CHIPS)),
-             pltpu.VMEM((dishes, 6 * ROWS, tdev), BF16), pltpu.VMEM((chans, 6 * ROWS), BF16),
-             pltpu.VMEM((chans, tdev), F32)],
+             pltpu.VMEM((dishes, 6 * ROWS, tdev), BF16), pltpu.VMEM((chans, 6 * ROWS), BF16)],
             [HBM] * (1 + CHIPS),
         )(place, sums, weights.reshape(dishes, 1, tdev), high, mid, low)
 
@@ -435,7 +434,8 @@
     with jax.named_scope("binning"):
         row_sums = call(
             ring_bin_kernel, "ring_bin",
-            [jax.ShapeDtypeStruct((times, part, PIX), F32)] * CHIPS,
+            [jax.ShapeDtypeStruct((tiles, part, PIX), F32)
+             for tiles in [times] * (CHIPS - 1) + [times - 1, 1]],
             [SMEM, SMEM] + [VMEM] * (2 * CHIPS),
             [pltpu.VMEM((times, half, PIX), F32)] * 4,
         )(place, ring_pointing, *near, *far)
@@ -447,9 +447,9 @@
         )(pointing, arrived)
 
     with jax.named_scope("tiles"):
-        last, sky = lax.optimization_barrier((row_sums[-1], sky))
-        row_sums = [*row_sums[:-1], last]
+        rest, sky = lax.optimization_barrier((row_sums[-1], sky))
         rows = [row_sums[0]] + [along(row_sums[s], "y", s) for s in range(1, CHIPS)]
+        rows[-1] = jnp.concatenate([rows[-1], along(rest, "y", CHIPS - 1)])
         rows = (rows[0] + rows[1]) + (rows[2] + rows[3])
         parts = lax.all_to_all(
             jnp.concatenate([sky, rows], axis=1), ("z", "x"), 0, 0, tiled=True

time: 209 us -> 209 us (level)
    ppermute x6 -> x7, waiting for transfers between devices: 29.3 us -> 29.1 us  [along(): lax.ppermute(value, axis, [(i, (i + shift) % CHIPS) for i in range(CHIPS)])]
    ppermute x6 -> x7, starting transfers between devices: 10.1 us -> 10.1 us  [along(): lax.ppermute(value, axis, [(i, (i + shift) % CHIPS) for i in range(CHIPS)])]
  transfers between devices with their start and end apart: 43 -> 44, of which waited for: 35 -> 36; matrix products, arithmetic and copies ran while one was open for 0% -> 0% of each run, Pallas kernels for 8% -> 8%
where the time goes in v5:
time: 209 us; the launch traced here: 208 us
  waiting for transfers between devices  77.3 us (37%)
  starting transfers between devices  63.9 us (31%)
  Pallas kernels  42.6 us (20%)
  blocking collectives  17.3 us (8%)
  local copies, waits for them, and re-layouts  4.04 us (2%)
  other arithmetic  2.35 us (1%)
    ppermute x30, starting transfers between devices, total_over(): lax.ppermute(value, axis, [(i, (i + s) % count) for i in range(count)])  43 us
    ppermute x30, waiting for transfers between devices, total_over(): lax.ppermute(value, axis, [(i, (i + s) % count) for i in range(count)])  33.2 us
    ppermute x7, waiting for transfers between devices, along(): lax.ppermute(value, axis, [(i, (i + shift) % CHIPS) for i in range(CHIPS)])  29.1 us
    all_to_all x1, blocking collectives, shards(): lax.all_to_all(jnp.concatenate([sky, rows], axis=1), ('z', 'x'), 0, 0, ti...  17.3 us
    ppermute x7, starting transfers between devices, along(): lax.ppermute(value, axis, [(i, (i + shift) % CHIPS) for i in range(CHIPS)])  10.1 us
    ppermute x1, waiting for transfers between devices, shards(): lax.ppermute(tail, ('z', 'x'), [(i, i + 1) for i in range(ends)])  9.39 us
    pallas_call x1, Pallas kernels, shards(): call(lambda *refs: own_kernel(reach, *refs), 'own', [rows_f32, jax.ShapeD...  7.77 us
    pallas_call x1, Pallas kernels, shards(): call(edge_kernel, 'edge', [piece, piece, piece, rows_f32], [VMEM] * 6)  7.74 us
  transfers between devices with their start and end apart: 44, of which 36 were waited for; matrix products, arithmetic and copies ran while one was open for 0% of the time, Pallas kernels for 8%

profile of v5, /device:TPU:0, one launch (start us, length us, event | category | flops | bytes accessed | tf_op | source)
XLA Modules:
  0.0 207.8 jit_solution(9439681428219389184)
XLA Ops:
  0.0 5.1 %pack.1 = (f32[8,256,128]{2,1,0:T(8,128)}, f32[8,256,128]{2,1,0:T(8,128)}) custom-call(f32[8,1024,256]{2,1,0:T(8,128)} %refs_0_.3), custom_call_target="tpu_custom_call" | custom-call | tf_op jit(solution)/shard_map/edges/pack/pallas_call | solution.py:363
  5.1 3.6 %collective-permute-start = (f32[8,256,128]{2,1,0:T(8,128)}, f32[8,256,128]{2,1,0:T(8,128)S(1)}, u32[]{:S(2)}, u32[]{:S(2)}) collective-permute-start(f32[8,256,128]{2,1,0:T(8,128)} %get-tuple-element.36), channel_id=1, source_target_pairs={{0,8},{8,16},{16,24},{24,32},{32,40},{40,48},{48,56},{56,64},{64,7... | collective-permute-start | bytes 3145736 | tf_op jit(solution)/shard_map/edges/ppermute | solution.py:368
  8.7 1.3 collective-permute-start.1
  10.7 3.4 %copy-done = f32[8,1024,256]{2,1,0:T(8,128)S(1)} copy-done((f32[8,1024,256]{2,1,0:T(8,128)S(1)}, f32[8,1024,256]{2,1,0:T(8,128)}, u32[]{:S(2)}) %copy-start) | copy-done | bytes 8388632
  14.1 7.8 %own.1 = (f32[8,1024]{1,0:T(8,128)S(1)}, bf16[2,4,256,256]{3,2,1,0:T(8,128)(2,1)S(1)}, f32[8,1024,256]{2,1,0:T(8,128)S(1)}) custom-call(f32[65]{0:T(128)S(1)} %copy-done.2, f32[8,1024]{1,0:T(8,128)S(1)} %pad.4.refs_1_, f32[8,1024,256]{2,1,0:T(8,128)S(1)} %copy-done), custom_call_target="tpu_custom_call" | custom-call | tf_op jit(solution)/shard_map/own/own/pallas_call | solution.py:373
  21.9 9.4 %collective-permute-done.left_ref = f32[8,256,128]{2,1,0:T(8,128)S(1)} collective-permute-done((f32[8,256,128]{2,1,0:T(8,128)}, f32[8,256,128]{2,1,0:T(8,128)S(1)}, u32[]{:S(2)}, u32[]{:S(2)}) %collective-permute-start) | collective-permute-done | bytes 1048608 | tf_op jit(solution)/shard_map/edges/ppermute | solution.py:368
  31.3 4.1 %collective-permute-done.1.right_ref = f32[8,256,128]{2,1,0:T(8,128)S(1)} collective-permute-done((f32[8,256,128]{2,1,0:T(8,128)}, f32[8,256,128]{2,1,0:T(8,128)S(1)}, u32[]{:S(2)}, u32[]{:S(2)}) %collective-permute-start.1) | collective-permute-done | bytes 1048608 | tf_op jit(solution)/shard_map/edges/ppermute | solution.py:369
  35.4 7.7 %edge.1 = (bf16[8,1024,256]{2,1,0:T(8,128)(2,1)S(1)}, bf16[8,1024,256]{2,1,0:T(8,128)(2,1)S(1)}, bf16[8,1024,256]{2,1,0:T(8,128)(2,1)S(1)}, f32[8,1024]{1,0:T(8,128)S(1)}) custom-call(f32[8,1024]{1,0:T(8,128)S(1)} %get-tuple-element.33.basis_ref, bf16[2,4,256,256]{3,2,1,0:T(8,128)(2,1)S(1)} %get-tuple-element.34.fix_ref, ...), custom_call_target="tpu_custom_call" | custom-call | tf_op jit(solution)/shard_map/filtered/edge/pallas_call | solution.py:394
  43.2 1.2 collective-permute-done.2
  44.4 1.6 collective-permute-start.3
  46.0 2.9 %collective-permute-start.4 = (f32[8,1024]{1,0:T(8,128)S(1)}, f32[8,1024]{1,0:T(8,128)S(1)}, u32[]{:S(2)}, u32[]{:S(2)}) collective-permute-start(f32[8,1024]{1,0:T(8,128)S(1)} %add.113), channel_id=1, source_target_pairs={{0,4},{2,6},{4,0},{6,2},{1,5},{3,7},{5,1},{7,3},{8,12},{10,14},{12... | collective-permute-start | bytes 98312 | tf_op jit(solution)/shard_map/iterations/ppermute | solution.py:338
  48.9 1.3 collective-permute-start.5
  50.2 1.2 collective-permute-done.4
  51.4 1.4 collective-permute-done.5
  52.8 1.5 collective-permute-start.6
  54.3 5.2 %collective-permute-start.7 = (f32[8,1024]{1,0:T(8,128)S(1)}, f32[8,1024]{1,0:T(8,128)S(1)}, u32[]{:S(2)}, u32[]{:S(2)}) collective-permute-start(f32[8,1024]{1,0:T(8,128)S(1)} %add_add_fusion.8), channel_id=1, source_target_pairs={{0,16},{8,24},{16,0},{24,8},{1,17},{9,25},{17,1},{25,9},{2,18},{10... | collective-permute-start | bytes 98312 | tf_op jit(solution)/shard_map/iterations/ppermute | solution.py:338
  59.9 1.8 collective-permute-done.7
  61.7 1.7 collective-permute-done.8
  63.4 3.7 %collective-permute-start.10 = (f32[8,1024]{1,0:T(8,128)S(1)}, f32[8,1024]{1,0:T(8,128)S(1)}, u32[]{:S(2)}, u32[]{:S(2)}) collective-permute-start(f32[8,1024]{1,0:T(8,128)S(1)} %add_add_fusion.7), channel_id=1, source_target_pairs={{0,64},{32,96},{64,0},{96,32},{1,65},{33,97},{65,1},{97,33},{2,66}... | collective-permute-start | bytes 98312 | tf_op jit(solution)/shard_map/iterations/ppermute | solution.py:338
  67.1 1.0 collective-permute-start.11
  68.1 1.0 collective-permute-start.9
  69.1 1.9 collective-permute-done.11
  71.0 2.2 %collective-permute-done.9 = f32[8,1024]{1,0:T(8,128)S(1)} collective-permute-done((f32[8,1024]{1,0:T(8,128)S(1)}, f32[8,1024]{1,0:T(8,128)S(1)}, u32[]{:S(2)}, u32[]{:S(2)}) %collective-permute-start.9) | collective-permute-done | bytes 32800 | tf_op jit(solution)/shard_map/iterations/ppermute | solution.py:338
  73.2 3.9 %step.2 = f32[8,1024]{1,0:T(8,128)S(1)} custom-call(f32[8,1024]{1,0:T(8,128)S(1)} %add_add_fusion.6.sums_ref, bf16[8,1024,256]{2,1,0:T(8,128)(2,1)S(1)} %get-tuple-element.40.high_ref, bf16[8,1024,256]{2,1,0:T(8,128)(2,1)S(1)} %get-tuple-element.41.mid_ref, f32[1,1024]{1,0:T(1,128)S(1)} %select_n.30.note_ref), custom_call_target="tpu_custom_call" | custom-call | tf_op jit(solution)/shard_map/iterations/step/pallas_call | solution.py:402
  77.2 1.2 collective-permute-done.12
  78.4 1.5 collective-permute-start.14
  79.8 1.8 collective-permute-start.15
  81.6 1.9 collective-permute-done.13
  85.1 3.8 %collective-permute-start.17 = (f32[8,1024]{1,0:T(8,128)S(1)}, f32[8,1024]{1,0:T(8,128)S(1)}, u32[]{:S(2)}, u32[]{:S(2)}) collective-permute-start(f32[8,1024]{1,0:T(8,128)S(1)} %add_add_fusion.5), channel_id=1, source_target_pairs={{0,4},{2,6},{4,0},{6,2},{1,5},{3,7},{5,1},{7,3},{8,12},{10,14},{12... | collective-permute-start | bytes 98312 | tf_op jit(solution)/shard_map/iterations/ppermute | solution.py:338
  89.1 1.0 collective-permute-done.16
  90.1 1.1 collective-permute-done.17
  91.2 1.7 collective-permute-done.18
  93.0 2.7 %collective-permute-start.20 = (f32[8,1024]{1,0:T(8,128)S(1)}, f32[8,1024]{1,0:T(8,128)S(1)}, u32[]{:S(2)}, u32[]{:S(2)}) collective-permute-start(f32[8,1024]{1,0:T(8,128)S(1)} %add_add_fusion.4), channel_id=1, source_target_pairs={{0,16},{8,24},{16,0},{24,8},{1,17},{9,25},{17,1},{25,9},{2,18},{10... | collective-permute-start | bytes 98312 | tf_op jit(solution)/shard_map/iterations/ppermute | solution.py:338
  95.6 1.5 collective-permute-start.21
  97.1 1.0 collective-permute-done.19
  98.5 1.1 collective-permute-done.21
  99.6 3.9 %step.3 = f32[8,1024]{1,0:T(8,128)S(1)} custom-call(f32[8,1024]{1,0:T(8,128)S(1)} %add_add_fusion.3.sums_ref, bf16[8,1024,256]{2,1,0:T(8,128)(2,1)S(1)} %get-tuple-element.40.high_ref, bf16[8,1024,256]{2,1,0:T(8,128)(2,1)S(1)} %get-tuple-element.41.mid_ref, f32[1,1024]{1,0:T(1,128)S(1)} %broadcast_in_dim.39.note_ref), custom_call_target="tpu_custom_call" | custom-call | tf_op jit(solution)/shard_map/iterations/step/pallas_call | solution.py:407
  103.5 1.2 collective-permute-done.22
  104.8 2.7 %collective-permute-start.24 = (f32[8,1024]{1,0:T(8,128)S(1)}, f32[8,1024]{1,0:T(8,128)S(1)}, u32[]{:S(2)}, u32[]{:S(2)}) collective-permute-start(f32[8,1024]{1,0:T(8,128)S(1)} %add.133), channel_id=1, source_target_pairs={{0,4},{2,6},{4,0},{6,2},{1,5},{3,7},{5,1},{7,3},{8,12},{10,14},{12... | collective-permute-start | bytes 98312 | tf_op jit(solution)/shard_map/iterations/ppermute | solution.py:338
  107.5 1.3 collective-permute-start.25
  108.9 1.5 collective-permute-done.23
  110.3 1.1 collective-permute-done.25
  111.5 1.5 collective-permute-start.26
  112.9 2.7 %collective-permute-start.27 = (f32[8,1024]{1,0:T(8,128)S(1)}, f32[8,1024]{1,0:T(8,128)S(1)}, u32[]{:S(2)}, u32[]{:S(2)}) collective-permute-start(f32[8,1024]{1,0:T(8,128)S(1)} %add_add_fusion.2), channel_id=1, source_target_pairs={{0,16},{8,24},{16,0},{24,8},{1,17},{9,25},{17,1},{25,9},{2,18},{10... | collective-permute-start | bytes 98312 | tf_op jit(solution)/shard_map/iterations/ppermute | solution.py:338
  115.7 0.9 collective-permute-done.26
  116.6 1.7 collective-permute-done.27
  118.4 1.2 collective-permute-done.28
  119.6 1.7 collective-permute-start.29
  121.3 2.2 %collective-permute-start.30 = (f32[8,1024]{1,0:T(8,128)S(1)}, f32[8,1024]{1,0:T(8,128)S(1)}, u32[]{:S(2)}, u32[]{:S(2)}) collective-permute-start(f32[8,1024]{1,0:T(8,128)S(1)} %add_add_fusion.1), channel_id=1, source_target_pairs={{0,64},{32,96},{64,0},{96,32},{1,65},{33,97},{65,1},{97,33},{2,66}... | collective-permute-start | bytes 98312 | tf_op jit(solution)/shard_map/iterations/ppermute | solution.py:338
  124.8 2.0 collective-permute-done.30
  127.4 6.3 %clean.1 = (bf16[32,16,16,128]{3,2,1,0:T(8,128)(2,1)}, bf16[2,16,64,128]{3,2,1,0:T(8,128)(2,1)}, bf16[2,16,64,128]{3,2,1,0:T(8,128)(2,1)}, bf16[2,16,64,128]{3,2,1,0:T(8,128)(2,1)}, bf16[2,16,64,128]{3,2,1,0:T(8,128)(2,1)}) custom-call(s32[4]{0:T(128)S(1)} %pad_add_fusion.place_ref, f32[8,1024]{1,0:T(8,128)S(1)} %add_add_fusion.sums_ref, ...), custom_call_target="tpu_custom_call" | custom-call | tf_op jit(solution)/shard_map/cleaned/clean/pallas_call | solution.py:414
  133.7 5.3 %all-to-all-start = ((bf16[32,16,16,128]{3,2,1,0:T(8,128)(2,1)}), bf16[32,16,16,128]{3,2,1,0:T(8,128)(2,1)S(1)}, u32[]{:S(2)}, u32[]{:S(2)}) async-start(bf16[32,16,16,128]{3,2,1,0:T(8,128)(2,1)} %get-tuple-element.50), calls=%async_computation | async-start | bytes 4194304 | tf_op jit(solution)/shard_map/channels/all_to_all | solution.py:430
  139.4 3.0 %collective-permute-start.33 = (bf16[2,16,64,128]{3,2,1,0:T(8,128)(2,1)}, bf16[2,16,64,128]{3,2,1,0:T(8,128)(2,1)S(1)}, u32[]{:S(2)}, u32[]{:S(2)}) collective-permute-start(bf16[2,16,64,128]{3,2,1,0:T(8,128)(2,1)} %get-tuple-element.47), channel_id=1, source_target_pairs={{0,64},{32,96},{64,0},{96,32},{1,65},{33,97},{65,1},{97,33},{2,66}... | collective-permute-start | bytes 1572872 | tf_op jit(solution)/shard_map/channels/ppermute | solution.py:427
  142.4 0.9 collective-permute-start.34
  143.4 11.9 %collective-permute-done.32.refs_1_ = bf16[2,16,64,128]{3,2,1,0:T(8,128)(2,1)S(1)} collective-permute-done((bf16[2,16,64,128]{3,2,1,0:T(8,128)(2,1)}, bf16[2,16,64,128]{3,2,1,0:T(8,128)(2,1)S(1)}, u32[]{:S(2)}, u32[]{:S(2)}) %collective-permute-start.32) | collective-permute-done | bytes 524320 | tf_op jit(solution)/shard_map/channels/ppermute | solution.py:427
  155.4 10.5 %collective-permute-done.33.refs_2_ = bf16[2,16,64,128]{3,2,1,0:T(8,128)(2,1)S(1)} collective-permute-done((bf16[2,16,64,128]{3,2,1,0:T(8,128)(2,1)}, bf16[2,16,64,128]{3,2,1,0:T(8,128)(2,1)S(1)}, u32[]{:S(2)}, u32[]{:S(2)}) %collective-permute-start.33) | collective-permute-done | bytes 524320 | tf_op jit(solution)/shard_map/channels/ppermute | solution.py:427
  168.4 3.7 %ring_bin.1 = (f32[16,16,256]{2,1,0:T(8,128)S(1)}, f32[16,16,256]{2,1,0:T(8,128)S(1)}, f32[16,16,256]{2,1,0:T(8,128)S(1)}, f32[15,16,256]{2,1,0:T(8,128)}, f32[1,16,256]{2,1,0:T(8,128)S(1)}) custom-call(s32[4]{0:T(128)S(1)} %pad_add_fusion.place_ref, s32[1024]{0:T(1024)S(1)} %bitcast.16, bf16[2,16,64,128]{3,2,1,0:T(8,128)(2,1)S(1)} %copy-done.1, ...), custom_call_target="tpu_custom_call" | custom-call | tf_op jit(solution)/shard_map/binning/ring_bin/pallas_call | solution.py:435
  172.1 1.7 collective-permute-start.39
  173.7 2.7 %collective-permute-start.40 = (f32[16,16,256]{2,1,0:T(8,128)S(1)}, f32[16,16,256]{2,1,0:T(8,128)}, u32[]{:S(2)}, u32[]{:S(2)}) collective-permute-start(f32[16,16,256]{2,1,0:T(8,128)S(1)} %get-tuple-element.54), channel_id=1, source_target_pairs={{0,4},{2,6},{4,0},{6,2},{1,5},{3,7},{5,1},{7,3},{8,12},{10,14},{12... | collective-permute-start | bytes 786440 | tf_op jit(solution)/shard_map/tiles/ppermute | solution.py:427
  176.4 1.5 collective-permute-start.41
  177.9 4.3 %flat_bin.1 = f32[16,16,256]{2,1,0:T(8,128)S(1)} custom-call(s32[1024]{0:T(1024)S(1)} %bitcast.17, bf16[32,16,16,128]{3,2,1,0:T(8,128)(2,1)S(1)} %all-to-all-done.arrived_ref), custom_call_target="tpu_custom_call" | custom-call | tf_op jit(solution)/shard_map/binning/flat_bin/pallas_call | solution.py:442
  182.3 5.5 %collective-permute-done.41 = f32[15,16,256]{2,1,0:T(8,128)} collective-permute-done((f32[15,16,256]{2,1,0:T(8,128)}, f32[15,16,256]{2,1,0:T(8,128)}, u32[]{:S(2)}, u32[]{:S(2)}) %collective-permute-start.41) | collective-permute-done | bytes 245792 | tf_op jit(solution)/shard_map/tiles/ppermute | solution.py:427
  188.5 1.3 fusion
  189.8 17.3 %all_to_all.10 = f32[16,32,256]{2,1,0:T(8,128)S(1)} all-to-all(f32[16,32,256]{2,1,0:T(8,128)S(1)} %pad_maximum_fusion), channel_id=1, replica_groups=mesh['z'=4,'x'=4,'y'=4,'c'=2] {'z','x'}, dimensions={0} | all-to-all | bytes 1048576 | tf_op jit(solution)/shard_map/tiles/all_to_all | solution.py:454
  (86 shorter events, 10.2 us)
Async XLA Ops:
  0.0 10.0 %copy-start.6 = (s32[8,2]{0,1:T(2,128)S(1)}, s32[8,2]{0,1:T(2,128)}, u32[]{:S(2)}) copy-start(s32[8,2]{0,1:T(2,128)} %param.10) | copy-start | bytes 196
  0.0 10.2 %copy-start.7 = (s32[8,2]{0,1:T(2,128)S(1)}, s32[8,2]{0,1:T(2,128)}, u32[]{:S(2)}) copy-start(s32[8,2]{0,1:T(2,128)} %param.11) | copy-start | bytes 196
  0.0 10.7 %copy-start.4 = (f32[6,1024]{1,0:T(8,128)S(1)}, f32[6,1024]{1,0:T(8,128)}, u32[]{:S(2)}) copy-start(f32[6,1024]{1,0:T(8,128)} %param.8) | copy-start | bytes 73732
  0.0 10.7 %copy-start.2 = (f32[65]{0:T(128)S(1)}, f32[65]{0:T(128)}, u32[]{:S(2)}) copy-start(f32[65]{0:T(128)} %refs_0_.2) | copy-start | bytes 784
  5.1 26.2 %collective-permute-start = (f32[8,256,128]{2,1,0:T(8,128)}, f32[8,256,128]{2,1,0:T(8,128)S(1)}, u32[]{:S(2)}, u32[]{:S(2)}) collective-permute-start(f32[8,256,128]{2,1,0:T(8,128)} %get-tuple-element.36), channel_id=1, source_target_pairs={{0,8},{8,16},{16,24},{24,32},{32,40},{40,48},{48,56},{56,64},{64,7... | collective-permute-start | bytes 3145736 | tf_op jit(solution)/shard_map/edges/ppermute | solution.py:368
  8.7 26.7 %collective-permute-start.1 = (f32[8,256,128]{2,1,0:T(8,128)}, f32[8,256,128]{2,1,0:T(8,128)S(1)}, u32[]{:S(2)}, u32[]{:S(2)}) collective-permute-start(f32[8,256,128]{2,1,0:T(8,128)} %get-tuple-element.37), channel_id=1, source_target_pairs={{8,0},{16,8},{24,16},{32,24},{40,32},{48,40},{56,48},{64,56},{72,6... | collective-permute-start | bytes 3145736 | tf_op jit(solution)/shard_map/edges/ppermute | solution.py:369
  10.7 3.4 %copy-start = (f32[8,1024,256]{2,1,0:T(8,128)S(1)}, f32[8,1024,256]{2,1,0:T(8,128)}, u32[]{:S(2)}) copy-start(f32[8,1024,256]{2,1,0:T(8,128)} %refs_0_.3) | copy-start | bytes 25165828
  43.1 1.2 collective-permute-start.2
  44.4 5.8 %collective-permute-start.3 = (f32[8,1024]{1,0:T(8,128)S(1)}, f32[8,1024]{1,0:T(8,128)S(1)}, u32[]{:S(2)}, u32[]{:S(2)}) collective-permute-start(f32[8,1024]{1,0:T(8,128)S(1)} %add.113), channel_id=1, source_target_pairs={{0,2},{2,4},{4,6},{6,0},{1,3},{3,5},{5,7},{7,1},{8,10},{10,12},{12... | collective-permute-start | bytes 98312 | tf_op jit(solution)/shard_map/iterations/ppermute | solution.py:338
  46.0 5.4 %collective-permute-start.4 = (f32[8,1024]{1,0:T(8,128)S(1)}, f32[8,1024]{1,0:T(8,128)S(1)}, u32[]{:S(2)}, u32[]{:S(2)}) collective-permute-start(f32[8,1024]{1,0:T(8,128)S(1)} %add.113), channel_id=1, source_target_pairs={{0,4},{2,6},{4,0},{6,2},{1,5},{3,7},{5,1},{7,3},{8,12},{10,14},{12... | collective-permute-start | bytes 98312 | tf_op jit(solution)/shard_map/iterations/ppermute | solution.py:338
  48.9 3.9 %collective-permute-start.5 = (f32[8,1024]{1,0:T(8,128)S(1)}, f32[8,1024]{1,0:T(8,128)S(1)}, u32[]{:S(2)}, u32[]{:S(2)}) collective-permute-start(f32[8,1024]{1,0:T(8,128)S(1)} %add.113), channel_id=1, source_target_pairs={{0,6},{2,0},{4,2},{6,4},{1,7},{3,1},{5,3},{7,5},{8,14},{10,8},{12,... | collective-permute-start | bytes 98312 | tf_op jit(solution)/shard_map/iterations/ppermute | solution.py:338
  52.8 7.1 %collective-permute-start.6 = (f32[8,1024]{1,0:T(8,128)S(1)}, f32[8,1024]{1,0:T(8,128)S(1)}, u32[]{:S(2)}, u32[]{:S(2)}) collective-permute-start(f32[8,1024]{1,0:T(8,128)S(1)} %add_add_fusion.8), channel_id=1, source_target_pairs={{0,8},{8,16},{16,24},{24,0},{1,9},{9,17},{17,25},{25,1},{2,10},{10... | collective-permute-start | bytes 98312 | tf_op jit(solution)/shard_map/iterations/ppermute | solution.py:338
  54.3 7.4 %collective-permute-start.7 = (f32[8,1024]{1,0:T(8,128)S(1)}, f32[8,1024]{1,0:T(8,128)S(1)}, u32[]{:S(2)}, u32[]{:S(2)}) collective-permute-start(f32[8,1024]{1,0:T(8,128)S(1)} %add_add_fusion.8), channel_id=1, source_target_pairs={{0,16},{8,24},{16,0},{24,8},{1,17},{9,25},{17,1},{25,9},{2,18},{10... | collective-permute-start | bytes 98312 | tf_op jit(solution)/shard_map/iterations/ppermute | solution.py:338
  59.5 3.9 %collective-permute-start.8 = (f32[8,1024]{1,0:T(8,128)S(1)}, f32[8,1024]{1,0:T(8,128)S(1)}, u32[]{:S(2)}, u32[]{:S(2)}) collective-permute-start(f32[8,1024]{1,0:T(8,128)S(1)} %add_add_fusion.8), channel_id=1, source_target_pairs={{0,24},{8,0},{16,8},{24,16},{1,25},{9,1},{17,9},{25,17},{2,26},{10... | collective-permute-start | bytes 98312 | tf_op jit(solution)/shard_map/iterations/ppermute | solution.py:338
  63.4 5.7 %collective-permute-start.10 = (f32[8,1024]{1,0:T(8,128)S(1)}, f32[8,1024]{1,0:T(8,128)S(1)}, u32[]{:S(2)}, u32[]{:S(2)}) collective-permute-start(f32[8,1024]{1,0:T(8,128)S(1)} %add_add_fusion.7), channel_id=1, source_target_pairs={{0,64},{32,96},{64,0},{96,32},{1,65},{33,97},{65,1},{97,33},{2,66}... | collective-permute-start | bytes 98312 | tf_op jit(solution)/shard_map/iterations/ppermute | solution.py:338
  67.1 3.9 %collective-permute-start.11 = (f32[8,1024]{1,0:T(8,128)S(1)}, f32[8,1024]{1,0:T(8,128)S(1)}, u32[]{:S(2)}, u32[]{:S(2)}) collective-permute-start(f32[8,1024]{1,0:T(8,128)S(1)} %add_add_fusion.7), channel_id=1, source_target_pairs={{0,96},{32,0},{64,32},{96,64},{1,97},{33,1},{65,33},{97,65},{2,98}... | collective-permute-start | bytes 98312 | tf_op jit(solution)/shard_map/iterations/ppermute | solution.py:338
  68.1 5.1 %collective-permute-start.9 = (f32[8,1024]{1,0:T(8,128)S(1)}, f32[8,1024]{1,0:T(8,128)S(1)}, u32[]{:S(2)}, u32[]{:S(2)}) collective-permute-start(f32[8,1024]{1,0:T(8,128)S(1)} %add_add_fusion.7), channel_id=1, source_target_pairs={{0,32},{32,64},{64,96},{96,0},{1,33},{33,65},{65,97},{97,1},{2,34}... | collective-permute-start | bytes 98312 | tf_op jit(solution)/shard_map/iterations/ppermute | solution.py:338
  77.1 1.2 collective-permute-start.12
  78.4 5.1 %collective-permute-start.13 = (f32[8,1024]{1,0:T(8,128)S(1)}, f32[8,1024]{1,0:T(8,128)S(1)}, u32[]{:S(2)}, u32[]{:S(2)}) collective-permute-start(f32[8,1024]{1,0:T(8,128)S(1)} %add.123), channel_id=1, source_target_pairs={{0,32},{32,64},{64,96},{96,0},{1,33},{33,65},{65,97},{97,1},{2,34}... | collective-permute-start | bytes 98312 | tf_op jit(solution)/shard_map/iterations/ppermute | solution.py:338
  78.4 5.5 %collective-permute-start.14 = (f32[8,1024]{1,0:T(8,128)S(1)}, f32[8,1024]{1,0:T(8,128)S(1)}, u32[]{:S(2)}, u32[]{:S(2)}) collective-permute-start(f32[8,1024]{1,0:T(8,128)S(1)} %add.123), channel_id=1, source_target_pairs={{0,64},{32,96},{64,0},{96,32},{1,65},{33,97},{65,1},{97,33},{2,66}... | collective-permute-start | bytes 98312 | tf_op jit(solution)/shard_map/iterations/ppermute | solution.py:338
  79.8 4.9 %collective-permute-start.15 = (f32[8,1024]{1,0:T(8,128)S(1)}, f32[8,1024]{1,0:T(8,128)S(1)}, u32[]{:S(2)}, u32[]{:S(2)}) collective-permute-start(f32[8,1024]{1,0:T(8,128)S(1)} %add.123), channel_id=1, source_target_pairs={{0,96},{32,0},{64,32},{96,64},{1,97},{33,1},{65,33},{97,65},{2,98}... | collective-permute-start | bytes 98312 | tf_op jit(solution)/shard_map/iterations/ppermute | solution.py:338
  84.7 5.4 %collective-permute-start.16 = (f32[8,1024]{1,0:T(8,128)S(1)}, f32[8,1024]{1,0:T(8,128)S(1)}, u32[]{:S(2)}, u32[]{:S(2)}) collective-permute-start(f32[8,1024]{1,0:T(8,128)S(1)} %add_add_fusion.5), channel_id=1, source_target_pairs={{0,2},{2,4},{4,6},{6,0},{1,3},{3,5},{5,7},{7,1},{8,10},{10,12},{12... | collective-permute-start | bytes 98312 | tf_op jit(solution)/shard_map/iterations/ppermute | solution.py:338
  85.1 6.1 %collective-permute-start.17 = (f32[8,1024]{1,0:T(8,128)S(1)}, f32[8,1024]{1,0:T(8,128)S(1)}, u32[]{:S(2)}, u32[]{:S(2)}) collective-permute-start(f32[8,1024]{1,0:T(8,128)S(1)} %add_add_fusion.5), channel_id=1, source_target_pairs={{0,4},{2,6},{4,0},{6,2},{1,5},{3,7},{5,1},{7,3},{8,12},{10,14},{12... | collective-permute-start | bytes 98312 | tf_op jit(solution)/shard_map/iterations/ppermute | solution.py:338
  89.0 3.9 %collective-permute-start.18 = (f32[8,1024]{1,0:T(8,128)S(1)}, f32[8,1024]{1,0:T(8,128)S(1)}, u32[]{:S(2)}, u32[]{:S(2)}) collective-permute-start(f32[8,1024]{1,0:T(8,128)S(1)} %add_add_fusion.5), channel_id=1, source_target_pairs={{0,6},{2,0},{4,2},{6,4},{1,7},{3,1},{5,3},{7,5},{8,14},{10,8},{12,... | collective-permute-start | bytes 98312 | tf_op jit(solution)/shard_map/iterations/ppermute | solution.py:338
  92.9 5.2 %collective-permute-start.19 = (f32[8,1024]{1,0:T(8,128)S(1)}, f32[8,1024]{1,0:T(8,128)S(1)}, u32[]{:S(2)}, u32[]{:S(2)}) collective-permute-start(f32[8,1024]{1,0:T(8,128)S(1)} %add_add_fusion.4), channel_id=1, source_target_pairs={{0,8},{8,16},{16,24},{24,0},{1,9},{9,17},{17,25},{25,1},{2,10},{10... | collective-permute-start | bytes 98312 | tf_op jit(solution)/shard_map/iterations/ppermute | solution.py:338
  93.0 5.5 %collective-permute-start.20 = (f32[8,1024]{1,0:T(8,128)S(1)}, f32[8,1024]{1,0:T(8,128)S(1)}, u32[]{:S(2)}, u32[]{:S(2)}) collective-permute-start(f32[8,1024]{1,0:T(8,128)S(1)} %add_add_fusion.4), channel_id=1, source_target_pairs={{0,16},{8,24},{16,0},{24,8},{1,17},{9,25},{17,1},{25,9},{2,18},{10... | collective-permute-start | bytes 98312 | tf_op jit(solution)/shard_map/iterations/ppermute | solution.py:338
  95.6 3.9 %collective-permute-start.21 = (f32[8,1024]{1,0:T(8,128)S(1)}, f32[8,1024]{1,0:T(8,128)S(1)}, u32[]{:S(2)}, u32[]{:S(2)}) collective-permute-start(f32[8,1024]{1,0:T(8,128)S(1)} %add_add_fusion.4), channel_id=1, source_target_pairs={{0,24},{8,0},{16,8},{24,16},{1,25},{9,1},{17,9},{25,17},{2,26},{10... | collective-permute-start | bytes 98312 | tf_op jit(solution)/shard_map/iterations/ppermute | solution.py:338
  99.6 24.5 %copy-start.5 = (f32[8,256]{1,0:T(8,128)S(1)}, f32[8,256]{1,0:T(8,128)}, u32[]{:S(2)}) copy-start(f32[8,256]{1,0:T(8,128)} %param.9) | copy-start | bytes 24580
  103.5 1.2 collective-permute-start.22
  104.7 5.6 %collective-permute-start.23 = (f32[8,1024]{1,0:T(8,128)S(1)}, f32[8,1024]{1,0:T(8,128)S(1)}, u32[]{:S(2)}, u32[]{:S(2)}) collective-permute-start(f32[8,1024]{1,0:T(8,128)S(1)} %add.133), channel_id=1, source_target_pairs={{0,2},{2,4},{4,6},{6,0},{1,3},{3,5},{5,7},{7,1},{8,10},{10,12},{12... | collective-permute-start | bytes 98312 | tf_op jit(solution)/shard_map/iterations/ppermute | solution.py:338
  104.8 5.5 %collective-permute-start.24 = (f32[8,1024]{1,0:T(8,128)S(1)}, f32[8,1024]{1,0:T(8,128)S(1)}, u32[]{:S(2)}, u32[]{:S(2)}) collective-permute-start(f32[8,1024]{1,0:T(8,128)S(1)} %add.133), channel_id=1, source_target_pairs={{0,4},{2,6},{4,0},{6,2},{1,5},{3,7},{5,1},{7,3},{8,12},{10,14},{12... | collective-permute-start | bytes 98312 | tf_op jit(solution)/shard_map/iterations/ppermute | solution.py:338
  107.5 3.9 %collective-permute-start.25 = (f32[8,1024]{1,0:T(8,128)S(1)}, f32[8,1024]{1,0:T(8,128)S(1)}, u32[]{:S(2)}, u32[]{:S(2)}) collective-permute-start(f32[8,1024]{1,0:T(8,128)S(1)} %add.133), channel_id=1, source_target_pairs={{0,6},{2,0},{4,2},{6,4},{1,7},{3,1},{5,3},{7,5},{8,14},{10,8},{12,... | collective-permute-start | bytes 98312 | tf_op jit(solution)/shard_map/iterations/ppermute | solution.py:338
  111.5 5.2 %collective-permute-start.26 = (f32[8,1024]{1,0:T(8,128)S(1)}, f32[8,1024]{1,0:T(8,128)S(1)}, u32[]{:S(2)}, u32[]{:S(2)}) collective-permute-start(f32[8,1024]{1,0:T(8,128)S(1)} %add_add_fusion.2), channel_id=1, source_target_pairs={{0,8},{8,16},{16,24},{24,0},{1,9},{9,17},{17,25},{25,1},{2,10},{10... | collective-permute-start | bytes 98312 | tf_op jit(solution)/shard_map/iterations/ppermute | solution.py:338
  112.9 5.4 %collective-permute-start.27 = (f32[8,1024]{1,0:T(8,128)S(1)}, f32[8,1024]{1,0:T(8,128)S(1)}, u32[]{:S(2)}, u32[]{:S(2)}) collective-permute-start(f32[8,1024]{1,0:T(8,128)S(1)} %add_add_fusion.2), channel_id=1, source_target_pairs={{0,16},{8,24},{16,0},{24,8},{1,17},{9,25},{17,1},{25,9},{2,18},{10... | collective-permute-start | bytes 98312 | tf_op jit(solution)/shard_map/iterations/ppermute | solution.py:338
  115.7 3.9 %collective-permute-start.28 = (f32[8,1024]{1,0:T(8,128)S(1)}, f32[8,1024]{1,0:T(8,128)S(1)}, u32[]{:S(2)}, u32[]{:S(2)}) collective-permute-start(f32[8,1024]{1,0:T(8,128)S(1)} %add_add_fusion.2), channel_id=1, source_target_pairs={{0,24},{8,0},{16,8},{24,16},{1,25},{9,1},{17,9},{25,17},{2,26},{10... | collective-permute-start | bytes 98312 | tf_op jit(solution)/shard_map/iterations/ppermute | solution.py:338
  119.6 5.2 %collective-permute-start.29 = (f32[8,1024]{1,0:T(8,128)S(1)}, f32[8,1024]{1,0:T(8,128)S(1)}, u32[]{:S(2)}, u32[]{:S(2)}) collective-permute-start(f32[8,1024]{1,0:T(8,128)S(1)} %add_add_fusion.1), channel_id=1, source_target_pairs={{0,32},{32,64},{64,96},{96,0},{1,33},{33,65},{65,97},{97,1},{2,34}... | collective-permute-start | bytes 98312 | tf_op jit(solution)/shard_map/iterations/ppermute | solution.py:338
  121.3 5.4 %collective-permute-start.30 = (f32[8,1024]{1,0:T(8,128)S(1)}, f32[8,1024]{1,0:T(8,128)S(1)}, u32[]{:S(2)}, u32[]{:S(2)}) collective-permute-start(f32[8,1024]{1,0:T(8,128)S(1)} %add_add_fusion.1), channel_id=1, source_target_pairs={{0,64},{32,96},{64,0},{96,32},{1,65},{33,97},{65,1},{97,33},{2,66}... | collective-permute-start | bytes 98312 | tf_op jit(solution)/shard_map/iterations/ppermute | solution.py:338
  123.5 3.9 %collective-permute-start.31 = (f32[8,1024]{1,0:T(8,128)S(1)}, f32[8,1024]{1,0:T(8,128)S(1)}, u32[]{:S(2)}, u32[]{:S(2)}) collective-permute-start(f32[8,1024]{1,0:T(8,128)S(1)} %add_add_fusion.1), channel_id=1, source_target_pairs={{0,96},{32,0},{64,32},{96,64},{1,97},{33,1},{65,33},{97,65},{2,98}... | collective-permute-start | bytes 98312 | tf_op jit(solution)/shard_map/iterations/ppermute | solution.py:338
  133.7 8.7 %copy-start.8 = (bf16[2,16,64,128]{3,2,1,0:T(8,128)(2,1)S(1)}, bf16[2,16,64,128]{3,2,1,0:T(8,128)(2,1)}, u32[]{:S(2)}) copy-start(bf16[2,16,64,128]{3,2,1,0:T(8,128)(2,1)} %get-tuple-element.48) | copy-start | bytes 1572868
  133.7 9.6 %copy-start.1 = (bf16[2,16,64,128]{3,2,1,0:T(8,128)(2,1)S(1)}, bf16[2,16,64,128]{3,2,1,0:T(8,128)(2,1)}, u32[]{:S(2)}) copy-start(bf16[2,16,64,128]{3,2,1,0:T(8,128)(2,1)} %get-tuple-element.45.refs_0_) | copy-start | bytes 1572868
  133.7 44.2 %all-to-all-start = ((bf16[32,16,16,128]{3,2,1,0:T(8,128)(2,1)}), bf16[32,16,16,128]{3,2,1,0:T(8,128)(2,1)S(1)}, u32[]{:S(2)}, u32[]{:S(2)}) async-start(bf16[32,16,16,128]{3,2,1,0:T(8,128)(2,1)} %get-tuple-element.50), calls=%async_computation | async-start | bytes 4194304 | tf_op jit(solution)/shard_map/channels/all_to_all | solution.py:430
  139.1 16.2 %collective-permute-start.32 = (bf16[2,16,64,128]{3,2,1,0:T(8,128)(2,1)}, bf16[2,16,64,128]{3,2,1,0:T(8,128)(2,1)S(1)}, u32[]{:S(2)}, u32[]{:S(2)}) collective-permute-start(bf16[2,16,64,128]{3,2,1,0:T(8,128)(2,1)} %get-tuple-element.46), channel_id=1, source_target_pairs={{0,32},{32,64},{64,96},{96,0},{1,33},{33,65},{65,97},{97,1},{2,34}... | collective-permute-start | bytes 1572872 | tf_op jit(solution)/shard_map/channels/ppermute | solution.py:427
  139.4 26.5 %collective-permute-start.33 = (bf16[2,16,64,128]{3,2,1,0:T(8,128)(2,1)}, bf16[2,16,64,128]{3,2,1,0:T(8,128)(2,1)S(1)}, u32[]{:S(2)}, u32[]{:S(2)}) collective-permute-start(bf16[2,16,64,128]{3,2,1,0:T(8,128)(2,1)} %get-tuple-element.47), channel_id=1, source_target_pairs={{0,64},{32,96},{64,0},{96,32},{1,65},{33,97},{65,1},{97,33},{2,66}... | collective-permute-start | bytes 1572872 | tf_op jit(solution)/shard_map/channels/ppermute | solution.py:427
  142.4 24.1 %collective-permute-start.34 = (bf16[2,16,64,128]{3,2,1,0:T(8,128)(2,1)S(1)}, bf16[2,16,64,128]{3,2,1,0:T(8,128)(2,1)S(1)}, u32[]{:S(2)}, u32[]{:S(2)}) collective-permute-start(bf16[2,16,64,128]{3,2,1,0:T(8,128)(2,1)S(1)} %copy-done.8), channel_id=1, source_target_pairs={{0,96},{32,0},{64,32},{96,64},{1,97},{33,1},{65,33},{97,65},{2,98}... | collective-permute-start | bytes 1572872 | tf_op jit(solution)/shard_map/channels/ppermute | solution.py:427
  143.3 23.6 %collective-permute-start.35 = (bf16[16,64,128]{2,1,0:T(8,128)(2,1)S(1)}, bf16[16,64,128]{2,1,0:T(8,128)(2,1)S(1)}, u32[]{:S(2)}, u32[]{:S(2)}) collective-permute-start(bf16[16,64,128]{2,1,0:T(8,128)(2,1)S(1)} %slice_bitcast_fusion.3), channel_id=1, source_target_pairs={{0,1},{1,0},{2,3},{3,2},{4,5},{5,4},{6,7},{7,6},{8,9},{9,8},{10,11... | collective-permute-start | bytes 786440 | tf_op jit(solution)/shard_map/channels/ppermute | solution.py:432
  155.3 11.6 %collective-permute-start.36 = (bf16[16,64,128]{2,1,0:T(8,128)(2,1)S(1)}, bf16[16,64,128]{2,1,0:T(8,128)(2,1)S(1)}, u32[]{:S(2)}, u32[]{:S(2)}) collective-permute-start(bf16[16,64,128]{2,1,0:T(8,128)(2,1)S(1)} %slice_bitcast_fusion.2), channel_id=1, source_target_pairs={{0,1},{1,0},{2,3},{3,2},{4,5},{5,4},{6,7},{7,6},{8,9},{9,8},{10,11... | collective-permute-start | bytes 786440 | tf_op jit(solution)/shard_map/channels/ppermute | solution.py:432
  165.9 1.6 collective-permute-start.37
  166.5 1.8 collective-permute-start.38
  172.1 15.7 %collective-permute-start.39 = (f32[16,16,256]{2,1,0:T(8,128)S(1)}, f32[16,16,256]{2,1,0:T(8,128)S(1)}, u32[]{:S(2)}, u32[]{:S(2)}) collective-permute-start(f32[16,16,256]{2,1,0:T(8,128)S(1)} %get-tuple-element.53), channel_id=1, source_target_pairs={{0,2},{2,4},{4,6},{6,0},{1,3},{3,5},{5,7},{7,1},{8,10},{10,12},{12... | collective-permute-start | bytes 786440 | tf_op jit(solution)/shard_map/tiles/ppermute | solution.py:427
  173.7 14.7 %collective-permute-start.40 = (f32[16,16,256]{2,1,0:T(8,128)S(1)}, f32[16,16,256]{2,1,0:T(8,128)}, u32[]{:S(2)}, u32[]{:S(2)}) collective-permute-start(f32[16,16,256]{2,1,0:T(8,128)S(1)} %get-tuple-element.54), channel_id=1, source_target_pairs={{0,4},{2,6},{4,0},{6,2},{1,5},{3,7},{5,1},{7,3},{8,12},{10,14},{12... | collective-permute-start | bytes 786440 | tf_op jit(solution)/shard_map/tiles/ppermute | solution.py:427
  176.4 11.4 %collective-permute-start.41 = (f32[15,16,256]{2,1,0:T(8,128)}, f32[15,16,256]{2,1,0:T(8,128)}, u32[]{:S(2)}, u32[]{:S(2)}) collective-permute-start(f32[15,16,256]{2,1,0:T(8,128)} %get-tuple-element.55), channel_id=1, source_target_pairs={{0,6},{2,0},{4,2},{6,4},{1,7},{3,1},{5,3},{7,5},{8,14},{10,8},{12,... | collective-permute-start | bytes 737288 | tf_op jit(solution)/shard_map/tiles/ppermute | solution.py:427
  182.2 6.3 %collective-permute-start.42 = (f32[1,16,256]{2,1,0:T(8,128)S(1)}, f32[1,16,256]{2,1,0:T(8,128)S(1)}, u32[]{:S(2)}, u32[]{:S(2)}) collective-permute-start(f32[1,16,256]{2,1,0:T(8,128)S(1)} %get-tuple-element.56), channel_id=1, source_target_pairs={{0,6},{2,0},{4,2},{6,4},{1,7},{3,1},{5,3},{7,5},{8,14},{10,8},{12,... | collective-permute-start | bytes 49160 | tf_op jit(solution)/shard_map/tiles/ppermute | solution.py:427
  187.8 0.7 copy-start.3

commit v6 on v5

--- a/solution.py
+++ b/solution.py
@@ -105,7 +105,6 @@
 
 def own_kernel(reach, taps_ref, modes_ref, tod_ref, basis_ref, fix_ref, own_ref, band):
     dishes, chans, tdev = tod_ref.shape
-    groups = BLOCK // reach
     part = 64
     source = lax.broadcasted_iota(jnp.int32, (part, tdev), 0)
     target = lax.broadcasted_iota(jnp.int32, (part, tdev), 1)
@@ -113,15 +112,15 @@
         pieces = split(taps_at(taps_ref, source + (start + reach) - target), 2)
         band[0, start:start + part] = pieces[0]
         band[1, start:start + part] = pieces[1]
-    source = lax.broadcasted_iota(jnp.int32, (reach, tdev), 0)
-    target = lax.broadcasted_iota(jnp.int32, (reach, tdev), 1)
-    fix_ref[...] = jnp.zeros_like(fix_ref)
-    for side, shift in ((0, 0), (1, tdev + reach)):
-        pieces = split(taps_at(taps_ref, source + shift - target), 2)
-        for group in range(groups):
-            rows = pl.ds(side * BLOCK + group * reach, reach)
-            fix_ref[0, group, rows, :] = pieces[0]
-            fix_ref[1, group, rows, :] = pieces[1]
+    span = 2 * BLOCK
+    target = lax.broadcasted_iota(jnp.int32, (part, span), 1)
+    for start in range(0, span, part):
+        source = lax.broadcasted_iota(jnp.int32, (part, span), 0) + start
+        lag = jnp.where(source < BLOCK, 0, 2 * reach) + source % reach - target % reach
+        lag = jnp.where(source // reach == target // reach, lag, -1)
+        pieces = split(taps_at(taps_ref, lag), 2)
+        fix_ref[0, start:start + part] = pieces[0]
+        fix_ref[1, start:start + part] = pieces[1]
     basis_ref[...] = orth(modes_ref[...])
     size = 256
 
@@ -152,26 +151,33 @@
     return folded(total, 2)
 
 
-def edge_kernel(basis_ref, fix_ref, own_ref, left_ref, right_ref, pointing_ref,
+def edge_kernel(reach, basis_ref, fix_ref, own_ref, left_ref, right_ref, pointing_ref,
                 high_ref, mid_ref, low_ref, total_ref):
     dishes, chans, tdev = own_ref.shape
-    groups = fix_ref.shape[1]
+    groups = BLOCK // reach
     size = chans // groups
     several = 4
+    lane = lax.broadcasted_iota(jnp.int32, (several * size, BLOCK), 1)
 
     def body(index, carry):
         some = pl.ds(index * several, several)
         edges = jnp.concatenate([left_ref[some], right_ref[some]], axis=2)
-        high, low = split(edges.reshape(several * size, tdev), 2)
+        high, low = split(edges.reshape(several * size, 2 * BLOCK), 2)
+        lowpass = mxu(high, fix_ref[0]) + (mxu(high, fix_ref[1]) + mxu(low, fix_ref[0]))
         for group in range(groups):
             rows = pl.ds(group * size, size)
-            lowpass = mxu(high, fix_ref[0, group]) + (
-                mxu(high, fix_ref[1, group]) + mxu(low, fix_ref[0, group])
-            )
-            pieces = split(own_ref[some, rows, :] - lowpass.reshape(several, size, tdev), 3)
-            high_ref[some, rows, :] = pieces[0]
-            mid_ref[some, rows, :] = pieces[1]
-            low_ref[some, rows, :] = pieces[2]
+            for side in range(2):
+                columns = slice(side * (tdev - BLOCK), side * (tdev - BLOCK) + BLOCK)
+                term = lowpass[:, side * BLOCK:(side + 1) * BLOCK]
+                move = (side * (BLOCK - reach) - group * reach) % BLOCK
+                if move:
+                    term = pltpu.roll(term, move, 1)
+                edge = lane >= BLOCK - reach if side else lane < reach
+                term = jnp.where(edge, term, 0.0).reshape(several, size, BLOCK)
+                pieces = split(own_ref[some, rows, columns] - term, 3)
+                high_ref[some, rows, columns] = pieces[0]
+                mid_ref[some, rows, columns] = pieces[1]
+                low_ref[some, rows, columns] = pieces[2]
         return carry
 
     lax.fori_loop(0, dishes // several, body, 0)
@@ -372,7 +378,7 @@
         modes = jnp.pad(modes_init, ((0, ROWS - MODES), (0, 0)))
         basis, fix, own = call(
             lambda *refs: own_kernel(reach, *refs), "own",
-            [rows_f32, jax.ShapeDtypeStruct((2, groups, tdev, tdev), BF16),
+            [rows_f32, jax.ShapeDtypeStruct((2, 2 * BLOCK, 2 * BLOCK), BF16),
              pltpu.VMEM((dishes, chans, tdev), F32)],
             [SMEM, VMEM, VMEM],
             [pltpu.VMEM((2, tdev, tdev), BF16)],
@@ -392,7 +398,7 @@
             (note, ring_note, jnp.zeros_like(note), place, own)
         )
         high, mid, low, sums = call(
-            edge_kernel, "edge", [piece, piece, piece, rows_f32], [VMEM] * 6
+            lambda *refs: edge_kernel(reach, *refs), "edge", [piece, piece, piece, rows_f32], [VMEM] * 6
         )(basis, fix, own, from_left, from_right, note)
 
     with jax.named_scope("iterations"):

time: 209 us -> 208 us (level)
  no operation moved by 1% of the time
where the time goes in v6:
time: 208 us; the launch traced here: 207 us
  waiting for transfers between devices  76.3 us (37%)
  starting transfers between devices  63.9 us (31%)
  Pallas kernels  42.7 us (21%)
  blocking collectives  17.3 us (8%)
  local copies, waits for them, and re-layouts  4.04 us (2%)
  other arithmetic  2.35 us (1%)
    ppermute x30, starting transfers between devices, total_over(): lax.ppermute(value, axis, [(i, (i + s) % count) for i in range(count)])  43 us
    ppermute x30, waiting for transfers between devices, total_over(): lax.ppermute(value, axis, [(i, (i + s) % count) for i in range(count)])  33.2 us
    ppermute x7, waiting for transfers between devices, along(): lax.ppermute(value, axis, [(i, (i + shift) % CHIPS) for i in range(CHIPS)])  29.1 us
    all_to_all x1, blocking collectives, shards(): lax.all_to_all(jnp.concatenate([sky, rows], axis=1), ('z', 'x'), 0, 0, ti...  17.3 us
    ppermute x7, starting transfers between devices, along(): lax.ppermute(value, axis, [(i, (i + shift) % CHIPS) for i in range(CHIPS)])  10.1 us
    pallas_call x1, Pallas kernels, shards(): call(lambda *refs: own_kernel(reach, *refs), 'own', [rows_f32, jax.ShapeD...  8.65 us
    ppermute x1, waiting for transfers between devices, shards(): lax.ppermute(tail, ('z', 'x'), [(i, i + 1) for i in range(ends)])  8.52 us
    pallas_call x1, Pallas kernels, shards(): call(lambda *refs: edge_kernel(reach, *refs), 'edge', [piece, piece, piec...  6.94 us
  transfers between devices with their start and end apart: 44, of which 36 were waited for; matrix products, arithmetic and copies ran while one was open for 0% of the time, Pallas kernels for 8%

profile of v6, /device:TPU:0, one launch (start us, length us, event | category | flops | bytes accessed | tf_op | source)
XLA Modules:
  0.0 207.0 jit_solution(2566456903427032830)
XLA Ops:
  0.0 5.1 %pack.1 = (f32[8,256,128]{2,1,0:T(8,128)}, f32[8,256,128]{2,1,0:T(8,128)}) custom-call(f32[8,1024,256]{2,1,0:T(8,128)} %refs_0_.3), custom_call_target="tpu_custom_call" | custom-call | tf_op jit(solution)/shard_map/edges/pack/pallas_call | solution.py:369
  5.1 3.6 %collective-permute-start = (f32[8,256,128]{2,1,0:T(8,128)}, f32[8,256,128]{2,1,0:T(8,128)S(1)}, u32[]{:S(2)}, u32[]{:S(2)}) collective-permute-start(f32[8,256,128]{2,1,0:T(8,128)} %get-tuple-element.36), channel_id=1, source_target_pairs={{0,8},{8,16},{16,24},{24,32},{32,40},{40,48},{48,56},{56,64},{64,7... | collective-permute-start | bytes 3145736 | tf_op jit(solution)/shard_map/edges/ppermute | solution.py:374
  8.7 1.3 collective-permute-start.1
  10.7 3.4 %copy-done = f32[8,1024,256]{2,1,0:T(8,128)S(1)} copy-done((f32[8,1024,256]{2,1,0:T(8,128)S(1)}, f32[8,1024,256]{2,1,0:T(8,128)}, u32[]{:S(2)}) %copy-start) | copy-done | bytes 8388632
  14.1 8.6 %own.1 = (f32[8,1024]{1,0:T(8,128)S(1)}, bf16[2,256,256]{2,1,0:T(8,128)(2,1)S(1)}, f32[8,1024,256]{2,1,0:T(8,128)S(1)}) custom-call(f32[65]{0:T(128)S(1)} %copy-done.2, f32[8,1024]{1,0:T(8,128)S(1)} %pad.4.refs_1_, f32[8,1024,256]{2,1,0:T(8,128)S(1)} %copy-done), custom_call_target="tpu_custom_call" | custom-call | tf_op jit(solution)/shard_map/own/own/pallas_call | solution.py:379
  22.8 8.5 %collective-permute-done.refs_3_ = f32[8,256,128]{2,1,0:T(8,128)S(1)} collective-permute-done((f32[8,256,128]{2,1,0:T(8,128)}, f32[8,256,128]{2,1,0:T(8,128)S(1)}, u32[]{:S(2)}, u32[]{:S(2)}) %collective-permute-start) | collective-permute-done | bytes 1048608 | tf_op jit(solution)/shard_map/edges/ppermute | solution.py:374
  31.3 4.1 %collective-permute-done.1.refs_4_ = f32[8,256,128]{2,1,0:T(8,128)S(1)} collective-permute-done((f32[8,256,128]{2,1,0:T(8,128)}, f32[8,256,128]{2,1,0:T(8,128)S(1)}, u32[]{:S(2)}, u32[]{:S(2)}) %collective-permute-start.1) | collective-permute-done | bytes 1048608 | tf_op jit(solution)/shard_map/edges/ppermute | solution.py:375
  35.4 6.9 %edge.1 = (bf16[8,1024,256]{2,1,0:T(8,128)(2,1)S(1)}, bf16[8,1024,256]{2,1,0:T(8,128)(2,1)S(1)}, bf16[8,1024,256]{2,1,0:T(8,128)(2,1)S(1)}, f32[8,1024]{1,0:T(8,128)S(1)}) custom-call(f32[8,1024]{1,0:T(8,128)S(1)} %get-tuple-element.33.refs_0_, bf16[2,256,256]{2,1,0:T(8,128)(2,1)S(1)} %get-tuple-element.34.refs_1_, ...), custom_call_target="tpu_custom_call" | custom-call | tf_op jit(solution)/shard_map/filtered/edge/pallas_call | solution.py:400
  42.4 1.2 collective-permute-done.2
  43.6 1.6 collective-permute-start.3
  45.2 2.9 %collective-permute-start.4 = (f32[8,1024]{1,0:T(8,128)S(1)}, f32[8,1024]{1,0:T(8,128)S(1)}, u32[]{:S(2)}, u32[]{:S(2)}) collective-permute-start(f32[8,1024]{1,0:T(8,128)S(1)} %add.113), channel_id=1, source_target_pairs={{0,4},{2,6},{4,0},{6,2},{1,5},{3,7},{5,1},{7,3},{8,12},{10,14},{12... | collective-permute-start | bytes 98312 | tf_op jit(solution)/shard_map/iterations/ppermute | solution.py:344
  48.1 1.3 collective-permute-start.5
  49.4 1.2 collective-permute-done.4
  50.6 1.4 collective-permute-done.5
  52.0 1.5 collective-permute-start.6
  53.5 5.2 %collective-permute-start.7 = (f32[8,1024]{1,0:T(8,128)S(1)}, f32[8,1024]{1,0:T(8,128)S(1)}, u32[]{:S(2)}, u32[]{:S(2)}) collective-permute-start(f32[8,1024]{1,0:T(8,128)S(1)} %add_add_fusion.8), channel_id=1, source_target_pairs={{0,16},{8,24},{16,0},{24,8},{1,17},{9,25},{17,1},{25,9},{2,18},{10... | collective-permute-start | bytes 98312 | tf_op jit(solution)/shard_map/iterations/ppermute | solution.py:344
  59.1 1.8 collective-permute-done.7
  60.9 1.7 collective-permute-done.8
  62.6 3.7 %collective-permute-start.10 = (f32[8,1024]{1,0:T(8,128)S(1)}, f32[8,1024]{1,0:T(8,128)S(1)}, u32[]{:S(2)}, u32[]{:S(2)}) collective-permute-start(f32[8,1024]{1,0:T(8,128)S(1)} %add_add_fusion.7), channel_id=1, source_target_pairs={{0,64},{32,96},{64,0},{96,32},{1,65},{33,97},{65,1},{97,33},{2,66}... | collective-permute-start | bytes 98312 | tf_op jit(solution)/shard_map/iterations/ppermute | solution.py:344
  66.3 1.0 collective-permute-start.11
  67.3 1.0 collective-permute-start.9
  68.3 1.9 collective-permute-done.11
  70.2 2.2 %collective-permute-done.9 = f32[8,1024]{1,0:T(8,128)S(1)} collective-permute-done((f32[8,1024]{1,0:T(8,128)S(1)}, f32[8,1024]{1,0:T(8,128)S(1)}, u32[]{:S(2)}, u32[]{:S(2)}) %collective-permute-start.9) | collective-permute-done | bytes 32800 | tf_op jit(solution)/shard_map/iterations/ppermute | solution.py:344
  72.4 3.9 %step.2 = f32[8,1024]{1,0:T(8,128)S(1)} custom-call(f32[8,1024]{1,0:T(8,128)S(1)} %add_add_fusion.6.sums_ref, bf16[8,1024,256]{2,1,0:T(8,128)(2,1)S(1)} %get-tuple-element.40.high_ref, bf16[8,1024,256]{2,1,0:T(8,128)(2,1)S(1)} %get-tuple-element.41.mid_ref, f32[1,1024]{1,0:T(1,128)S(1)} %select_n.30.note_ref), custom_call_target="tpu_custom_call" | custom-call | tf_op jit(solution)/shard_map/iterations/step/pallas_call | solution.py:408
  76.4 1.2 collective-permute-done.12
  77.6 1.5 collective-permute-start.14
  79.0 1.8 collective-permute-start.15
  80.8 1.9 collective-permute-done.13
  83.1 0.8 collective-permute-done.15
  84.3 3.8 %collective-permute-start.17 = (f32[8,1024]{1,0:T(8,128)S(1)}, f32[8,1024]{1,0:T(8,128)S(1)}, u32[]{:S(2)}, u32[]{:S(2)}) collective-permute-start(f32[8,1024]{1,0:T(8,128)S(1)} %add_add_fusion.5), channel_id=1, source_target_pairs={{0,4},{2,6},{4,0},{6,2},{1,5},{3,7},{5,1},{7,3},{8,12},{10,14},{12... | collective-permute-start | bytes 98312 | tf_op jit(solution)/shard_map/iterations/ppermute | solution.py:344
  88.3 1.0 collective-permute-done.16
  89.3 1.1 collective-permute-done.17
  90.4 1.7 collective-permute-done.18
  92.2 2.7 %collective-permute-start.20 = (f32[8,1024]{1,0:T(8,128)S(1)}, f32[8,1024]{1,0:T(8,128)S(1)}, u32[]{:S(2)}, u32[]{:S(2)}) collective-permute-start(f32[8,1024]{1,0:T(8,128)S(1)} %add_add_fusion.4), channel_id=1, source_target_pairs={{0,16},{8,24},{16,0},{24,8},{1,17},{9,25},{17,1},{25,9},{2,18},{10... | collective-permute-start | bytes 98312 | tf_op jit(solution)/shard_map/iterations/ppermute | solution.py:344
  94.8 1.5 collective-permute-start.21
  96.3 1.0 collective-permute-done.19
  97.7 1.1 collective-permute-done.21
  98.8 3.9 %step.3 = f32[8,1024]{1,0:T(8,128)S(1)} custom-call(f32[8,1024]{1,0:T(8,128)S(1)} %add_add_fusion.3.sums_ref, bf16[8,1024,256]{2,1,0:T(8,128)(2,1)S(1)} %get-tuple-element.40.high_ref, bf16[8,1024,256]{2,1,0:T(8,128)(2,1)S(1)} %get-tuple-element.41.mid_ref, f32[1,1024]{1,0:T(1,128)S(1)} %broadcast_in_dim.39.note_ref), custom_call_target="tpu_custom_call" | custom-call | tf_op jit(solution)/shard_map/iterations/step/pallas_call | solution.py:413
  102.7 1.2 collective-permute-done.22
  104.0 2.7 %collective-permute-start.24 = (f32[8,1024]{1,0:T(8,128)S(1)}, f32[8,1024]{1,0:T(8,128)S(1)}, u32[]{:S(2)}, u32[]{:S(2)}) collective-permute-start(f32[8,1024]{1,0:T(8,128)S(1)} %add.133), channel_id=1, source_target_pairs={{0,4},{2,6},{4,0},{6,2},{1,5},{3,7},{5,1},{7,3},{8,12},{10,14},{12... | collective-permute-start | bytes 98312 | tf_op jit(solution)/shard_map/iterations/ppermute | solution.py:344
  106.7 1.3 collective-permute-start.25
  108.1 1.5 collective-permute-done.23
  109.6 1.1 collective-permute-done.25
  110.7 1.5 collective-permute-start.26
  112.1 2.7 %collective-permute-start.27 = (f32[8,1024]{1,0:T(8,128)S(1)}, f32[8,1024]{1,0:T(8,128)S(1)}, u32[]{:S(2)}, u32[]{:S(2)}) collective-permute-start(f32[8,1024]{1,0:T(8,128)S(1)} %add_add_fusion.2), channel_id=1, source_target_pairs={{0,16},{8,24},{16,0},{24,8},{1,17},{9,25},{17,1},{25,9},{2,18},{10... | collective-permute-start | bytes 98312 | tf_op jit(solution)/shard_map/iterations/ppermute | solution.py:344
  114.9 0.9 collective-permute-done.26
  115.8 1.7 collective-permute-done.27
  117.6 1.2 collective-permute-done.28
  118.8 1.7 collective-permute-start.29
  120.5 2.2 %collective-permute-start.30 = (f32[8,1024]{1,0:T(8,128)S(1)}, f32[8,1024]{1,0:T(8,128)S(1)}, u32[]{:S(2)}, u32[]{:S(2)}) collective-permute-start(f32[8,1024]{1,0:T(8,128)S(1)} %add_add_fusion.1), channel_id=1, source_target_pairs={{0,64},{32,96},{64,0},{96,32},{1,65},{33,97},{65,1},{97,33},{2,66}... | collective-permute-start | bytes 98312 | tf_op jit(solution)/shard_map/iterations/ppermute | solution.py:344
  124.0 2.0 collective-permute-done.30
  126.6 6.3 %clean.1 = (bf16[32,16,16,128]{3,2,1,0:T(8,128)(2,1)}, bf16[2,16,64,128]{3,2,1,0:T(8,128)(2,1)}, bf16[2,16,64,128]{3,2,1,0:T(8,128)(2,1)}, bf16[2,16,64,128]{3,2,1,0:T(8,128)(2,1)}, bf16[2,16,64,128]{3,2,1,0:T(8,128)(2,1)}) custom-call(s32[4]{0:T(128)S(1)} %pad_add_fusion.place_ref, f32[8,1024]{1,0:T(8,128)S(1)} %add_add_fusion.sums_ref, ...), custom_call_target="tpu_custom_call" | custom-call | tf_op jit(solution)/shard_map/cleaned/clean/pallas_call | solution.py:420
  132.9 5.3 %all-to-all-start = ((bf16[32,16,16,128]{3,2,1,0:T(8,128)(2,1)}), bf16[32,16,16,128]{3,2,1,0:T(8,128)(2,1)S(1)}, u32[]{:S(2)}, u32[]{:S(2)}) async-start(bf16[32,16,16,128]{3,2,1,0:T(8,128)(2,1)} %get-tuple-element.50), calls=%async_computation | async-start | bytes 4194304 | tf_op jit(solution)/shard_map/channels/all_to_all | solution.py:436
  138.6 3.1 %collective-permute-start.33 = (bf16[2,16,64,128]{3,2,1,0:T(8,128)(2,1)}, bf16[2,16,64,128]{3,2,1,0:T(8,128)(2,1)S(1)}, u32[]{:S(2)}, u32[]{:S(2)}) collective-permute-start(bf16[2,16,64,128]{3,2,1,0:T(8,128)(2,1)} %get-tuple-element.47), channel_id=1, source_target_pairs={{0,64},{32,96},{64,0},{96,32},{1,65},{33,97},{65,1},{97,33},{2,66}... | collective-permute-start | bytes 1572872 | tf_op jit(solution)/shard_map/channels/ppermute | solution.py:433
  142.6 11.8 %collective-permute-done.32.refs_1_ = bf16[2,16,64,128]{3,2,1,0:T(8,128)(2,1)S(1)} collective-permute-done((bf16[2,16,64,128]{3,2,1,0:T(8,128)(2,1)}, bf16[2,16,64,128]{3,2,1,0:T(8,128)(2,1)S(1)}, u32[]{:S(2)}, u32[]{:S(2)}) %collective-permute-start.32) | collective-permute-done | bytes 524320 | tf_op jit(solution)/shard_map/channels/ppermute | solution.py:433
  154.5 10.6 %collective-permute-done.33.refs_2_ = bf16[2,16,64,128]{3,2,1,0:T(8,128)(2,1)S(1)} collective-permute-done((bf16[2,16,64,128]{3,2,1,0:T(8,128)(2,1)}, bf16[2,16,64,128]{3,2,1,0:T(8,128)(2,1)S(1)}, u32[]{:S(2)}, u32[]{:S(2)}) %collective-permute-start.33) | collective-permute-done | bytes 524320 | tf_op jit(solution)/shard_map/channels/ppermute | solution.py:433
  167.6 3.7 %ring_bin.1 = (f32[16,16,256]{2,1,0:T(8,128)S(1)}, f32[16,16,256]{2,1,0:T(8,128)S(1)}, f32[16,16,256]{2,1,0:T(8,128)S(1)}, f32[15,16,256]{2,1,0:T(8,128)}, f32[1,16,256]{2,1,0:T(8,128)S(1)}) custom-call(s32[4]{0:T(128)S(1)} %pad_add_fusion.place_ref, s32[1024]{0:T(1024)S(1)} %bitcast.16, bf16[2,16,64,128]{3,2,1,0:T(8,128)(2,1)S(1)} %copy-done.1, ...), custom_call_target="tpu_custom_call" | custom-call | tf_op jit(solution)/shard_map/binning/ring_bin/pallas_call | solution.py:441
  171.3 1.7 collective-permute-start.39
  172.9 2.7 %collective-permute-start.40 = (f32[16,16,256]{2,1,0:T(8,128)S(1)}, f32[16,16,256]{2,1,0:T(8,128)}, u32[]{:S(2)}, u32[]{:S(2)}) collective-permute-start(f32[16,16,256]{2,1,0:T(8,128)S(1)} %get-tuple-element.54), channel_id=1, source_target_pairs={{0,4},{2,6},{4,0},{6,2},{1,5},{3,7},{5,1},{7,3},{8,12},{10,14},{12... | collective-permute-start | bytes 786440 | tf_op jit(solution)/shard_map/tiles/ppermute | solution.py:433
  175.6 1.5 collective-permute-start.41
  177.1 4.3 %flat_bin.1 = f32[16,16,256]{2,1,0:T(8,128)S(1)} custom-call(s32[1024]{0:T(1024)S(1)} %bitcast.17, bf16[32,16,16,128]{3,2,1,0:T(8,128)(2,1)S(1)} %all-to-all-done.arrived_ref), custom_call_target="tpu_custom_call" | custom-call | tf_op jit(solution)/shard_map/binning/flat_bin/pallas_call | solution.py:448
  181.5 5.5 %collective-permute-done.41 = f32[15,16,256]{2,1,0:T(8,128)} collective-permute-done((f32[15,16,256]{2,1,0:T(8,128)}, f32[15,16,256]{2,1,0:T(8,128)}, u32[]{:S(2)}, u32[]{:S(2)}) %collective-permute-start.41) | collective-permute-done | bytes 245792 | tf_op jit(solution)/shard_map/tiles/ppermute | solution.py:433
  187.7 1.3 fusion
  189.0 17.3 %all_to_all.10 = f32[16,32,256]{2,1,0:T(8,128)S(1)} all-to-all(f32[16,32,256]{2,1,0:T(8,128)S(1)} %pad_maximum_fusion), channel_id=1, replica_groups=mesh['z'=4,'x'=4,'y'=4,'c'=2] {'z','x'}, dimensions={0} | all-to-all | bytes 1048576 | tf_op jit(solution)/shard_map/tiles/all_to_all | solution.py:460
  (86 shorter events, 10.1 us)
Async XLA Ops:
  0.0 10.0 %copy-start.6 = (s32[8,2]{0,1:T(2,128)S(1)}, s32[8,2]{0,1:T(2,128)}, u32[]{:S(2)}) copy-start(s32[8,2]{0,1:T(2,128)} %param.10) | copy-start | bytes 196
  0.0 10.2 %copy-start.7 = (s32[8,2]{0,1:T(2,128)S(1)}, s32[8,2]{0,1:T(2,128)}, u32[]{:S(2)}) copy-start(s32[8,2]{0,1:T(2,128)} %param.11) | copy-start | bytes 196
  0.0 10.7 %copy-start.4 = (f32[6,1024]{1,0:T(8,128)S(1)}, f32[6,1024]{1,0:T(8,128)}, u32[]{:S(2)}) copy-start(f32[6,1024]{1,0:T(8,128)} %param.8) | copy-start | bytes 73732
  0.0 10.7 %copy-start.2 = (f32[65]{0:T(128)S(1)}, f32[65]{0:T(128)}, u32[]{:S(2)}) copy-start(f32[65]{0:T(128)} %refs_0_.2) | copy-start | bytes 784
  5.1 26.2 %collective-permute-start = (f32[8,256,128]{2,1,0:T(8,128)}, f32[8,256,128]{2,1,0:T(8,128)S(1)}, u32[]{:S(2)}, u32[]{:S(2)}) collective-permute-start(f32[8,256,128]{2,1,0:T(8,128)} %get-tuple-element.36), channel_id=1, source_target_pairs={{0,8},{8,16},{16,24},{24,32},{32,40},{40,48},{48,56},{56,64},{64,7... | collective-permute-start | bytes 3145736 | tf_op jit(solution)/shard_map/edges/ppermute | solution.py:374
  8.7 26.7 %collective-permute-start.1 = (f32[8,256,128]{2,1,0:T(8,128)}, f32[8,256,128]{2,1,0:T(8,128)S(1)}, u32[]{:S(2)}, u32[]{:S(2)}) collective-permute-start(f32[8,256,128]{2,1,0:T(8,128)} %get-tuple-element.37), channel_id=1, source_target_pairs={{8,0},{16,8},{24,16},{32,24},{40,32},{48,40},{56,48},{64,56},{72,6... | collective-permute-start | bytes 3145736 | tf_op jit(solution)/shard_map/edges/ppermute | solution.py:375
  10.7 3.4 %copy-start = (f32[8,1024,256]{2,1,0:T(8,128)S(1)}, f32[8,1024,256]{2,1,0:T(8,128)}, u32[]{:S(2)}) copy-start(f32[8,1024,256]{2,1,0:T(8,128)} %refs_0_.3) | copy-start | bytes 25165828
  42.3 1.2 collective-permute-start.2
  43.6 5.8 %collective-permute-start.3 = (f32[8,1024]{1,0:T(8,128)S(1)}, f32[8,1024]{1,0:T(8,128)S(1)}, u32[]{:S(2)}, u32[]{:S(2)}) collective-permute-start(f32[8,1024]{1,0:T(8,128)S(1)} %add.113), channel_id=1, source_target_pairs={{0,2},{2,4},{4,6},{6,0},{1,3},{3,5},{5,7},{7,1},{8,10},{10,12},{12... | collective-permute-start | bytes 98312 | tf_op jit(solution)/shard_map/iterations/ppermute | solution.py:344
  45.2 5.4 %collective-permute-start.4 = (f32[8,1024]{1,0:T(8,128)S(1)}, f32[8,1024]{1,0:T(8,128)S(1)}, u32[]{:S(2)}, u32[]{:S(2)}) collective-permute-start(f32[8,1024]{1,0:T(8,128)S(1)} %add.113), channel_id=1, source_target_pairs={{0,4},{2,6},{4,0},{6,2},{1,5},{3,7},{5,1},{7,3},{8,12},{10,14},{12... | collective-permute-start | bytes 98312 | tf_op jit(solution)/shard_map/iterations/ppermute | solution.py:344
  48.1 3.9 %collective-permute-start.5 = (f32[8,1024]{1,0:T(8,128)S(1)}, f32[8,1024]{1,0:T(8,128)S(1)}, u32[]{:S(2)}, u32[]{:S(2)}) collective-permute-start(f32[8,1024]{1,0:T(8,128)S(1)} %add.113), channel_id=1, source_target_pairs={{0,6},{2,0},{4,2},{6,4},{1,7},{3,1},{5,3},{7,5},{8,14},{10,8},{12,... | collective-permute-start | bytes 98312 | tf_op jit(solution)/shard_map/iterations/ppermute | solution.py:344
  52.0 7.1 %collective-permute-start.6 = (f32[8,1024]{1,0:T(8,128)S(1)}, f32[8,1024]{1,0:T(8,128)S(1)}, u32[]{:S(2)}, u32[]{:S(2)}) collective-permute-start(f32[8,1024]{1,0:T(8,128)S(1)} %add_add_fusion.8), channel_id=1, source_target_pairs={{0,8},{8,16},{16,24},{24,0},{1,9},{9,17},{17,25},{25,1},{2,10},{10... | collective-permute-start | bytes 98312 | tf_op jit(solution)/shard_map/iterations/ppermute | solution.py:344
  53.5 7.4 %collective-permute-start.7 = (f32[8,1024]{1,0:T(8,128)S(1)}, f32[8,1024]{1,0:T(8,128)S(1)}, u32[]{:S(2)}, u32[]{:S(2)}) collective-permute-start(f32[8,1024]{1,0:T(8,128)S(1)} %add_add_fusion.8), channel_id=1, source_target_pairs={{0,16},{8,24},{16,0},{24,8},{1,17},{9,25},{17,1},{25,9},{2,18},{10... | collective-permute-start | bytes 98312 | tf_op jit(solution)/shard_map/iterations/ppermute | solution.py:344
  58.7 3.9 %collective-permute-start.8 = (f32[8,1024]{1,0:T(8,128)S(1)}, f32[8,1024]{1,0:T(8,128)S(1)}, u32[]{:S(2)}, u32[]{:S(2)}) collective-permute-start(f32[8,1024]{1,0:T(8,128)S(1)} %add_add_fusion.8), channel_id=1, source_target_pairs={{0,24},{8,0},{16,8},{24,16},{1,25},{9,1},{17,9},{25,17},{2,26},{10... | collective-permute-start | bytes 98312 | tf_op jit(solution)/shard_map/iterations/ppermute | solution.py:344
  62.6 5.7 %collective-permute-start.10 = (f32[8,1024]{1,0:T(8,128)S(1)}, f32[8,1024]{1,0:T(8,128)S(1)}, u32[]{:S(2)}, u32[]{:S(2)}) collective-permute-start(f32[8,1024]{1,0:T(8,128)S(1)} %add_add_fusion.7), channel_id=1, source_target_pairs={{0,64},{32,96},{64,0},{96,32},{1,65},{33,97},{65,1},{97,33},{2,66}... | collective-permute-start | bytes 98312 | tf_op jit(solution)/shard_map/iterations/ppermute | solution.py:344
  66.3 3.9 %collective-permute-start.11 = (f32[8,1024]{1,0:T(8,128)S(1)}, f32[8,1024]{1,0:T(8,128)S(1)}, u32[]{:S(2)}, u32[]{:S(2)}) collective-permute-start(f32[8,1024]{1,0:T(8,128)S(1)} %add_add_fusion.7), channel_id=1, source_target_pairs={{0,96},{32,0},{64,32},{96,64},{1,97},{33,1},{65,33},{97,65},{2,98}... | collective-permute-start | bytes 98312 | tf_op jit(solution)/shard_map/iterations/ppermute | solution.py:344
  67.3 5.1 %collective-permute-start.9 = (f32[8,1024]{1,0:T(8,128)S(1)}, f32[8,1024]{1,0:T(8,128)S(1)}, u32[]{:S(2)}, u32[]{:S(2)}) collective-permute-start(f32[8,1024]{1,0:T(8,128)S(1)} %add_add_fusion.7), channel_id=1, source_target_pairs={{0,32},{32,64},{64,96},{96,0},{1,33},{33,65},{65,97},{97,1},{2,34}... | collective-permute-start | bytes 98312 | tf_op jit(solution)/shard_map/iterations/ppermute | solution.py:344
  76.3 1.2 collective-permute-start.12
  77.6 5.1 %collective-permute-start.13 = (f32[8,1024]{1,0:T(8,128)S(1)}, f32[8,1024]{1,0:T(8,128)S(1)}, u32[]{:S(2)}, u32[]{:S(2)}) collective-permute-start(f32[8,1024]{1,0:T(8,128)S(1)} %add.123), channel_id=1, source_target_pairs={{0,32},{32,64},{64,96},{96,0},{1,33},{33,65},{65,97},{97,1},{2,34}... | collective-permute-start | bytes 98312 | tf_op jit(solution)/shard_map/iterations/ppermute | solution.py:344
  77.6 5.5 %collective-permute-start.14 = (f32[8,1024]{1,0:T(8,128)S(1)}, f32[8,1024]{1,0:T(8,128)S(1)}, u32[]{:S(2)}, u32[]{:S(2)}) collective-permute-start(f32[8,1024]{1,0:T(8,128)S(1)} %add.123), channel_id=1, source_target_pairs={{0,64},{32,96},{64,0},{96,32},{1,65},{33,97},{65,1},{97,33},{2,66}... | collective-permute-start | bytes 98312 | tf_op jit(solution)/shard_map/iterations/ppermute | solution.py:344
  79.0 4.9 %collective-permute-start.15 = (f32[8,1024]{1,0:T(8,128)S(1)}, f32[8,1024]{1,0:T(8,128)S(1)}, u32[]{:S(2)}, u32[]{:S(2)}) collective-permute-start(f32[8,1024]{1,0:T(8,128)S(1)} %add.123), channel_id=1, source_target_pairs={{0,96},{32,0},{64,32},{96,64},{1,97},{33,1},{65,33},{97,65},{2,98}... | collective-permute-start | bytes 98312 | tf_op jit(solution)/shard_map/iterations/ppermute | solution.py:344
  83.9 5.4 %collective-permute-start.16 = (f32[8,1024]{1,0:T(8,128)S(1)}, f32[8,1024]{1,0:T(8,128)S(1)}, u32[]{:S(2)}, u32[]{:S(2)}) collective-permute-start(f32[8,1024]{1,0:T(8,128)S(1)} %add_add_fusion.5), channel_id=1, source_target_pairs={{0,2},{2,4},{4,6},{6,0},{1,3},{3,5},{5,7},{7,1},{8,10},{10,12},{12... | collective-permute-start | bytes 98312 | tf_op jit(solution)/shard_map/iterations/ppermute | solution.py:344
  84.3 6.1 %collective-permute-start.17 = (f32[8,1024]{1,0:T(8,128)S(1)}, f32[8,1024]{1,0:T(8,128)S(1)}, u32[]{:S(2)}, u32[]{:S(2)}) collective-permute-start(f32[8,1024]{1,0:T(8,128)S(1)} %add_add_fusion.5), channel_id=1, source_target_pairs={{0,4},{2,6},{4,0},{6,2},{1,5},{3,7},{5,1},{7,3},{8,12},{10,14},{12... | collective-permute-start | bytes 98312 | tf_op jit(solution)/shard_map/iterations/ppermute | solution.py:344
  88.2 3.9 %collective-permute-start.18 = (f32[8,1024]{1,0:T(8,128)S(1)}, f32[8,1024]{1,0:T(8,128)S(1)}, u32[]{:S(2)}, u32[]{:S(2)}) collective-permute-start(f32[8,1024]{1,0:T(8,128)S(1)} %add_add_fusion.5), channel_id=1, source_target_pairs={{0,6},{2,0},{4,2},{6,4},{1,7},{3,1},{5,3},{7,5},{8,14},{10,8},{12,... | collective-permute-start | bytes 98312 | tf_op jit(solution)/shard_map/iterations/ppermute | solution.py:344
  92.1 5.2 %collective-permute-start.19 = (f32[8,1024]{1,0:T(8,128)S(1)}, f32[8,1024]{1,0:T(8,128)S(1)}, u32[]{:S(2)}, u32[]{:S(2)}) collective-permute-start(f32[8,1024]{1,0:T(8,128)S(1)} %add_add_fusion.4), channel_id=1, source_target_pairs={{0,8},{8,16},{16,24},{24,0},{1,9},{9,17},{17,25},{25,1},{2,10},{10... | collective-permute-start | bytes 98312 | tf_op jit(solution)/shard_map/iterations/ppermute | solution.py:344
  92.2 5.5 %collective-permute-start.20 = (f32[8,1024]{1,0:T(8,128)S(1)}, f32[8,1024]{1,0:T(8,128)S(1)}, u32[]{:S(2)}, u32[]{:S(2)}) collective-permute-start(f32[8,1024]{1,0:T(8,128)S(1)} %add_add_fusion.4), channel_id=1, source_target_pairs={{0,16},{8,24},{16,0},{24,8},{1,17},{9,25},{17,1},{25,9},{2,18},{10... | collective-permute-start | bytes 98312 | tf_op jit(solution)/shard_map/iterations/ppermute | solution.py:344
  94.8 3.9 %collective-permute-start.21 = (f32[8,1024]{1,0:T(8,128)S(1)}, f32[8,1024]{1,0:T(8,128)S(1)}, u32[]{:S(2)}, u32[]{:S(2)}) collective-permute-start(f32[8,1024]{1,0:T(8,128)S(1)} %add_add_fusion.4), channel_id=1, source_target_pairs={{0,24},{8,0},{16,8},{24,16},{1,25},{9,1},{17,9},{25,17},{2,26},{10... | collective-permute-start | bytes 98312 | tf_op jit(solution)/shard_map/iterations/ppermute | solution.py:344
  98.8 24.5 %copy-start.5 = (f32[8,256]{1,0:T(8,128)S(1)}, f32[8,256]{1,0:T(8,128)}, u32[]{:S(2)}) copy-start(f32[8,256]{1,0:T(8,128)} %param.9) | copy-start | bytes 24580
  102.7 1.2 collective-permute-start.22
  103.9 5.6 %collective-permute-start.23 = (f32[8,1024]{1,0:T(8,128)S(1)}, f32[8,1024]{1,0:T(8,128)S(1)}, u32[]{:S(2)}, u32[]{:S(2)}) collective-permute-start(f32[8,1024]{1,0:T(8,128)S(1)} %add.133), channel_id=1, source_target_pairs={{0,2},{2,4},{4,6},{6,0},{1,3},{3,5},{5,7},{7,1},{8,10},{10,12},{12... | collective-permute-start | bytes 98312 | tf_op jit(solution)/shard_map/iterations/ppermute | solution.py:344
  104.0 5.5 %collective-permute-start.24 = (f32[8,1024]{1,0:T(8,128)S(1)}, f32[8,1024]{1,0:T(8,128)S(1)}, u32[]{:S(2)}, u32[]{:S(2)}) collective-permute-start(f32[8,1024]{1,0:T(8,128)S(1)} %add.133), channel_id=1, source_target_pairs={{0,4},{2,6},{4,0},{6,2},{1,5},{3,7},{5,1},{7,3},{8,12},{10,14},{12... | collective-permute-start | bytes 98312 | tf_op jit(solution)/shard_map/iterations/ppermute | solution.py:344
  106.7 3.9 %collective-permute-start.25 = (f32[8,1024]{1,0:T(8,128)S(1)}, f32[8,1024]{1,0:T(8,128)S(1)}, u32[]{:S(2)}, u32[]{:S(2)}) collective-permute-start(f32[8,1024]{1,0:T(8,128)S(1)} %add.133), channel_id=1, source_target_pairs={{0,6},{2,0},{4,2},{6,4},{1,7},{3,1},{5,3},{7,5},{8,14},{10,8},{12,... | collective-permute-start | bytes 98312 | tf_op jit(solution)/shard_map/iterations/ppermute | solution.py:344
  110.7 5.2 %collective-permute-start.26 = (f32[8,1024]{1,0:T(8,128)S(1)}, f32[8,1024]{1,0:T(8,128)S(1)}, u32[]{:S(2)}, u32[]{:S(2)}) collective-permute-start(f32[8,1024]{1,0:T(8,128)S(1)} %add_add_fusion.2), channel_id=1, source_target_pairs={{0,8},{8,16},{16,24},{24,0},{1,9},{9,17},{17,25},{25,1},{2,10},{10... | collective-permute-start | bytes 98312 | tf_op jit(solution)/shard_map/iterations/ppermute | solution.py:344
  112.1 5.4 %collective-permute-start.27 = (f32[8,1024]{1,0:T(8,128)S(1)}, f32[8,1024]{1,0:T(8,128)S(1)}, u32[]{:S(2)}, u32[]{:S(2)}) collective-permute-start(f32[8,1024]{1,0:T(8,128)S(1)} %add_add_fusion.2), channel_id=1, source_target_pairs={{0,16},{8,24},{16,0},{24,8},{1,17},{9,25},{17,1},{25,9},{2,18},{10... | collective-permute-start | bytes 98312 | tf_op jit(solution)/shard_map/iterations/ppermute | solution.py:344
  114.9 3.9 %collective-permute-start.28 = (f32[8,1024]{1,0:T(8,128)S(1)}, f32[8,1024]{1,0:T(8,128)S(1)}, u32[]{:S(2)}, u32[]{:S(2)}) collective-permute-start(f32[8,1024]{1,0:T(8,128)S(1)} %add_add_fusion.2), channel_id=1, source_target_pairs={{0,24},{8,0},{16,8},{24,16},{1,25},{9,1},{17,9},{25,17},{2,26},{10... | collective-permute-start | bytes 98312 | tf_op jit(solution)/shard_map/iterations/ppermute | solution.py:344
  118.8 5.2 %collective-permute-start.29 = (f32[8,1024]{1,0:T(8,128)S(1)}, f32[8,1024]{1,0:T(8,128)S(1)}, u32[]{:S(2)}, u32[]{:S(2)}) collective-permute-start(f32[8,1024]{1,0:T(8,128)S(1)} %add_add_fusion.1), channel_id=1, source_target_pairs={{0,32},{32,64},{64,96},{96,0},{1,33},{33,65},{65,97},{97,1},{2,34}... | collective-permute-start | bytes 98312 | tf_op jit(solution)/shard_map/iterations/ppermute | solution.py:344
  120.5 5.4 %collective-permute-start.30 = (f32[8,1024]{1,0:T(8,128)S(1)}, f32[8,1024]{1,0:T(8,128)S(1)}, u32[]{:S(2)}, u32[]{:S(2)}) collective-permute-start(f32[8,1024]{1,0:T(8,128)S(1)} %add_add_fusion.1), channel_id=1, source_target_pairs={{0,64},{32,96},{64,0},{96,32},{1,65},{33,97},{65,1},{97,33},{2,66}... | collective-permute-start | bytes 98312 | tf_op jit(solution)/shard_map/iterations/ppermute | solution.py:344
  122.7 3.9 %collective-permute-start.31 = (f32[8,1024]{1,0:T(8,128)S(1)}, f32[8,1024]{1,0:T(8,128)S(1)}, u32[]{:S(2)}, u32[]{:S(2)}) collective-permute-start(f32[8,1024]{1,0:T(8,128)S(1)} %add_add_fusion.1), channel_id=1, source_target_pairs={{0,96},{32,0},{64,32},{96,64},{1,97},{33,1},{65,33},{97,65},{2,98}... | collective-permute-start | bytes 98312 | tf_op jit(solution)/shard_map/iterations/ppermute | solution.py:344
  132.9 8.7 %copy-start.8 = (bf16[2,16,64,128]{3,2,1,0:T(8,128)(2,1)S(1)}, bf16[2,16,64,128]{3,2,1,0:T(8,128)(2,1)}, u32[]{:S(2)}) copy-start(bf16[2,16,64,128]{3,2,1,0:T(8,128)(2,1)} %get-tuple-element.48) | copy-start | bytes 1572868
  132.9 9.5 %copy-start.1 = (bf16[2,16,64,128]{3,2,1,0:T(8,128)(2,1)S(1)}, bf16[2,16,64,128]{3,2,1,0:T(8,128)(2,1)}, u32[]{:S(2)}) copy-start(bf16[2,16,64,128]{3,2,1,0:T(8,128)(2,1)} %get-tuple-element.45.refs_0_) | copy-start | bytes 1572868
  132.9 44.1 %all-to-all-start = ((bf16[32,16,16,128]{3,2,1,0:T(8,128)(2,1)}), bf16[32,16,16,128]{3,2,1,0:T(8,128)(2,1)S(1)}, u32[]{:S(2)}, u32[]{:S(2)}) async-start(bf16[32,16,16,128]{3,2,1,0:T(8,128)(2,1)} %get-tuple-element.50), calls=%async_computation | async-start | bytes 4194304 | tf_op jit(solution)/shard_map/channels/all_to_all | solution.py:436
  138.2 16.2 %collective-permute-start.32 = (bf16[2,16,64,128]{3,2,1,0:T(8,128)(2,1)}, bf16[2,16,64,128]{3,2,1,0:T(8,128)(2,1)S(1)}, u32[]{:S(2)}, u32[]{:S(2)}) collective-permute-start(bf16[2,16,64,128]{3,2,1,0:T(8,128)(2,1)} %get-tuple-element.46), channel_id=1, source_target_pairs={{0,32},{32,64},{64,96},{96,0},{1,33},{33,65},{65,97},{97,1},{2,34}... | collective-permute-start | bytes 1572872 | tf_op jit(solution)/shard_map/channels/ppermute | solution.py:433
  138.6 26.6 %collective-permute-start.33 = (bf16[2,16,64,128]{3,2,1,0:T(8,128)(2,1)}, bf16[2,16,64,128]{3,2,1,0:T(8,128)(2,1)S(1)}, u32[]{:S(2)}, u32[]{:S(2)}) collective-permute-start(bf16[2,16,64,128]{3,2,1,0:T(8,128)(2,1)} %get-tuple-element.47), channel_id=1, source_target_pairs={{0,64},{32,96},{64,0},{96,32},{1,65},{33,97},{65,1},{97,33},{2,66}... | collective-permute-start | bytes 1572872 | tf_op jit(solution)/shard_map/channels/ppermute | solution.py:433
  141.6 24.1 %collective-permute-start.34 = (bf16[2,16,64,128]{3,2,1,0:T(8,128)(2,1)S(1)}, bf16[2,16,64,128]{3,2,1,0:T(8,128)(2,1)S(1)}, u32[]{:S(2)}, u32[]{:S(2)}) collective-permute-start(bf16[2,16,64,128]{3,2,1,0:T(8,128)(2,1)S(1)} %copy-done.8), channel_id=1, source_target_pairs={{0,96},{32,0},{64,32},{96,64},{1,97},{33,1},{65,33},{97,65},{2,98}... | collective-permute-start | bytes 1572872 | tf_op jit(solution)/shard_map/channels/ppermute | solution.py:433
  142.5 23.6 %collective-permute-start.35 = (bf16[16,64,128]{2,1,0:T(8,128)(2,1)S(1)}, bf16[16,64,128]{2,1,0:T(8,128)(2,1)S(1)}, u32[]{:S(2)}, u32[]{:S(2)}) collective-permute-start(bf16[16,64,128]{2,1,0:T(8,128)(2,1)S(1)} %slice_bitcast_fusion.3), channel_id=1, source_target_pairs={{0,1},{1,0},{2,3},{3,2},{4,5},{5,4},{6,7},{7,6},{8,9},{9,8},{10,11... | collective-permute-start | bytes 786440 | tf_op jit(solution)/shard_map/channels/ppermute | solution.py:438
  154.4 11.7 %collective-permute-start.36 = (bf16[16,64,128]{2,1,0:T(8,128)(2,1)S(1)}, bf16[16,64,128]{2,1,0:T(8,128)(2,1)S(1)}, u32[]{:S(2)}, u32[]{:S(2)}) collective-permute-start(bf16[16,64,128]{2,1,0:T(8,128)(2,1)S(1)} %slice_bitcast_fusion.2), channel_id=1, source_target_pairs={{0,1},{1,0},{2,3},{3,2},{4,5},{5,4},{6,7},{7,6},{8,9},{9,8},{10,11... | collective-permute-start | bytes 786440 | tf_op jit(solution)/shard_map/channels/ppermute | solution.py:438
  165.2 1.6 collective-permute-start.37
  165.7 1.8 collective-permute-start.38
  171.3 15.7 %collective-permute-start.39 = (f32[16,16,256]{2,1,0:T(8,128)S(1)}, f32[16,16,256]{2,1,0:T(8,128)S(1)}, u32[]{:S(2)}, u32[]{:S(2)}) collective-permute-start(f32[16,16,256]{2,1,0:T(8,128)S(1)} %get-tuple-element.53), channel_id=1, source_target_pairs={{0,2},{2,4},{4,6},{6,0},{1,3},{3,5},{5,7},{7,1},{8,10},{10,12},{12... | collective-permute-start | bytes 786440 | tf_op jit(solution)/shard_map/tiles/ppermute | solution.py:433
  172.9 14.7 %collective-permute-start.40 = (f32[16,16,256]{2,1,0:T(8,128)S(1)}, f32[16,16,256]{2,1,0:T(8,128)}, u32[]{:S(2)}, u32[]{:S(2)}) collective-permute-start(f32[16,16,256]{2,1,0:T(8,128)S(1)} %get-tuple-element.54), channel_id=1, source_target_pairs={{0,4},{2,6},{4,0},{6,2},{1,5},{3,7},{5,1},{7,3},{8,12},{10,14},{12... | collective-permute-start | bytes 786440 | tf_op jit(solution)/shard_map/tiles/ppermute | solution.py:433
  175.6 11.4 %collective-permute-start.41 = (f32[15,16,256]{2,1,0:T(8,128)}, f32[15,16,256]{2,1,0:T(8,128)}, u32[]{:S(2)}, u32[]{:S(2)}) collective-permute-start(f32[15,16,256]{2,1,0:T(8,128)} %get-tuple-element.55), channel_id=1, source_target_pairs={{0,6},{2,0},{4,2},{6,4},{1,7},{3,1},{5,3},{7,5},{8,14},{10,8},{12,... | collective-permute-start | bytes 737288 | tf_op jit(solution)/shard_map/tiles/ppermute | solution.py:433
  181.4 6.3 %collective-permute-start.42 = (f32[1,16,256]{2,1,0:T(8,128)S(1)}, f32[1,16,256]{2,1,0:T(8,128)S(1)}, u32[]{:S(2)}, u32[]{:S(2)}) collective-permute-start(f32[1,16,256]{2,1,0:T(8,128)S(1)} %get-tuple-element.56), channel_id=1, source_target_pairs={{0,6},{2,0},{4,2},{6,4},{1,7},{3,1},{5,3},{7,5},{8,14},{10,8},{12,... | collective-permute-start | bytes 49160 | tf_op jit(solution)/shard_map/tiles/ppermute | solution.py:433
  187.0 0.7 copy-start.3

commit v7 on v6

--- a/solution.py
+++ b/solution.py
@@ -434,7 +434,8 @@
 
     with jax.named_scope("channels"):
         arrived = lax.all_to_all(flat, ("x", "y", "c"), 0, 0, tiled=True)
-        near = [ring[0]] + [along(ring[s], "z", s) for s in range(1, CHIPS)]
+        away = {s: along(ring[s], "z", s) for s in (2, 1, 3)}
+        near = [ring[0]] + [away[s] for s in range(1, CHIPS)]
         far = [lax.ppermute(value[1], "c", [(0, 1), (1, 0)]) for value in near]
 
     with jax.named_scope("binning"):

time: 208 us -> 208 us (level)
  no operation moved by 1% of the time
where the time goes in v7:
time: 208 us; the launch traced here: 207 us
  waiting for transfers between devices  76.3 us (37%)
  starting transfers between devices  63.9 us (31%)
  Pallas kernels  42.7 us (21%)
  blocking collectives  17.3 us (8%)
  local copies, waits for them, and re-layouts  4.04 us (2%)
  other arithmetic  2.35 us (1%)
    ppermute x30, starting transfers between devices, total_over(): lax.ppermute(value, axis, [(i, (i + s) % count) for i in range(count)])  43 us
    ppermute x30, waiting for transfers between devices, total_over(): lax.ppermute(value, axis, [(i, (i + s) % count) for i in range(count)])  33.2 us
    ppermute x7, waiting for transfers between devices, along(): lax.ppermute(value, axis, [(i, (i + shift) % CHIPS) for i in range(CHIPS)])  29.1 us
    all_to_all x1, blocking collectives, shards(): lax.all_to_all(jnp.concatenate([sky, rows], axis=1), ('z', 'x'), 0, 0, ti...  17.3 us
    ppermute x7, starting transfers between devices, along(): lax.ppermute(value, axis, [(i, (i + shift) % CHIPS) for i in range(CHIPS)])  10.1 us
    pallas_call x1, Pallas kernels, shards(): call(lambda *refs: own_kernel(reach, *refs), 'own', [rows_f32, jax.ShapeD...  8.65 us
    ppermute x1, waiting for transfers between devices, shards(): lax.ppermute(tail, ('z', 'x'), [(i, i + 1) for i in range(ends)])  8.52 us
    pallas_call x1, Pallas kernels, shards(): call(lambda *refs: edge_kernel(reach, *refs), 'edge', [piece, piece, piec...  6.94 us
  transfers between devices with their start and end apart: 44, of which 36 were waited for; matrix products, arithmetic and copies ran while one was open for 0% of the time, Pallas kernels for 8%

profile of v7, /device:TPU:0, one launch (start us, length us, event | category | flops | bytes accessed | tf_op | source)
XLA Modules:
  0.0 207.0 jit_solution(2566456903427032830)
XLA Ops:
  0.0 5.1 %pack.1 = (f32[8,256,128]{2,1,0:T(8,128)}, f32[8,256,128]{2,1,0:T(8,128)}) custom-call(f32[8,1024,256]{2,1,0:T(8,128)} %refs_0_.3), custom_call_target="tpu_custom_call" | custom-call | tf_op jit(solution)/shard_map/edges/pack/pallas_call | solution.py:369
  5.1 3.6 %collective-permute-start = (f32[8,256,128]{2,1,0:T(8,128)}, f32[8,256,128]{2,1,0:T(8,128)S(1)}, u32[]{:S(2)}, u32[]{:S(2)}) collective-permute-start(f32[8,256,128]{2,1,0:T(8,128)} %get-tuple-element.36), channel_id=1, source_target_pairs={{0,8},{8,16},{16,24},{24,32},{32,40},{40,48},{48,56},{56,64},{64,7... | collective-permute-start | bytes 3145736 | tf_op jit(solution)/shard_map/edges/ppermute | solution.py:374
  8.7 1.3 collective-permute-start.1
  10.7 3.4 %copy-done = f32[8,1024,256]{2,1,0:T(8,128)S(1)} copy-done((f32[8,1024,256]{2,1,0:T(8,128)S(1)}, f32[8,1024,256]{2,1,0:T(8,128)}, u32[]{:S(2)}) %copy-start) | copy-done | bytes 8388632
  14.1 8.6 %own.1 = (f32[8,1024]{1,0:T(8,128)S(1)}, bf16[2,256,256]{2,1,0:T(8,128)(2,1)S(1)}, f32[8,1024,256]{2,1,0:T(8,128)S(1)}) custom-call(f32[65]{0:T(128)S(1)} %copy-done.2, f32[8,1024]{1,0:T(8,128)S(1)} %pad.4.refs_1_, f32[8,1024,256]{2,1,0:T(8,128)S(1)} %copy-done), custom_call_target="tpu_custom_call" | custom-call | tf_op jit(solution)/shard_map/own/own/pallas_call | solution.py:379
  22.8 8.5 %collective-permute-done.refs_3_ = f32[8,256,128]{2,1,0:T(8,128)S(1)} collective-permute-done((f32[8,256,128]{2,1,0:T(8,128)}, f32[8,256,128]{2,1,0:T(8,128)S(1)}, u32[]{:S(2)}, u32[]{:S(2)}) %collective-permute-start) | collective-permute-done | bytes 1048608 | tf_op jit(solution)/shard_map/edges/ppermute | solution.py:374
  31.3 4.1 %collective-permute-done.1.refs_4_ = f32[8,256,128]{2,1,0:T(8,128)S(1)} collective-permute-done((f32[8,256,128]{2,1,0:T(8,128)}, f32[8,256,128]{2,1,0:T(8,128)S(1)}, u32[]{:S(2)}, u32[]{:S(2)}) %collective-permute-start.1) | collective-permute-done | bytes 1048608 | tf_op jit(solution)/shard_map/edges/ppermute | solution.py:375
  35.4 6.9 %edge.1 = (bf16[8,1024,256]{2,1,0:T(8,128)(2,1)S(1)}, bf16[8,1024,256]{2,1,0:T(8,128)(2,1)S(1)}, bf16[8,1024,256]{2,1,0:T(8,128)(2,1)S(1)}, f32[8,1024]{1,0:T(8,128)S(1)}) custom-call(f32[8,1024]{1,0:T(8,128)S(1)} %get-tuple-element.33.refs_0_, bf16[2,256,256]{2,1,0:T(8,128)(2,1)S(1)} %get-tuple-element.34.refs_1_, ...), custom_call_target="tpu_custom_call" | custom-call | tf_op jit(solution)/shard_map/filtered/edge/pallas_call | solution.py:400
  42.4 1.2 collective-permute-done.2
  43.6 1.6 collective-permute-start.3
  45.2 2.9 %collective-permute-start.4 = (f32[8,1024]{1,0:T(8,128)S(1)}, f32[8,1024]{1,0:T(8,128)S(1)}, u32[]{:S(2)}, u32[]{:S(2)}) collective-permute-start(f32[8,1024]{1,0:T(8,128)S(1)} %add.113), channel_id=1, source_target_pairs={{0,4},{2,6},{4,0},{6,2},{1,5},{3,7},{5,1},{7,3},{8,12},{10,14},{12... | collective-permute-start | bytes 98312 | tf_op jit(solution)/shard_map/iterations/ppermute | solution.py:344
  48.1 1.3 collective-permute-start.5
  49.4 1.2 collective-permute-done.4
  50.6 1.4 collective-permute-done.5
  52.0 1.5 collective-permute-start.6
  53.5 5.2 %collective-permute-start.7 = (f32[8,1024]{1,0:T(8,128)S(1)}, f32[8,1024]{1,0:T(8,128)S(1)}, u32[]{:S(2)}, u32[]{:S(2)}) collective-permute-start(f32[8,1024]{1,0:T(8,128)S(1)} %add_add_fusion.8), channel_id=1, source_target_pairs={{0,16},{8,24},{16,0},{24,8},{1,17},{9,25},{17,1},{25,9},{2,18},{10... | collective-permute-start | bytes 98312 | tf_op jit(solution)/shard_map/iterations/ppermute | solution.py:344
  59.1 1.8 collective-permute-done.7
  60.9 1.7 collective-permute-done.8
  62.6 3.7 %collective-permute-start.10 = (f32[8,1024]{1,0:T(8,128)S(1)}, f32[8,1024]{1,0:T(8,128)S(1)}, u32[]{:S(2)}, u32[]{:S(2)}) collective-permute-start(f32[8,1024]{1,0:T(8,128)S(1)} %add_add_fusion.7), channel_id=1, source_target_pairs={{0,64},{32,96},{64,0},{96,32},{1,65},{33,97},{65,1},{97,33},{2,66}... | collective-permute-start | bytes 98312 | tf_op jit(solution)/shard_map/iterations/ppermute | solution.py:344
  66.3 1.0 collective-permute-start.11
  67.3 1.0 collective-permute-start.9
  68.3 1.9 collective-permute-done.11
  70.2 2.2 %collective-permute-done.9 = f32[8,1024]{1,0:T(8,128)S(1)} collective-permute-done((f32[8,1024]{1,0:T(8,128)S(1)}, f32[8,1024]{1,0:T(8,128)S(1)}, u32[]{:S(2)}, u32[]{:S(2)}) %collective-permute-start.9) | collective-permute-done | bytes 32800 | tf_op jit(solution)/shard_map/iterations/ppermute | solution.py:344
  72.4 3.9 %step.2 = f32[8,1024]{1,0:T(8,128)S(1)} custom-call(f32[8,1024]{1,0:T(8,128)S(1)} %add_add_fusion.6.sums_ref, bf16[8,1024,256]{2,1,0:T(8,128)(2,1)S(1)} %get-tuple-element.40.high_ref, bf16[8,1024,256]{2,1,0:T(8,128)(2,1)S(1)} %get-tuple-element.41.mid_ref, f32[1,1024]{1,0:T(1,128)S(1)} %select_n.30.note_ref), custom_call_target="tpu_custom_call" | custom-call | tf_op jit(solution)/shard_map/iterations/step/pallas_call | solution.py:408
  76.4 1.2 collective-permute-done.12
  77.6 1.5 collective-permute-start.14
  79.0 1.8 collective-permute-start.15
  80.8 1.9 collective-permute-done.13
  83.1 0.8 collective-permute-done.15
  84.3 3.8 %collective-permute-start.17 = (f32[8,1024]{1,0:T(8,128)S(1)}, f32[8,1024]{1,0:T(8,128)S(1)}, u32[]{:S(2)}, u32[]{:S(2)}) collective-permute-start(f32[8,1024]{1,0:T(8,128)S(1)} %add_add_fusion.5), channel_id=1, source_target_pairs={{0,4},{2,6},{4,0},{6,2},{1,5},{3,7},{5,1},{7,3},{8,12},{10,14},{12... | collective-permute-start | bytes 98312 | tf_op jit(solution)/shard_map/iterations/ppermute | solution.py:344
  88.3 1.0 collective-permute-done.16
  89.3 1.1 collective-permute-done.17
  90.4 1.7 collective-permute-done.18
  92.2 2.7 %collective-permute-start.20 = (f32[8,1024]{1,0:T(8,128)S(1)}, f32[8,1024]{1,0:T(8,128)S(1)}, u32[]{:S(2)}, u32[]{:S(2)}) collective-permute-start(f32[8,1024]{1,0:T(8,128)S(1)} %add_add_fusion.4), channel_id=1, source_target_pairs={{0,16},{8,24},{16,0},{24,8},{1,17},{9,25},{17,1},{25,9},{2,18},{10... | collective-permute-start | bytes 98312 | tf_op jit(solution)/shard_map/iterations/ppermute | solution.py:344
  94.8 1.5 collective-permute-start.21
  96.3 1.0 collective-permute-done.19
  97.7 1.1 collective-permute-done.21
  98.8 3.9 %step.3 = f32[8,1024]{1,0:T(8,128)S(1)} custom-call(f32[8,1024]{1,0:T(8,128)S(1)} %add_add_fusion.3.sums_ref, bf16[8,1024,256]{2,1,0:T(8,128)(2,1)S(1)} %get-tuple-element.40.high_ref, bf16[8,1024,256]{2,1,0:T(8,128)(2,1)S(1)} %get-tuple-element.41.mid_ref, f32[1,1024]{1,0:T(1,128)S(1)} %broadcast_in_dim.39.note_ref), custom_call_target="tpu_custom_call" | custom-call | tf_op jit(solution)/shard_map/iterations/step/pallas_call | solution.py:413
  102.7 1.2 collective-permute-done.22
  104.0 2.7 %collective-permute-start.24 = (f32[8,1024]{1,0:T(8,128)S(1)}, f32[8,1024]{1,0:T(8,128)S(1)}, u32[]{:S(2)}, u32[]{:S(2)}) collective-permute-start(f32[8,1024]{1,0:T(8,128)S(1)} %add.133), channel_id=1, source_target_pairs={{0,4},{2,6},{4,0},{6,2},{1,5},{3,7},{5,1},{7,3},{8,12},{10,14},{12... | collective-permute-start | bytes 98312 | tf_op jit(solution)/shard_map/iterations/ppermute | solution.py:344
  106.7 1.3 collective-permute-start.25
  108.1 1.5 collective-permute-done.23
  109.6 1.1 collective-permute-done.25
  110.7 1.5 collective-permute-start.26
  112.1 2.7 %collective-permute-start.27 = (f32[8,1024]{1,0:T(8,128)S(1)}, f32[8,1024]{1,0:T(8,128)S(1)}, u32[]{:S(2)}, u32[]{:S(2)}) collective-permute-start(f32[8,1024]{1,0:T(8,128)S(1)} %add_add_fusion.2), channel_id=1, source_target_pairs={{0,16},{8,24},{16,0},{24,8},{1,17},{9,25},{17,1},{25,9},{2,18},{10... | collective-permute-start | bytes 98312 | tf_op jit(solution)/shard_map/iterations/ppermute | solution.py:344
  114.9 0.9 collective-permute-done.26
  115.8 1.7 collective-permute-done.27
  117.6 1.2 collective-permute-done.28
  118.8 1.7 collective-permute-start.29
  120.5 2.2 %collective-permute-start.30 = (f32[8,1024]{1,0:T(8,128)S(1)}, f32[8,1024]{1,0:T(8,128)S(1)}, u32[]{:S(2)}, u32[]{:S(2)}) collective-permute-start(f32[8,1024]{1,0:T(8,128)S(1)} %add_add_fusion.1), channel_id=1, source_target_pairs={{0,64},{32,96},{64,0},{96,32},{1,65},{33,97},{65,1},{97,33},{2,66}... | collective-permute-start | bytes 98312 | tf_op jit(solution)/shard_map/iterations/ppermute | solution.py:344
  124.0 2.0 collective-permute-done.30
  126.6 6.3 %clean.1 = (bf16[32,16,16,128]{3,2,1,0:T(8,128)(2,1)}, bf16[2,16,64,128]{3,2,1,0:T(8,128)(2,1)}, bf16[2,16,64,128]{3,2,1,0:T(8,128)(2,1)}, bf16[2,16,64,128]{3,2,1,0:T(8,128)(2,1)}, bf16[2,16,64,128]{3,2,1,0:T(8,128)(2,1)}) custom-call(s32[4]{0:T(128)S(1)} %pad_add_fusion.place_ref, f32[8,1024]{1,0:T(8,128)S(1)} %add_add_fusion.sums_ref, ...), custom_call_target="tpu_custom_call" | custom-call | tf_op jit(solution)/shard_map/cleaned/clean/pallas_call | solution.py:420
  132.9 5.3 %all-to-all-start = ((bf16[32,16,16,128]{3,2,1,0:T(8,128)(2,1)}), bf16[32,16,16,128]{3,2,1,0:T(8,128)(2,1)S(1)}, u32[]{:S(2)}, u32[]{:S(2)}) async-start(bf16[32,16,16,128]{3,2,1,0:T(8,128)(2,1)} %get-tuple-element.50), calls=%async_computation | async-start | bytes 4194304 | tf_op jit(solution)/shard_map/channels/all_to_all | solution.py:436
  138.6 3.1 %collective-permute-start.33 = (bf16[2,16,64,128]{3,2,1,0:T(8,128)(2,1)}, bf16[2,16,64,128]{3,2,1,0:T(8,128)(2,1)S(1)}, u32[]{:S(2)}, u32[]{:S(2)}) collective-permute-start(bf16[2,16,64,128]{3,2,1,0:T(8,128)(2,1)} %get-tuple-element.47), channel_id=1, source_target_pairs={{0,64},{32,96},{64,0},{96,32},{1,65},{33,97},{65,1},{97,33},{2,66}... | collective-permute-start | bytes 1572872 | tf_op jit(solution)/shard_map/channels/ppermute | solution.py:433
  142.6 11.8 %collective-permute-done.32.refs_1_ = bf16[2,16,64,128]{3,2,1,0:T(8,128)(2,1)S(1)} collective-permute-done((bf16[2,16,64,128]{3,2,1,0:T(8,128)(2,1)}, bf16[2,16,64,128]{3,2,1,0:T(8,128)(2,1)S(1)}, u32[]{:S(2)}, u32[]{:S(2)}) %collective-permute-start.32) | collective-permute-done | bytes 524320 | tf_op jit(solution)/shard_map/channels/ppermute | solution.py:433
  154.5 10.6 %collective-permute-done.33.refs_2_ = bf16[2,16,64,128]{3,2,1,0:T(8,128)(2,1)S(1)} collective-permute-done((bf16[2,16,64,128]{3,2,1,0:T(8,128)(2,1)}, bf16[2,16,64,128]{3,2,1,0:T(8,128)(2,1)S(1)}, u32[]{:S(2)}, u32[]{:S(2)}) %collective-permute-start.33) | collective-permute-done | bytes 524320 | tf_op jit(solution)/shard_map/channels/ppermute | solution.py:433
  167.6 3.7 %ring_bin.1 = (f32[16,16,256]{2,1,0:T(8,128)S(1)}, f32[16,16,256]{2,1,0:T(8,128)S(1)}, f32[16,16,256]{2,1,0:T(8,128)S(1)}, f32[15,16,256]{2,1,0:T(8,128)}, f32[1,16,256]{2,1,0:T(8,128)S(1)}) custom-call(s32[4]{0:T(128)S(1)} %pad_add_fusion.place_ref, s32[1024]{0:T(1024)S(1)} %bitcast.16, bf16[2,16,64,128]{3,2,1,0:T(8,128)(2,1)S(1)} %copy-done.1, ...), custom_call_target="tpu_custom_call" | custom-call | tf_op jit(solution)/shard_map/binning/ring_bin/pallas_call | solution.py:442
  171.3 1.7 collective-permute-start.39
  172.9 2.7 %collective-permute-start.40 = (f32[16,16,256]{2,1,0:T(8,128)S(1)}, f32[16,16,256]{2,1,0:T(8,128)}, u32[]{:S(2)}, u32[]{:S(2)}) collective-permute-start(f32[16,16,256]{2,1,0:T(8,128)S(1)} %get-tuple-element.54), channel_id=1, source_target_pairs={{0,4},{2,6},{4,0},{6,2},{1,5},{3,7},{5,1},{7,3},{8,12},{10,14},{12... | collective-permute-start | bytes 786440 | tf_op jit(solution)/shard_map/tiles/ppermute | solution.py:433
  175.6 1.5 collective-permute-start.41
  177.1 4.3 %flat_bin.1 = f32[16,16,256]{2,1,0:T(8,128)S(1)} custom-call(s32[1024]{0:T(1024)S(1)} %bitcast.17, bf16[32,16,16,128]{3,2,1,0:T(8,128)(2,1)S(1)} %all-to-all-done.arrived_ref), custom_call_target="tpu_custom_call" | custom-call | tf_op jit(solution)/shard_map/binning/flat_bin/pallas_call | solution.py:449
  181.5 5.5 %collective-permute-done.41 = f32[15,16,256]{2,1,0:T(8,128)} collective-permute-done((f32[15,16,256]{2,1,0:T(8,128)}, f32[15,16,256]{2,1,0:T(8,128)}, u32[]{:S(2)}, u32[]{:S(2)}) %collective-permute-start.41) | collective-permute-done | bytes 245792 | tf_op jit(solution)/shard_map/tiles/ppermute | solution.py:433
  187.7 1.3 fusion
  189.0 17.3 %all_to_all.10 = f32[16,32,256]{2,1,0:T(8,128)S(1)} all-to-all(f32[16,32,256]{2,1,0:T(8,128)S(1)} %pad_maximum_fusion), channel_id=1, replica_groups=mesh['z'=4,'x'=4,'y'=4,'c'=2] {'z','x'}, dimensions={0} | all-to-all | bytes 1048576 | tf_op jit(solution)/shard_map/tiles/all_to_all | solution.py:461
  (86 shorter events, 10.1 us)
Async XLA Ops:
  0.0 10.0 %copy-start.6 = (s32[8,2]{0,1:T(2,128)S(1)}, s32[8,2]{0,1:T(2,128)}, u32[]{:S(2)}) copy-start(s32[8,2]{0,1:T(2,128)} %param.10) | copy-start | bytes 196
  0.0 10.2 %copy-start.7 = (s32[8,2]{0,1:T(2,128)S(1)}, s32[8,2]{0,1:T(2,128)}, u32[]{:S(2)}) copy-start(s32[8,2]{0,1:T(2,128)} %param.11) | copy-start | bytes 196
  0.0 10.7 %copy-start.4 = (f32[6,1024]{1,0:T(8,128)S(1)}, f32[6,1024]{1,0:T(8,128)}, u32[]{:S(2)}) copy-start(f32[6,1024]{1,0:T(8,128)} %param.8) | copy-start | bytes 73732
  0.0 10.7 %copy-start.2 = (f32[65]{0:T(128)S(1)}, f32[65]{0:T(128)}, u32[]{:S(2)}) copy-start(f32[65]{0:T(128)} %refs_0_.2) | copy-start | bytes 784
  5.1 26.2 %collective-permute-start = (f32[8,256,128]{2,1,0:T(8,128)}, f32[8,256,128]{2,1,0:T(8,128)S(1)}, u32[]{:S(2)}, u32[]{:S(2)}) collective-permute-start(f32[8,256,128]{2,1,0:T(8,128)} %get-tuple-element.36), channel_id=1, source_target_pairs={{0,8},{8,16},{16,24},{24,32},{32,40},{40,48},{48,56},{56,64},{64,7... | collective-permute-start | bytes 3145736 | tf_op jit(solution)/shard_map/edges/ppermute | solution.py:374
  8.7 26.7 %collective-permute-start.1 = (f32[8,256,128]{2,1,0:T(8,128)}, f32[8,256,128]{2,1,0:T(8,128)S(1)}, u32[]{:S(2)}, u32[]{:S(2)}) collective-permute-start(f32[8,256,128]{2,1,0:T(8,128)} %get-tuple-element.37), channel_id=1, source_target_pairs={{8,0},{16,8},{24,16},{32,24},{40,32},{48,40},{56,48},{64,56},{72,6... | collective-permute-start | bytes 3145736 | tf_op jit(solution)/shard_map/edges/ppermute | solution.py:375
  10.7 3.4 %copy-start = (f32[8,1024,256]{2,1,0:T(8,128)S(1)}, f32[8,1024,256]{2,1,0:T(8,128)}, u32[]{:S(2)}) copy-start(f32[8,1024,256]{2,1,0:T(8,128)} %refs_0_.3) | copy-start | bytes 25165828
  42.3 1.2 collective-permute-start.2
  43.6 5.8 %collective-permute-start.3 = (f32[8,1024]{1,0:T(8,128)S(1)}, f32[8,1024]{1,0:T(8,128)S(1)}, u32[]{:S(2)}, u32[]{:S(2)}) collective-permute-start(f32[8,1024]{1,0:T(8,128)S(1)} %add.113), channel_id=1, source_target_pairs={{0,2},{2,4},{4,6},{6,0},{1,3},{3,5},{5,7},{7,1},{8,10},{10,12},{12... | collective-permute-start | bytes 98312 | tf_op jit(solution)/shard_map/iterations/ppermute | solution.py:344
  45.2 5.4 %collective-permute-start.4 = (f32[8,1024]{1,0:T(8,128)S(1)}, f32[8,1024]{1,0:T(8,128)S(1)}, u32[]{:S(2)}, u32[]{:S(2)}) collective-permute-start(f32[8,1024]{1,0:T(8,128)S(1)} %add.113), channel_id=1, source_target_pairs={{0,4},{2,6},{4,0},{6,2},{1,5},{3,7},{5,1},{7,3},{8,12},{10,14},{12... | collective-permute-start | bytes 98312 | tf_op jit(solution)/shard_map/iterations/ppermute | solution.py:344
  48.1 3.9 %collective-permute-start.5 = (f32[8,1024]{1,0:T(8,128)S(1)}, f32[8,1024]{1,0:T(8,128)S(1)}, u32[]{:S(2)}, u32[]{:S(2)}) collective-permute-start(f32[8,1024]{1,0:T(8,128)S(1)} %add.113), channel_id=1, source_target_pairs={{0,6},{2,0},{4,2},{6,4},{1,7},{3,1},{5,3},{7,5},{8,14},{10,8},{12,... | collective-permute-start | bytes 98312 | tf_op jit(solution)/shard_map/iterations/ppermute | solution.py:344
  52.0 7.1 %collective-permute-start.6 = (f32[8,1024]{1,0:T(8,128)S(1)}, f32[8,1024]{1,0:T(8,128)S(1)}, u32[]{:S(2)}, u32[]{:S(2)}) collective-permute-start(f32[8,1024]{1,0:T(8,128)S(1)} %add_add_fusion.8), channel_id=1, source_target_pairs={{0,8},{8,16},{16,24},{24,0},{1,9},{9,17},{17,25},{25,1},{2,10},{10... | collective-permute-start | bytes 98312 | tf_op jit(solution)/shard_map/iterations/ppermute | solution.py:344
  53.5 7.4 %collective-permute-start.7 = (f32[8,1024]{1,0:T(8,128)S(1)}, f32[8,1024]{1,0:T(8,128)S(1)}, u32[]{:S(2)}, u32[]{:S(2)}) collective-permute-start(f32[8,1024]{1,0:T(8,128)S(1)} %add_add_fusion.8), channel_id=1, source_target_pairs={{0,16},{8,24},{16,0},{24,8},{1,17},{9,25},{17,1},{25,9},{2,18},{10... | collective-permute-start | bytes 98312 | tf_op jit(solution)/shard_map/iterations/ppermute | solution.py:344
  58.7 3.9 %collective-permute-start.8 = (f32[8,1024]{1,0:T(8,128)S(1)}, f32[8,1024]{1,0:T(8,128)S(1)}, u32[]{:S(2)}, u32[]{:S(2)}) collective-permute-start(f32[8,1024]{1,0:T(8,128)S(1)} %add_add_fusion.8), channel_id=1, source_target_pairs={{0,24},{8,0},{16,8},{24,16},{1,25},{9,1},{17,9},{25,17},{2,26},{10... | collective-permute-start | bytes 98312 | tf_op jit(solution)/shard_map/iterations/ppermute | solution.py:344
  62.6 5.7 %collective-permute-start.10 = (f32[8,1024]{1,0:T(8,128)S(1)}, f32[8,1024]{1,0:T(8,128)S(1)}, u32[]{:S(2)}, u32[]{:S(2)}) collective-permute-start(f32[8,1024]{1,0:T(8,128)S(1)} %add_add_fusion.7), channel_id=1, source_target_pairs={{0,64},{32,96},{64,0},{96,32},{1,65},{33,97},{65,1},{97,33},{2,66}... | collective-permute-start | bytes 98312 | tf_op jit(solution)/shard_map/iterations/ppermute | solution.py:344
  66.3 3.9 %collective-permute-start.11 = (f32[8,1024]{1,0:T(8,128)S(1)}, f32[8,1024]{1,0:T(8,128)S(1)}, u32[]{:S(2)}, u32[]{:S(2)}) collective-permute-start(f32[8,1024]{1,0:T(8,128)S(1)} %add_add_fusion.7), channel_id=1, source_target_pairs={{0,96},{32,0},{64,32},{96,64},{1,97},{33,1},{65,33},{97,65},{2,98}... | collective-permute-start | bytes 98312 | tf_op jit(solution)/shard_map/iterations/ppermute | solution.py:344
  67.3 5.1 %collective-permute-start.9 = (f32[8,1024]{1,0:T(8,128)S(1)}, f32[8,1024]{1,0:T(8,128)S(1)}, u32[]{:S(2)}, u32[]{:S(2)}) collective-permute-start(f32[8,1024]{1,0:T(8,128)S(1)} %add_add_fusion.7), channel_id=1, source_target_pairs={{0,32},{32,64},{64,96},{96,0},{1,33},{33,65},{65,97},{97,1},{2,34}... | collective-permute-start | bytes 98312 | tf_op jit(solution)/shard_map/iterations/ppermute | solution.py:344
  76.3 1.2 collective-permute-start.12
  77.6 5.1 %collective-permute-start.13 = (f32[8,1024]{1,0:T(8,128)S(1)}, f32[8,1024]{1,0:T(8,128)S(1)}, u32[]{:S(2)}, u32[]{:S(2)}) collective-permute-start(f32[8,1024]{1,0:T(8,128)S(1)} %add.123), channel_id=1, source_target_pairs={{0,32},{32,64},{64,96},{96,0},{1,33},{33,65},{65,97},{97,1},{2,34}... | collective-permute-start | bytes 98312 | tf_op jit(solution)/shard_map/iterations/ppermute | solution.py:344
  77.6 5.5 %collective-permute-start.14 = (f32[8,1024]{1,0:T(8,128)S(1)}, f32[8,1024]{1,0:T(8,128)S(1)}, u32[]{:S(2)}, u32[]{:S(2)}) collective-permute-start(f32[8,1024]{1,0:T(8,128)S(1)} %add.123), channel_id=1, source_target_pairs={{0,64},{32,96},{64,0},{96,32},{1,65},{33,97},{65,1},{97,33},{2,66}... | collective-permute-start | bytes 98312 | tf_op jit(solution)/shard_map/iterations/ppermute | solution.py:344
  79.0 4.9 %collective-permute-start.15 = (f32[8,1024]{1,0:T(8,128)S(1)}, f32[8,1024]{1,0:T(8,128)S(1)}, u32[]{:S(2)}, u32[]{:S(2)}) collective-permute-start(f32[8,1024]{1,0:T(8,128)S(1)} %add.123), channel_id=1, source_target_pairs={{0,96},{32,0},{64,32},{96,64},{1,97},{33,1},{65,33},{97,65},{2,98}... | collective-permute-start | bytes 98312 | tf_op jit(solution)/shard_map/iterations/ppermute | solution.py:344
  83.9 5.4 %collective-permute-start.16 = (f32[8,1024]{1,0:T(8,128)S(1)}, f32[8,1024]{1,0:T(8,128)S(1)}, u32[]{:S(2)}, u32[]{:S(2)}) collective-permute-start(f32[8,1024]{1,0:T(8,128)S(1)} %add_add_fusion.5), channel_id=1, source_target_pairs={{0,2},{2,4},{4,6},{6,0},{1,3},{3,5},{5,7},{7,1},{8,10},{10,12},{12... | collective-permute-start | bytes 98312 | tf_op jit(solution)/shard_map/iterations/ppermute | solution.py:344
  84.3 6.1 %collective-permute-start.17 = (f32[8,1024]{1,0:T(8,128)S(1)}, f32[8,1024]{1,0:T(8,128)S(1)}, u32[]{:S(2)}, u32[]{:S(2)}) collective-permute-start(f32[8,1024]{1,0:T(8,128)S(1)} %add_add_fusion.5), channel_id=1, source_target_pairs={{0,4},{2,6},{4,0},{6,2},{1,5},{3,7},{5,1},{7,3},{8,12},{10,14},{12... | collective-permute-start | bytes 98312 | tf_op jit(solution)/shard_map/iterations/ppermute | solution.py:344
  88.2 3.9 %collective-permute-start.18 = (f32[8,1024]{1,0:T(8,128)S(1)}, f32[8,1024]{1,0:T(8,128)S(1)}, u32[]{:S(2)}, u32[]{:S(2)}) collective-permute-start(f32[8,1024]{1,0:T(8,128)S(1)} %add_add_fusion.5), channel_id=1, source_target_pairs={{0,6},{2,0},{4,2},{6,4},{1,7},{3,1},{5,3},{7,5},{8,14},{10,8},{12,... | collective-permute-start | bytes 98312 | tf_op jit(solution)/shard_map/iterations/ppermute | solution.py:344
  92.1 5.2 %collective-permute-start.19 = (f32[8,1024]{1,0:T(8,128)S(1)}, f32[8,1024]{1,0:T(8,128)S(1)}, u32[]{:S(2)}, u32[]{:S(2)}) collective-permute-start(f32[8,1024]{1,0:T(8,128)S(1)} %add_add_fusion.4), channel_id=1, source_target_pairs={{0,8},{8,16},{16,24},{24,0},{1,9},{9,17},{17,25},{25,1},{2,10},{10... | collective-permute-start | bytes 98312 | tf_op jit(solution)/shard_map/iterations/ppermute | solution.py:344
  92.2 5.5 %collective-permute-start.20 = (f32[8,1024]{1,0:T(8,128)S(1)}, f32[8,1024]{1,0:T(8,128)S(1)}, u32[]{:S(2)}, u32[]{:S(2)}) collective-permute-start(f32[8,1024]{1,0:T(8,128)S(1)} %add_add_fusion.4), channel_id=1, source_target_pairs={{0,16},{8,24},{16,0},{24,8},{1,17},{9,25},{17,1},{25,9},{2,18},{10... | collective-permute-start | bytes 98312 | tf_op jit(solution)/shard_map/iterations/ppermute | solution.py:344
  94.8 3.9 %collective-permute-start.21 = (f32[8,1024]{1,0:T(8,128)S(1)}, f32[8,1024]{1,0:T(8,128)S(1)}, u32[]{:S(2)}, u32[]{:S(2)}) collective-permute-start(f32[8,1024]{1,0:T(8,128)S(1)} %add_add_fusion.4), channel_id=1, source_target_pairs={{0,24},{8,0},{16,8},{24,16},{1,25},{9,1},{17,9},{25,17},{2,26},{10... | collective-permute-start | bytes 98312 | tf_op jit(solution)/shard_map/iterations/ppermute | solution.py:344
  98.8 24.5 %copy-start.5 = (f32[8,256]{1,0:T(8,128)S(1)}, f32[8,256]{1,0:T(8,128)}, u32[]{:S(2)}) copy-start(f32[8,256]{1,0:T(8,128)} %param.9) | copy-start | bytes 24580
  102.7 1.2 collective-permute-start.22
  103.9 5.6 %collective-permute-start.23 = (f32[8,1024]{1,0:T(8,128)S(1)}, f32[8,1024]{1,0:T(8,128)S(1)}, u32[]{:S(2)}, u32[]{:S(2)}) collective-permute-start(f32[8,1024]{1,0:T(8,128)S(1)} %add.133), channel_id=1, source_target_pairs={{0,2},{2,4},{4,6},{6,0},{1,3},{3,5},{5,7},{7,1},{8,10},{10,12},{12... | collective-permute-start | bytes 98312 | tf_op jit(solution)/shard_map/iterations/ppermute | solution.py:344
  104.0 5.5 %collective-permute-start.24 = (f32[8,1024]{1,0:T(8,128)S(1)}, f32[8,1024]{1,0:T(8,128)S(1)}, u32[]{:S(2)}, u32[]{:S(2)}) collective-permute-start(f32[8,1024]{1,0:T(8,128)S(1)} %add.133), channel_id=1, source_target_pairs={{0,4},{2,6},{4,0},{6,2},{1,5},{3,7},{5,1},{7,3},{8,12},{10,14},{12... | collective-permute-start | bytes 98312 | tf_op jit(solution)/shard_map/iterations/ppermute | solution.py:344
  106.7 3.9 %collective-permute-start.25 = (f32[8,1024]{1,0:T(8,128)S(1)}, f32[8,1024]{1,0:T(8,128)S(1)}, u32[]{:S(2)}, u32[]{:S(2)}) collective-permute-start(f32[8,1024]{1,0:T(8,128)S(1)} %add.133), channel_id=1, source_target_pairs={{0,6},{2,0},{4,2},{6,4},{1,7},{3,1},{5,3},{7,5},{8,14},{10,8},{12,... | collective-permute-start | bytes 98312 | tf_op jit(solution)/shard_map/iterations/ppermute | solution.py:344
  110.7 5.2 %collective-permute-start.26 = (f32[8,1024]{1,0:T(8,128)S(1)}, f32[8,1024]{1,0:T(8,128)S(1)}, u32[]{:S(2)}, u32[]{:S(2)}) collective-permute-start(f32[8,1024]{1,0:T(8,128)S(1)} %add_add_fusion.2), channel_id=1, source_target_pairs={{0,8},{8,16},{16,24},{24,0},{1,9},{9,17},{17,25},{25,1},{2,10},{10... | collective-permute-start | bytes 98312 | tf_op jit(solution)/shard_map/iterations/ppermute | solution.py:344
  112.1 5.4 %collective-permute-start.27 = (f32[8,1024]{1,0:T(8,128)S(1)}, f32[8,1024]{1,0:T(8,128)S(1)}, u32[]{:S(2)}, u32[]{:S(2)}) collective-permute-start(f32[8,1024]{1,0:T(8,128)S(1)} %add_add_fusion.2), channel_id=1, source_target_pairs={{0,16},{8,24},{16,0},{24,8},{1,17},{9,25},{17,1},{25,9},{2,18},{10... | collective-permute-start | bytes 98312 | tf_op jit(solution)/shard_map/iterations/ppermute | solution.py:344
  114.9 3.9 %collective-permute-start.28 = (f32[8,1024]{1,0:T(8,128)S(1)}, f32[8,1024]{1,0:T(8,128)S(1)}, u32[]{:S(2)}, u32[]{:S(2)}) collective-permute-start(f32[8,1024]{1,0:T(8,128)S(1)} %add_add_fusion.2), channel_id=1, source_target_pairs={{0,24},{8,0},{16,8},{24,16},{1,25},{9,1},{17,9},{25,17},{2,26},{10... | collective-permute-start | bytes 98312 | tf_op jit(solution)/shard_map/iterations/ppermute | solution.py:344
  118.8 5.2 %collective-permute-start.29 = (f32[8,1024]{1,0:T(8,128)S(1)}, f32[8,1024]{1,0:T(8,128)S(1)}, u32[]{:S(2)}, u32[]{:S(2)}) collective-permute-start(f32[8,1024]{1,0:T(8,128)S(1)} %add_add_fusion.1), channel_id=1, source_target_pairs={{0,32},{32,64},{64,96},{96,0},{1,33},{33,65},{65,97},{97,1},{2,34}... | collective-permute-start | bytes 98312 | tf_op jit(solution)/shard_map/iterations/ppermute | solution.py:344
  120.5 5.4 %collective-permute-start.30 = (f32[8,1024]{1,0:T(8,128)S(1)}, f32[8,1024]{1,0:T(8,128)S(1)}, u32[]{:S(2)}, u32[]{:S(2)}) collective-permute-start(f32[8,1024]{1,0:T(8,128)S(1)} %add_add_fusion.1), channel_id=1, source_target_pairs={{0,64},{32,96},{64,0},{96,32},{1,65},{33,97},{65,1},{97,33},{2,66}... | collective-permute-start | bytes 98312 | tf_op jit(solution)/shard_map/iterations/ppermute | solution.py:344
  122.7 3.9 %collective-permute-start.31 = (f32[8,1024]{1,0:T(8,128)S(1)}, f32[8,1024]{1,0:T(8,128)S(1)}, u32[]{:S(2)}, u32[]{:S(2)}) collective-permute-start(f32[8,1024]{1,0:T(8,128)S(1)} %add_add_fusion.1), channel_id=1, source_target_pairs={{0,96},{32,0},{64,32},{96,64},{1,97},{33,1},{65,33},{97,65},{2,98}... | collective-permute-start | bytes 98312 | tf_op jit(solution)/shard_map/iterations/ppermute | solution.py:344
  132.9 8.7 %copy-start.8 = (bf16[2,16,64,128]{3,2,1,0:T(8,128)(2,1)S(1)}, bf16[2,16,64,128]{3,2,1,0:T(8,128)(2,1)}, u32[]{:S(2)}) copy-start(bf16[2,16,64,128]{3,2,1,0:T(8,128)(2,1)} %get-tuple-element.48) | copy-start | bytes 1572868
  132.9 9.5 %copy-start.1 = (bf16[2,16,64,128]{3,2,1,0:T(8,128)(2,1)S(1)}, bf16[2,16,64,128]{3,2,1,0:T(8,128)(2,1)}, u32[]{:S(2)}) copy-start(bf16[2,16,64,128]{3,2,1,0:T(8,128)(2,1)} %get-tuple-element.45.refs_0_) | copy-start | bytes 1572868
  132.9 44.1 %all-to-all-start = ((bf16[32,16,16,128]{3,2,1,0:T(8,128)(2,1)}), bf16[32,16,16,128]{3,2,1,0:T(8,128)(2,1)S(1)}, u32[]{:S(2)}, u32[]{:S(2)}) async-start(bf16[32,16,16,128]{3,2,1,0:T(8,128)(2,1)} %get-tuple-element.50), calls=%async_computation | async-start | bytes 4194304 | tf_op jit(solution)/shard_map/channels/all_to_all | solution.py:436
  138.2 16.2 %collective-permute-start.32 = (bf16[2,16,64,128]{3,2,1,0:T(8,128)(2,1)}, bf16[2,16,64,128]{3,2,1,0:T(8,128)(2,1)S(1)}, u32[]{:S(2)}, u32[]{:S(2)}) collective-permute-start(bf16[2,16,64,128]{3,2,1,0:T(8,128)(2,1)} %get-tuple-element.46), channel_id=1, source_target_pairs={{0,32},{32,64},{64,96},{96,0},{1,33},{33,65},{65,97},{97,1},{2,34}... | collective-permute-start | bytes 1572872 | tf_op jit(solution)/shard_map/channels/ppermute | solution.py:433
  138.6 26.6 %collective-permute-start.33 = (bf16[2,16,64,128]{3,2,1,0:T(8,128)(2,1)}, bf16[2,16,64,128]{3,2,1,0:T(8,128)(2,1)S(1)}, u32[]{:S(2)}, u32[]{:S(2)}) collective-permute-start(bf16[2,16,64,128]{3,2,1,0:T(8,128)(2,1)} %get-tuple-element.47), channel_id=1, source_target_pairs={{0,64},{32,96},{64,0},{96,32},{1,65},{33,97},{65,1},{97,33},{2,66}... | collective-permute-start | bytes 1572872 | tf_op jit(solution)/shard_map/channels/ppermute | solution.py:433
  141.6 24.1 %collective-permute-start.34 = (bf16[2,16,64,128]{3,2,1,0:T(8,128)(2,1)S(1)}, bf16[2,16,64,128]{3,2,1,0:T(8,128)(2,1)S(1)}, u32[]{:S(2)}, u32[]{:S(2)}) collective-permute-start(bf16[2,16,64,128]{3,2,1,0:T(8,128)(2,1)S(1)} %copy-done.8), channel_id=1, source_target_pairs={{0,96},{32,0},{64,32},{96,64},{1,97},{33,1},{65,33},{97,65},{2,98}... | collective-permute-start | bytes 1572872 | tf_op jit(solution)/shard_map/channels/ppermute | solution.py:433
  142.5 23.6 %collective-permute-start.35 = (bf16[16,64,128]{2,1,0:T(8,128)(2,1)S(1)}, bf16[16,64,128]{2,1,0:T(8,128)(2,1)S(1)}, u32[]{:S(2)}, u32[]{:S(2)}) collective-permute-start(bf16[16,64,128]{2,1,0:T(8,128)(2,1)S(1)} %slice_bitcast_fusion.3), channel_id=1, source_target_pairs={{0,1},{1,0},{2,3},{3,2},{4,5},{5,4},{6,7},{7,6},{8,9},{9,8},{10,11... | collective-permute-start | bytes 786440 | tf_op jit(solution)/shard_map/channels/ppermute | solution.py:439
  154.4 11.7 %collective-permute-start.36 = (bf16[16,64,128]{2,1,0:T(8,128)(2,1)S(1)}, bf16[16,64,128]{2,1,0:T(8,128)(2,1)S(1)}, u32[]{:S(2)}, u32[]{:S(2)}) collective-permute-start(bf16[16,64,128]{2,1,0:T(8,128)(2,1)S(1)} %slice_bitcast_fusion.2), channel_id=1, source_target_pairs={{0,1},{1,0},{2,3},{3,2},{4,5},{5,4},{6,7},{7,6},{8,9},{9,8},{10,11... | collective-permute-start | bytes 786440 | tf_op jit(solution)/shard_map/channels/ppermute | solution.py:439
  165.2 1.6 collective-permute-start.37
  165.7 1.8 collective-permute-start.38
  171.3 15.7 %collective-permute-start.39 = (f32[16,16,256]{2,1,0:T(8,128)S(1)}, f32[16,16,256]{2,1,0:T(8,128)S(1)}, u32[]{:S(2)}, u32[]{:S(2)}) collective-permute-start(f32[16,16,256]{2,1,0:T(8,128)S(1)} %get-tuple-element.53), channel_id=1, source_target_pairs={{0,2},{2,4},{4,6},{6,0},{1,3},{3,5},{5,7},{7,1},{8,10},{10,12},{12... | collective-permute-start | bytes 786440 | tf_op jit(solution)/shard_map/tiles/ppermute | solution.py:433
  172.9 14.7 %collective-permute-start.40 = (f32[16,16,256]{2,1,0:T(8,128)S(1)}, f32[16,16,256]{2,1,0:T(8,128)}, u32[]{:S(2)}, u32[]{:S(2)}) collective-permute-start(f32[16,16,256]{2,1,0:T(8,128)S(1)} %get-tuple-element.54), channel_id=1, source_target_pairs={{0,4},{2,6},{4,0},{6,2},{1,5},{3,7},{5,1},{7,3},{8,12},{10,14},{12... | collective-permute-start | bytes 786440 | tf_op jit(solution)/shard_map/tiles/ppermute | solution.py:433
  175.6 11.4 %collective-permute-start.41 = (f32[15,16,256]{2,1,0:T(8,128)}, f32[15,16,256]{2,1,0:T(8,128)}, u32[]{:S(2)}, u32[]{:S(2)}) collective-permute-start(f32[15,16,256]{2,1,0:T(8,128)} %get-tuple-element.55), channel_id=1, source_target_pairs={{0,6},{2,0},{4,2},{6,4},{1,7},{3,1},{5,3},{7,5},{8,14},{10,8},{12,... | collective-permute-start | bytes 737288 | tf_op jit(solution)/shard_map/tiles/ppermute | solution.py:433
  181.4 6.3 %collective-permute-start.42 = (f32[1,16,256]{2,1,0:T(8,128)S(1)}, f32[1,16,256]{2,1,0:T(8,128)S(1)}, u32[]{:S(2)}, u32[]{:S(2)}) collective-permute-start(f32[1,16,256]{2,1,0:T(8,128)S(1)} %get-tuple-element.56), channel_id=1, source_target_pairs={{0,6},{2,0},{4,2},{6,4},{1,7},{3,1},{5,3},{7,5},{8,14},{10,8},{12,... | collective-permute-start | bytes 49160 | tf_op jit(solution)/shard_map/tiles/ppermute | solution.py:433
  187.0 0.7 copy-start.3
